TPU v7x, 32 devices: a whole 2x2x4 slice. The times are simulated.
32 devices in a mesh: row: 8 (over z, x), col: 4 (over y, core).
Axes of the slice: x: 2, y: 2, z: 4, core: 2. Of those that a mesh axis runs over, the one named last changes fastest.
Arguments:
- integrals: bfloat16 [16384, 4096], P('row', 'col'), may hold values from -0.046875 to 0.046875
- lambda2: bfloat16 [2016, 16384], P('col', 'row'), may hold values from -6 to 6
- source_terms: float32 [2016, 4096], P('row', 'col'), may hold values from -6 to 6
- hist_amp: bfloat16 [5, 2016, 4096], P(None, 'row', 'col'), may hold values from -6 to 6
- hist_err: bfloat16 [5, 2016, 4096], P(None, 'row', 'col'), may hold values from -64 to 64
- eps_occ: float32 [64], replicated, may hold values from -1 to -0.3
- eps_vir: float32 [800], replicated, may hold values from 0.1 to 1
- occ_pair: int32 [2, 2016], P(None, 'row'), may hold values from 0 to 63, as said below
- vir_pair: int32 [2, 4096], P(None, 'col'), may hold values from 0 to 799, as said below
Outputs:
- updated: float32 [2016, 4096], P('row', 'col')
Inputs may be any that keep to these rules, and one draw needn't show every extreme that they name: `occ_pair`: every pair i < j of the 64 occupied orbitals appears exactly once, in some order. `vir_pair`: in every column the first orbital is smaller than the second.
All inputs are finite; a program needn't handle non-finite values.
Results may differ from a plain program's by a relative error of at most 0.0003.
Values may be sent and summed in bfloat16 or wider, within the bound.
No kernel may reach another device: no remote copies, remote signals or barrier semaphores. Data moves between devices by JAX's collectives and lax.ppermute only.
A program may use at most 64 MiB of HBM per device.

v0:
```python
import jax
import jax.numpy as jnp
from jax import lax
from jax.sharding import PartitionSpec as P

precise = lax.Precision.HIGHEST


def pair_energy(pairs, energies):
    levels = jnp.arange(energies.shape[0], dtype=jnp.int32)
    first = jnp.sum(jnp.where(pairs[0][:, None] == levels[None, :], energies[None, :], 0.0), axis=1)
    second = jnp.sum(
        jnp.where(pairs[1][:, None] == levels[None, :], energies[None, :], 0.0), axis=1
    )
    return first + second


def diis_weights(correlation):
    factor = jnp.linalg.cholesky(correlation)
    order = correlation.shape[0]
    forward = []
    for k in range(order):
        running = jnp.ones((), correlation.dtype)
        for m in range(k):
            running = running - factor[k, m] * forward[m]
        forward.append(running / factor[k, k])
    backward = [None] * order
    for k in reversed(range(order)):
        running = forward[k]
        for m in range(k + 1, order):
            running = running - factor[m, k] * backward[m]
        backward[k] = running / factor[k, k]
    solved = jnp.stack(backward)
    return solved / jnp.sum(solved)


def on_device(
    integrals, lambda2, source_terms, hist_amp, hist_err, eps_occ, eps_vir, occ_pair, vir_pair
):
    stored_count = hist_err.shape[0]
    flat_stored = hist_err.astype(jnp.float32).reshape(stored_count, -1)
    stored_correlation = lax.psum(
        jnp.dot(flat_stored, flat_stored.T, precision=precise), ("row", "col")
    )
    all_cols = lax.all_gather(lambda2, "col", axis=0, tiled=True)
    ladder = lax.psum_scatter(
        jnp.dot(all_cols, integrals, preferred_element_type=jnp.float32),
        "row",
        scatter_dimension=0,
        tiled=True,
    )
    denominator = pair_energy(occ_pair, eps_occ)[:, None] - pair_energy(vir_pair, eps_vir)[None, :]
    raw_update = (source_terms + ladder) / denominator
    err_new = raw_update - hist_amp[0].astype(jnp.float32)
    flat_new = err_new.reshape(1, -1)
    stacked = jnp.concatenate([flat_stored, flat_new], axis=0)
    cross_terms = lax.psum(jnp.dot(stacked, flat_new[0], precision=precise), ("row", "col"))
    upper_rows = jnp.concatenate([stored_correlation, cross_terms[:stored_count, None]], axis=1)
    correlation = jnp.concatenate([upper_rows, cross_terms[None, :]], axis=0)
    weights = diis_weights(correlation)
    updated = weights[stored_count] * raw_update
    for k in range(stored_count):
        updated = updated + weights[k] * hist_amp[k].astype(jnp.float32)
    return updated


def solution(mesh):
    placed = (
        P("row", "col"),
        P("col", "row"),
        P("row", "col"),
        P(None, "row", "col"),
        P(None, "row", "col"),
        P(),
        P(),
        P(None, "row"),
        P(None, "col"),
    )
    return jax.shard_map(
        on_device, mesh=mesh, in_specs=placed, out_specs=P("row", "col"), check_vma=False
    )
```

profile of v0, /device:TPU:0, one launch (start us, length us, event | category | flops | bytes accessed | tf_op | source)
XLA Modules:
  0.0 370.1 jit_solution(8937989237410411831)
XLA Ops:
  6.5 0.7 all-gather.2.cloned.1.call-update
  7.3 2.4 convert_bitcast_fusion
  9.6 0.0 copy-start.5
  9.6 0.0 copy-start.3
  9.7 0.0 copy-start.2
  9.7 6.4 %copy.27 = f32[1,5,252,1024]{3,1,2,0:T(8,128)} copy(f32[1,5,252,1024]{3,2,1,0:T(8,128)S(1)} %convert_bitcast_fusion) | data formatting | bytes 10321920
  16.0 0.6 dynamic-slice.4
  17.3 0.8 select_reduce_fusion
  18.1 6.8 %fusion.7 = f32[5,5]{0,1:T(8,128)S(1)} fusion(bf16[5,252,1024]{2,1,0:T(8,128)(2,1)} %param.13), kind=kOutput, calls=%fused_computation.13 | convolution fusion | flops 12902400 | bytes 2580580 | tf_op jit(solution)/shard_map/dot_general | solution.py:43
  24.9 44.2 %all-gather.2.cloned.1.call-done = bf16[2016,2048]{1,0:T(8,128)(2,1)} async-done(((bf16[504,2048]{1,0:T(8,128)(2,1)}), bf16[2016,2048]{1,0:T(8,128)(2,1)}) %all-gather.2.cloned.1.call-update) | async-done | bytes 8257552 | tf_op jit(solution)/shard_map/all_gather | solution.py:45
  69.2 14.2 %fusion.27 = f32[2016,1024]{1,0:T(8,128)} fusion(bf16[2016,2048]{1,0:T(8,128)(2,1)} %all-gather.2.cloned.1.call-done, bf16[2048,1024]{1,0:T(8,128)(2,1)} %param.9), kind=kOutput, calls=%fused_computation.43 | convolution fusion | flops 8455716864 | bytes 20709376 | tf_op jit(solution)/shard_map/dot_general | solution.py:47
  83.4 168.8 %fusion = f32[256,1024]{1,0:T(8,128)S(1)} fusion(f32[2016,1024]{1,0:T(8,128)} %fusion.27), kind=kCustom, calls=%all-reduce-scatter | all-reduce-scatter fusion | flops 2097153 | bytes 9306624
  252.2 1.5 collective-permute-start
  253.7 0.1 select_reduce_fusion.2
  253.8 2.4 collective-permute-done
  256.2 0.6 concatenate.12
  256.8 1.3 fusion.13
  258.2 1.1 copy.28
  259.2 20.7 %fusion.10 = f32[6]{0:T(128)S(1)} fusion(f32[258048,1]{0,1:T(1,128)S(1)} %bitcast.78, f32[1,258048]{1,0:T(1,128)S(1)} %bitcast.79, f32[5,258048]{1,0:T(8,128)} %bitcast.77), kind=kOutput, calls=%fused_computation.14 | convolution fusion | flops 20127744 | bytes 7225368 | tf_op jit(solution)/shard_map/dot_general | solution.py:57
  279.9 45.2 %all-reduce.2 = (f32[6]{0:T(128)S(1)}, f32[5,5]{0,1:T(8,128)S(1)}) all-reduce(f32[6]{0:T(128)S(1)} %fusion.10, f32[5,5]{0,1:T(8,128)S(1)} %fusion.7), channel_id=1, replica_groups=mesh['row'=8,'col'=4] {'row','col'}, use_global_device_ids=true, to_apply=%region_6.7 | all-reduce | flops 31 | bytes 248 | tf_op jit(solution)/shard_map/psum | solution.py:57
  325.1 0.1 copy.23
  325.2 0.1 pad_maximum_fusion
  325.3 0.1 copy.24
  325.4 0.1 fusion.20
  325.5 0.5 cholesky.18
  326.1 0.6 compare_reduce_fusion
  326.7 0.6 select_select_fusion
  327.4 0.6 fusion.24
  328.0 0.7 fusion.23
  355.3 0.1 stack.27
  355.4 0.7 fusion.26
  356.0 7.2 %fusion.18 = f32[252,1024]{1,0:T(8,128)} fusion(bf16[5,252,1024]{2,1,0:T(8,128)(2,1)} %param.12, f32[]{:T(128)} %bitcast.46, f32[]{:T(128)} %bitcast.44, f32[]{:T(128)} %bitcast.42, f32[]{:T(128)} %bitcast.40, f32[]{:T(128)} %bitcast.38, f32[]{:T(128)} %bitcast.37, f32[1024]{0:T(1024)S(1)} %add.49, f32[252]{0:T(256)S(1)} %add.48, ...), kind=kLoop, calls=%fused_computation.20 | loop fusion | flops 4902912 | bytes 5682188 | tf_op jit(solution)/shard_map/add | solution.py:63
  (18 shorter events, 0.1 us)
Async XLA Ops:
  6.5 62.7 %all-gather.2.cloned.1.call-start = ((), (), s32[]{:S(2)}) async-start(), calls=%async_computation | async-start | bytes 10321920 | tf_op jit(solution)/shard_map/all_gather | solution.py:45
  9.6 6.4 %copy-start.5 = (u32[32]{0:T(128)S(1)}, u32[32]{0:T(128)}, u32[]{:S(2)}) copy-start(u32[32]{0:T(128)} %constant.46) | copy-start | bytes 388
  9.6 7.6 %copy-start.3 = (s32[2,252]{1,0:T(2,128)S(1)}, s32[2,252]{1,0:T(2,128)}, u32[]{:S(2)}) copy-start(s32[2,252]{1,0:T(2,128)} %param.16) | copy-start | bytes 6052
  9.6 7.6 %copy-start.1 = (s32[2,1024]{1,0:T(2,128)S(1)}, s32[2,1024]{1,0:T(2,128)}, u32[]{:S(2)}) copy-start(s32[2,1024]{1,0:T(2,128)} %param.17) | copy-start | bytes 24580
  9.7 7.7 %copy-start.2 = (f32[800]{0:T(1024)S(1)}, f32[800]{0:T(1024)}, u32[]{:S(2)}) copy-start(f32[800]{0:T(1024)} %param.15) | copy-start | bytes 9604
  83.4 170.3 %copy-start.4 = (f32[64]{0:T(128)S(1)}, f32[64]{0:T(128)}, u32[]{:S(2)}) copy-start(f32[64]{0:T(128)} %param.14) | copy-start | bytes 772
  83.4 173.4 %copy-start = (f32[252,1024]{1,0:T(8,128)S(1)}, f32[252,1024]{1,0:T(8,128)}, u32[]{:S(2)}) copy-start(f32[252,1024]{1,0:T(8,128)} %param.11) | copy-start | bytes 3096580
  252.2 4.0 %collective-permute-start = (f32[28,1024]{1,0:T(8,128)S(1)}, f32[28,1024]{1,0:T(8,128)S(1)}, u32[]{:S(2)}, u32[]{:S(2)}) collective-permute-start(f32[28,1024]{1,0:T(8,128)S(1)} %slice.176), channel_id=1, source_target_pairs={{0,4},{4,8},{8,12},{12,16},{16,20},{20,24},{24,28},{1,5},{5,9},{9,... | collective-permute-start | bytes 344072
Sparse Core Ops, SparseCore 0:
  8.9 60.2 all-gather.1
where the time goes:
time: 371 us; the launch traced here: 370 us
  blocking collectives  214 us (58%)
  waiting for transfers between devices  47.3 us (13%)
  matrix products  41.7 us (11%)
  between operations  40.8 us (11%)
  other arithmetic  13.8 us (4%)
  local copies, waits for them, and re-layouts  10.9 us (3%)
    unnamed x1, blocking collectives  169 us
    psum x1, blocking collectives, on_device(): lax.psum(jnp.dot(stacked, flat_new[0], precision=precise), ('row', 'col'))  45.2 us
    all_gather x1, waiting for transfers between devices, on_device(): all_cols = lax.all_gather(lambda2, 'col', axis=0, tiled=True)  44.2 us
    dot_general x1, matrix products, on_device(): jnp.dot(stacked, flat_new[0], precision=precise)  20.7 us
    dot_general x1, matrix products, on_device(): jnp.dot(all_cols, integrals, preferred_element_type=jnp.float32)  14.2 us
    unnamed x17, local copies, waits for them, and re-layouts  8.66 us
  transfers between devices with their start and end apart: 2, of which 2 were waited for; matrix products, arithmetic and copies ran while one was open for 5% of the time, Pallas kernels for 0%

commit v1 on v0

v1 whole, which is shorter than its diff:
```python
import jax
import jax.numpy as jnp
from jax import lax
from jax.experimental import pallas as pl
from jax.experimental.pallas import tpu as pltpu
from jax.sharding import PartitionSpec as P

f32 = jnp.float32
wire = jnp.float16


def pair_energy(pairs, energies):
    levels = jnp.arange(energies.shape[0], dtype=jnp.int32)
    first = jnp.sum(jnp.where(pairs[0][:, None] == levels[None, :], energies[None, :], 0.0), axis=1)
    second = jnp.sum(
        jnp.where(pairs[1][:, None] == levels[None, :], energies[None, :], 0.0), axis=1
    )
    return first + second


def row_steps(rows, step, width, count, term):
    whole = rows // step

    def body(i, acc):
        parts = term(pl.ds(pl.multiple_of(i * step, step), step))
        return tuple(a + jnp.sum(p.reshape(step // 8, 8, width), axis=0) for a, p in zip(acc, parts))

    acc = lax.fori_loop(
        0, whole, body, tuple(jnp.zeros((8, width), f32) for _ in range(count))
    )
    sums = [jnp.sum(a, axis=0, keepdims=True) for a in acc]
    if rows % step:
        parts = term(pl.ds(whole * step, rows % step))
        sums = [s + jnp.sum(p, axis=0, keepdims=True) for s, p in zip(sums, parts)]
    return sums


def column_block(width):
    return 256 if width % 256 == 0 else width


def stored_products(hist_err):
    count, rows, width = hist_err.shape
    block = column_block(width)
    pairs = [(k, m) for k in range(count) for m in range(k + 1)]

    def kernel(err_ref, out_ref):
        def term(at):
            e = [err_ref[k, at, :].astype(f32) for k in range(count)]
            return [e[k] * e[m] for k, m in pairs]

        out_ref[...] = jnp.zeros_like(out_ref)
        for n, s in enumerate(row_steps(rows, 16, block, len(pairs), term)):
            out_ref[n : n + 1, :] = s

    padded = -(-len(pairs) // 8) * 8
    return pl.pallas_call(
        kernel,
        grid=(width // block,),
        in_specs=[pl.BlockSpec((count, rows, block), lambda i: (0, 0, i))],
        out_specs=pl.BlockSpec((padded, block), lambda i: (0, i)),
        out_shape=jax.ShapeDtypeStruct((padded, width), f32),
        cost_estimate=pl.CostEstimate(
            flops=2 * 15 * rows * width, bytes_accessed=hist_err.size * 2, transcendentals=0
        ),
    )(hist_err)


def new_products(ladder, source_terms, occ_energy, vir_energy, hist_amp, hist_err):
    count, rows, width = hist_err.shape
    block = column_block(width)

    def kernel(lad_ref, src_ref, occ_ref, vir_ref, amp_ref, err_ref, raw_ref, out_ref):
        def term(at):
            n = at.size
            den = occ_ref[at, 0:1] - vir_ref[...]
            raw = (src_ref[at, :] + lad_ref[at, :]) / den
            raw_ref[at, :] = raw
            new = raw - amp_ref[0, at, :].astype(f32)
            return [err_ref[k, at, :].astype(f32) * new for k in range(count)] + [new * new]

        out_ref[...] = jnp.zeros_like(out_ref)
        for n, s in enumerate(row_steps(rows, 16, block, count + 1, term)):
            out_ref[n : n + 1, :] = s

    columns = lambda i: (0, i)
    return pl.pallas_call(
        kernel,
        grid=(width // block,),
        in_specs=[
            pl.BlockSpec((rows, block), columns),
            pl.BlockSpec((rows, block), columns),
            pl.BlockSpec((rows, 128), lambda i: (0, 0)),
            pl.BlockSpec((1, block), columns),
            pl.BlockSpec((1, rows, block), lambda i: (0, 0, i)),
            pl.BlockSpec((count, rows, block), lambda i: (0, 0, i)),
        ],
        out_specs=[pl.BlockSpec((rows, block), columns), pl.BlockSpec((8, block), columns)],
        out_shape=[
            jax.ShapeDtypeStruct((rows, width), f32),
            jax.ShapeDtypeStruct((8, width), f32),
        ],
        cost_estimate=pl.CostEstimate(
            flops=20 * rows * width, bytes_accessed=hist_err.size * 2 + 14 * rows * width, transcendentals=0
        ),
    )(ladder, source_terms, occ_energy, vir_energy, hist_amp, hist_err)


def extrapolate(gathered, raw, hist_amp):
    count, rows, width = hist_amp.shape
    order = count + 1
    block = column_block(width)

    def kernel(sum_ref, raw_ref, amp_ref, out_ref):
        totals = jnp.sum(sum_ref[...], axis=0)
        lanes = lax.broadcasted_iota(jnp.int32, totals.shape, 1)
        subs = lax.broadcasted_iota(jnp.int32, totals.shape, 0)
        corr = {}
        n = 0
        for k in range(order):
            for m in range(k + 1):
                hit = (lanes == n) & (subs == 0)
                corr[k, m] = jnp.sum(jnp.where(hit, totals, 0.0), keepdims=True)
                n += 1
        factor = {}
        for m in range(order):
            diag = corr[m, m]
            for j in range(m):
                diag = diag - factor[m, j] * factor[m, j]
            factor[m, m] = jnp.sqrt(diag)
            for k in range(m + 1, order):
                value = corr[k, m]
                for j in range(m):
                    value = value - factor[k, j] * factor[m, j]
                factor[k, m] = value / factor[m, m]
        forward = []
        for k in range(order):
            running = jnp.ones((1, 1), f32)
            for m in range(k):
                running = running - factor[k, m] * forward[m]
            forward.append(running / factor[k, k])
        backward = [None] * order
        for k in reversed(range(order)):
            running = forward[k]
            for m in range(k + 1, order):
                running = running - factor[m, k] * backward[m]
            backward[k] = running / factor[k, k]
        whole = backward[0]
        for k in range(1, order):
            whole = whole + backward[k]
        weights = [b / whole for b in backward]
        updated = weights[count] * raw_ref[...]
        for k in range(count):
            updated = updated + weights[k] * amp_ref[k].astype(f32)
        out_ref[...] = updated

    columns = lambda i: (0, i)
    return pl.pallas_call(
        kernel,
        grid=(width // block,),
        in_specs=[
            pl.BlockSpec(gathered.shape, lambda i: (0, 0, 0)),
            pl.BlockSpec((rows, block), columns),
            pl.BlockSpec((count, rows, block), lambda i: (0, 0, i)),
        ],
        out_specs=pl.BlockSpec((rows, block), columns),
        out_shape=jax.ShapeDtypeStruct((rows, width), f32),
    )(gathered, raw, hist_amp)


def cuts_of(rows):
    step = max(16, -(-rows // 64) * 16)
    return [(at, min(step, rows - at)) for at in range(0, rows, step)]


def make(mesh):
    row_n, col_n = mesh.shape["row"], mesh.shape["col"]
    total = row_n * col_n

    def send_col(x, m):
        return lax.ppermute(x, "col", [(i, i ^ m) for i in range(col_n)])

    def send_row(x, m):
        return lax.ppermute(x, "row", [(i, i ^ m) for i in range(row_n)])

    def on_device(
        integrals, lambda2, source_terms, hist_amp, hist_err, eps_occ, eps_vir, occ_pair, vir_pair
    ):
        rows, width = source_terms.shape
        depth = lambda2.shape[1]
        near = lambda2.shape[0] // rows
        r, c = lax.axis_index("row"), lax.axis_index("col")
        zi = r // near
        low = lax.rem(zi, 2) == lax.rem(c, 2)

        def multiply(piece):
            out = jnp.dot(
                piece.reshape(-1, depth), integrals, preferred_element_type=f32
            )
            return out.reshape(near, -1, width)

        def over_near(part):
            bit = 1
            while part.shape[0] > 1:
                halves = part.reshape(part.shape[0] // 2, 2, *part.shape[1:])
                mine = (r // bit) % 2 == 0
                send = jnp.where(mine, halves[:, 1], halves[:, 0])
                keep = jnp.where(mine, halves[:, 0], halves[:, 1])
                part = keep + send_row(send.astype(wire), bit).astype(f32)
                bit *= 2
            return part[0]

        def over_pair(first, second):
            send = jnp.where(low, second, first)
            keep = jnp.where(low, first, second)
            return keep + send_row(send.astype(wire), near).astype(f32)

        def over_far(part, pair):
            kept = jnp.where(zi // 2 == (c // 2) ^ pair, part, 0.0)
            data = part.astype(wire)
            for d in range(1, col_n // 2):
                links = []
                for z in range(col_n):
                    for y in range(col_n):
                        if (z // 2) ^ (y // 2) ^ pair == d:
                            for x in range(near):
                                source = (z * near + x) * col_n + y
                                target = ((z ^ (2 * d)) * near + x) * col_n + y
                                links.append((source, target))
                kept = kept + lax.ppermute(data, ("row", "col"), links).astype(f32)
            return kept

        own = lambda2.reshape(near, rows, depth)
        cuts = cuts_of(rows)
        pieces = [own[:, at : at + size] for at, size in cuts]
        far = {
            (m, q): send_col(piece, m)
            for m in range(2, col_n, 2)
            for q, piece in enumerate(pieces)
        }
        sibling = send_col(own, 1)
        part = over_pair(over_near(multiply(own)), over_near(multiply(sibling)))
        ladder = over_far(part, 0)
        for m in range(2, col_n, 2):
            done = []
            for q in range(len(cuts)):
                other = send_col(far[m, q], 1)
                part = over_pair(
                    over_near(multiply(far[m, q])), over_near(multiply(other))
                )
                done.append(over_far(part, m // 2))
            ladder = ladder + jnp.concatenate(done, axis=0)

        occ_energy = jnp.broadcast_to(pair_energy(occ_pair, eps_occ)[:, None], (rows, 128))
        vir_energy = pair_energy(vir_pair, eps_vir)[None, :]
        stored = stored_products(hist_err)
        raw, fresh = new_products(
            ladder, source_terms, occ_energy, vir_energy, hist_amp, hist_err
        )
        count = hist_err.shape[0]
        pairs = count * (count + 1) // 2
        sums = jnp.concatenate(
            [jnp.sum(stored, axis=1)[:pairs], jnp.sum(fresh, axis=1)[: count + 1]]
        )
        tile = jnp.zeros((8, 128), f32).at[0, : sums.shape[0]].set(sums)
        gathered = lax.all_to_all(
            jnp.broadcast_to(tile[None], (total, 8, 128)), ("row", "col"), 0, 0, tiled=True
        )
        return extrapolate(gathered, raw, hist_amp)

    return on_device


def solution(mesh):
    placed = (
        P("row", "col"),
        P("col", "row"),
        P("row", "col"),
        P(None, "row", "col"),
        P(None, "row", "col"),
        P(),
        P(),
        P(None, "row"),
        P(None, "col"),
    )
    return jax.shard_map(
        make(mesh), mesh=mesh, in_specs=placed, out_specs=P("row", "col"), check_vma=False
    )
```

time: 371 us -> 166 us (0.45)
  blocking collectives: 214 us -> 10.6 us
  between operations: 40.8 us -> 0.45 us
  starting transfers between devices: 1.48 us -> 33.5 us
  matrix products: 41.7 us -> 18.6 us
  Pallas kernels: 0 us -> 17.4 us
  waiting for transfers between devices: 47.3 us -> 62.2 us
    unnamed x1 -> x0, blocking collectives: 169 us -> none
    ppermute x0 -> x29, waiting for transfers between devices: none -> 62.2 us  [the longest x5 27.4 us: over_far(): kept = kept + lax.ppermute(data, ('row', 'col'), links).astype(f32)]
    psum x1 -> x0, blocking collectives: 45.2 us -> none  [on_device(): lax.psum(jnp.dot(stacked, flat_new[0], precision=precise), ('row', 'col'))]
    all_gather x1 -> x0, waiting for transfers between devices: 44.2 us -> none  [on_device(): all_cols = lax.all_gather(lambda2, 'col', axis=0, tiled=True)]
    ppermute x0 -> x29, starting transfers between devices: none -> 33.5 us  [the longest x15 15.2 us: send_row(): return lax.ppermute(x, 'row', [(i, i ^ m) for i in range(row_n)])]
    dot_general x3 -> x10, matrix products: 41.7 us -> 18.6 us  [multiply(): jnp.dot(piece.reshape(-1, depth), integrals, preferred_element_type=f32)]
    pallas_call x0 -> x3, Pallas kernels: none -> 17.4 us  [the longest x1 8.14 us: new_products(): pl.pallas_call(kernel, grid=(width // block,), in_specs=[pl.BlockSpec((ro...]
    all_to_all x0 -> x1, blocking collectives: none -> 10.6 us  [on_device(): lax.all_to_all(jnp.broadcast_to(tile[None], (total, 8, 128)), ('row', 'co...]
  transfers between devices with their start and end apart: 2 -> 29, of which waited for: 2 -> 13; matrix products, arithmetic and copies ran while one was open for 5% -> 21% of each run, Pallas kernels for 0% -> 3%
where the time goes in v1:
time: 166 us; the launch traced here: 165 us
  waiting for transfers between devices  62.2 us (37%)
  starting transfers between devices  33.5 us (20%)
  matrix products  18.6 us (11%)
  Pallas kernels  17.4 us (10%)
  local copies, waits for them, and re-layouts  11.4 us (7%)
  other arithmetic  10.9 us (7%)
  blocking collectives  10.6 us (6%)
    ppermute x5, waiting for transfers between devices, over_far(): kept = kept + lax.ppermute(data, ('row', 'col'), links).astype(f32)  27.4 us
    ppermute x15, waiting for transfers between devices, send_row(): return lax.ppermute(x, 'row', [(i, i ^ m) for i in range(row_n)])  19.5 us
    dot_general x10, matrix products, multiply(): jnp.dot(piece.reshape(-1, depth), integrals, preferred_element_type=f32)  18.6 us
    ppermute x9, waiting for transfers between devices, send_col(): return lax.ppermute(x, 'col', [(i, i ^ m) for i in range(col_n)])  15.3 us
    ppermute x15, starting transfers between devices, send_row(): return lax.ppermute(x, 'row', [(i, i ^ m) for i in range(row_n)])  15.2 us
    ppermute x5, starting transfers between devices, over_far(): kept = kept + lax.ppermute(data, ('row', 'col'), links).astype(f32)  12.9 us
    all_to_all x1, blocking collectives, on_device(): lax.all_to_all(jnp.broadcast_to(tile[None], (total, 8, 128)), ('row', 'co...  10.6 us
    pallas_call x1, Pallas kernels, new_products(): pl.pallas_call(kernel, grid=(width // block,), in_specs=[pl.BlockSpec((ro...  8.14 us
  transfers between devices with their start and end apart: 29, of which 13 were waited for; matrix products, arithmetic and copies ran while one was open for 21% of the time, Pallas kernels for 3%

profile of v1, /device:TPU:0, one launch (start us, length us, event | category | flops | bytes accessed | tf_op | source)
XLA Modules:
  0.0 165.0 jit_solution(2284732054469957072)
XLA Ops:
  0.0 2.0 %reshape.629 = bf16[2,252,2048]{2,1,0:T(8,128)(2,1)S(1)} reshape(bf16[504,2048]{1,0:T(8,128)(2,1)} %param.12) | data formatting | bytes 4128768 | tf_op jit(solution)/shard_map/reshape | solution.py:233
  2.8 3.0 %collective-permute-start.23 = (bf16[2,60,2048]{2,1,0:T(8,128)(2,1)}, bf16[2,60,2048]{2,1,0:T(8,128)(2,1)}, u32[]{:S(2)}, u32[]{:S(2)}) collective-permute-start(bf16[2,60,2048]{2,1,0:T(8,128)(2,1)} %slice.175), channel_id=1, source_target_pairs={{0,2},{1,3},{2,0},{3,1},{4,6},{5,7},{6,4},{7,5},{8,10},{9,11},{10,... | collective-permute-start | bytes 1474568 | tf_op jit(solution)/shard_map/ppermute | solution.py:181
  7.0 2.0 %collective-permute-start.11 = (bf16[2,64,2048]{2,1,0:T(8,128)(2,1)}, bf16[2,64,2048]{2,1,0:T(8,128)(2,1)S(1)}, u32[]{:S(2)}, u32[]{:S(2)}) collective-permute-start(bf16[2,64,2048]{2,1,0:T(8,128)(2,1)} %get-tuple-element.42), channel_id=1, source_target_pairs={{0,2},{1,3},{2,0},{3,1},{4,6},{5,7},{6,4},{7,5},{8,10},{9,11},{10,... | collective-permute-start | bytes 1572872 | tf_op jit(solution)/shard_map/ppermute | solution.py:181
  9.1 6.4 %fusion.71 = f32[504,1024]{1,0:T(8,128)} fusion(bf16[504,2048]{1,0:T(8,128)(2,1)} %param.12, bf16[2048,1024]{1,0:T(8,128)(2,1)} %param.11), kind=kOutput, calls=%fused_computation.95 | convolution fusion | flops 2113929216 | bytes 8323072 | tf_op jit(solution)/shard_map/dot_general | solution.py:197
  15.5 3.1 %reshape_reshape.2 = f32[1,2,252,1024]{3,2,1,0:T(8,128)} reshape(f32[504,1024]{1,0:T(8,128)} %fusion.71) | data formatting | bytes 4128768 | tf_op jit(solution)/shard_map/reshape;reshape | solution.py:205
  18.6 2.6 %fusion.48 = f16[1,252,1024]{2,1,0:T(8,128)(2,1)} fusion(f32[1,2,252,1024]{3,2,1,0:T(8,128)} %reshape_reshape.2, pred[]{:T(512)S(6)} %eq.97), kind=kLoop, calls=%fused_computation.39 | loop fusion | flops 516096 | bytes 2580481 | tf_op jit(solution)/shard_map/convert_element_type | solution.py:209
  21.2 1.9 %collective-permute-start = (f16[1,252,1024]{2,1,0:T(8,128)(2,1)}, f16[1,252,1024]{2,1,0:T(8,128)(2,1)}, u32[]{:S(2)}, u32[]{:S(2)}) collective-permute-start(f16[1,252,1024]{2,1,0:T(8,128)(2,1)} %fusion.48), channel_id=1, source_target_pairs={{0,4},{4,0},{8,12},{12,8},{16,20},{20,16},{24,28},{28,24},{1,5},{5... | collective-permute-start | bytes 1548296 | tf_op jit(solution)/shard_map/ppermute | solution.py:184
  23.2 3.4 %copy.12 = bf16[2,252,2048]{2,0,1:T(2,128)(2,1)} copy(bf16[2,252,2048]{2,1,0:T(8,128)(2,1)S(1)} %reshape.629) | data formatting | bytes 4128768 | tf_op jit(solution)/shard_map/reshape | solution.py:233
  28.1 4.4 %shard_map.91 = f32[16,1024]{1,0:T(8,128)} custom-call(bf16[5,252,1024]{2,1,0:T(8,128)(2,1)} %err_ref.3), custom_call_target="tpu_custom_call" | custom-call | flops 7741440 | bytes 2580480 | tf_op jit(solution)/shard_map/pallas_call | solution.py:57
  33.6 3.2 %fusion.42 = f32[1,2,60,1024]{3,2,1,0:T(8,128)S(1)} fusion(bf16[2,60,2048]{2,1,0:T(8,128)(2,1)} %collective-permute-done.23, bf16[2048,1024]{1,0:T(8,128)(2,1)} %param.11), kind=kOutput, calls=%fused_computation.30 | convolution fusion | flops 503316480 | bytes 5177344 | tf_op jit(solution)/shard_map/dot_general | solution.py:197
  37.1 1.8 %fusion.36 = f32[1,2,64,1024]{3,2,1,0:T(8,128)S(1)} fusion(bf16[2,64,2048]{2,1,0:T(8,128)(2,1)} %collective-permute-done.17, bf16[2048,1024]{1,0:T(8,128)(2,1)S(1)} %copy-done), kind=kOutput, calls=%fused_computation.28 | convolution fusion | flops 536870912 | bytes 5242880 | tf_op jit(solution)/shard_map/dot_general | solution.py:197
  38.9 2.3 %collective-permute-done.11 = bf16[2,64,2048]{2,1,0:T(8,128)(2,1)S(1)} collective-permute-done((bf16[2,64,2048]{2,1,0:T(8,128)(2,1)}, bf16[2,64,2048]{2,1,0:T(8,128)(2,1)S(1)}, u32[]{:S(2)}, u32[]{:S(2)}) %collective-permute-start.11) | collective-permute-done | bytes 524320 | tf_op jit(solution)/shard_map/ppermute | solution.py:181
  42.0 9.7 %collective-permute-done.5 = bf16[2,64,2048]{2,1,0:T(8,128)(2,1)S(1)} collective-permute-done((bf16[2,64,2048]{2,1,0:T(8,128)(2,1)}, bf16[2,64,2048]{2,1,0:T(8,128)(2,1)S(1)}, u32[]{:S(2)}, u32[]{:S(2)}) %collective-permute-start.5) | collective-permute-done | bytes 524320 | tf_op jit(solution)/shard_map/ppermute | solution.py:181
  51.6 1.7 %collective-permute-start.18 = (f16[1,64,1024]{2,1,0:T(8,128)(2,1)S(1)}, f16[1,64,1024]{2,1,0:T(8,128)(2,1)S(1)}, u32[]{:S(2)}, u32[]{:S(2)}) collective-permute-start(f16[1,64,1024]{2,1,0:T(8,128)(2,1)S(1)} %fusion.58), channel_id=1, source_target_pairs={{0,4},{4,0},{8,12},{12,8},{16,20},{20,16},{24,28},{28,24},{1,5},{5... | collective-permute-start | bytes 393224 | tf_op jit(solution)/shard_map/ppermute | solution.py:184
  61.3 1.8 %collective-permute-start.12 = (f16[1,64,1024]{2,1,0:T(8,128)(2,1)S(1)}, f16[1,64,1024]{2,1,0:T(8,128)(2,1)S(1)}, u32[]{:S(2)}, u32[]{:S(2)}) collective-permute-start(f16[1,64,1024]{2,1,0:T(8,128)(2,1)S(1)} %fusion.55), channel_id=1, source_target_pairs={{0,4},{4,0},{8,12},{12,8},{16,20},{20,16},{24,28},{28,24},{1,5},{5... | collective-permute-start | bytes 393224 | tf_op jit(solution)/shard_map/ppermute | solution.py:184
  63.1 3.5 %collective-permute-done.26 = f16[1,60,1024]{2,1,0:T(8,128)(2,1)S(1)} collective-permute-done((f16[1,60,1024]{2,1,0:T(8,128)(2,1)S(1)}, f16[1,60,1024]{2,1,0:T(8,128)(2,1)S(1)}, u32[]{:S(2)}, u32[]{:S(2)}) %collective-permute-start.26) | collective-permute-done | bytes 122912 | tf_op jit(solution)/shard_map/ppermute | solution.py:184
  66.7 2.1 %collective-permute-start.6 = (f16[1,64,1024]{2,1,0:T(8,128)(2,1)S(1)}, f16[1,64,1024]{2,1,0:T(8,128)(2,1)S(1)}, u32[]{:S(2)}, u32[]{:S(2)}) collective-permute-start(f16[1,64,1024]{2,1,0:T(8,128)(2,1)S(1)} %fusion.52), channel_id=1, source_target_pairs={{0,4},{4,0},{8,12},{12,8},{16,20},{20,16},{24,28},{28,24},{1,5},{5... | collective-permute-start | bytes 393224 | tf_op jit(solution)/shard_map/ppermute | solution.py:184
  68.8 4.2 %collective-permute-done.20 = f16[1,64,1024]{2,1,0:T(8,128)(2,1)S(1)} collective-permute-done((f16[1,64,1024]{2,1,0:T(8,128)(2,1)S(1)}, f16[1,64,1024]{2,1,0:T(8,128)(2,1)S(1)}, u32[]{:S(2)}, u32[]{:S(2)}) %collective-permute-start.20) | collective-permute-done | bytes 131104 | tf_op jit(solution)/shard_map/ppermute | solution.py:184
  73.1 2.1 %collective-permute-start.8 = (f16[1,64,1024]{2,1,0:T(8,128)(2,1)S(1)}, f16[1,64,1024]{2,1,0:T(8,128)(2,1)S(1)}, u32[]{:S(2)}, u32[]{:S(2)}) collective-permute-start(f16[1,64,1024]{2,1,0:T(8,128)(2,1)S(1)} %fusion.53), channel_id=1, source_target_pairs={{0,4},{4,0},{8,12},{12,8},{16,20},{20,16},{24,28},{28,24},{1,5},{5... | collective-permute-start | bytes 393224 | tf_op jit(solution)/shard_map/ppermute | solution.py:184
  75.2 3.2 %collective-permute-done.14 = f16[1,64,1024]{2,1,0:T(8,128)(2,1)S(1)} collective-permute-done((f16[1,64,1024]{2,1,0:T(8,128)(2,1)S(1)}, f16[1,64,1024]{2,1,0:T(8,128)(2,1)S(1)}, u32[]{:S(2)}, u32[]{:S(2)}) %collective-permute-start.14) | collective-permute-done | bytes 131104 | tf_op jit(solution)/shard_map/ppermute | solution.py:184
  78.4 1.6 collective-permute-start.27
  80.6 2.8 %fusion.19 = f32[1,2,252,1024]{3,2,1,0:T(8,128)S(1)} fusion(bf16[2048,1024]{1,0:T(8,128)(2,1)S(1)} %copy-done, bf16[2,252,2048]{2,0,1:T(2,128)(2,1)S(1)} %collective-permute-done.1), kind=kOutput, calls=%fused_computation.23 | convolution fusion | flops 2113929216 | bytes 8323072 | tf_op jit(solution)/shard_map/dot_general | solution.py:197
  83.6 1.6 collective-permute-start.15
  86.7 4.5 %collective-permute-start.28 = (f16[60,1024]{1,0:T(8,128)(2,1)S(1)}, f16[60,1024]{1,0:T(8,128)(2,1)S(1)}, u32[]{:S(2)}, u32[]{:S(2)}) collective-permute-start(f16[60,1024]{1,0:T(8,128)(2,1)S(1)} %fusion.67), channel_id=1, source_target_pairs={{0,16},{4,20},{1,17},{5,21},{8,24},{12,28},{9,25},{13,29},{18,2},{... | collective-permute-start | bytes 368648 | tf_op jit(solution)/shard_map/ppermute | solution.py:230
  92.6 2.8 %collective-permute-done.2 = f16[1,252,1024]{2,1,0:T(8,128)(2,1)S(1)} collective-permute-done((f16[1,252,1024]{2,1,0:T(8,128)(2,1)S(1)}, f16[1,252,1024]{2,1,0:T(8,128)(2,1)S(1)}, u32[]{:S(2)}, u32[]{:S(2)}) %collective-permute-start.2) | collective-permute-done | bytes 516128 | tf_op jit(solution)/shard_map/ppermute | solution.py:184
  95.3 1.8 %fusion.50 = (f16[252,1024]{1,0:T(8,128)(2,1)S(1)}, f32[1,252,1024]{2,1,0:T(8,128)S(1)}, f32[1,252,1024]{2,1,0:T(8,128)S(1)}) fusion(pred[]{:T(512)S(6)} %eq.96, f16[1,252,1024]{2,1,0:T(8,128)(2,1)} %collective-permute-done, f32[1,2,252,1024]{3,2,1,0:T(8,128)S(1)} %copy-done.1, pred[]{:T(512)S(6)} %eq.97, ...), kind=kLoop, calls=%fused_computation.41 | loop fusion | flops 2064384 | bytes 7741442 | tf_op jit(solution)/shard_map/convert_element_type | solution.py:216
  97.7 4.5 %collective-permute-start.16 = (f16[64,1024]{1,0:T(8,128)(2,1)S(1)}, f16[64,1024]{1,0:T(8,128)(2,1)S(1)}, u32[]{:S(2)}, u32[]{:S(2)}) collective-permute-start(f16[64,1024]{1,0:T(8,128)(2,1)S(1)} %fusion.65), channel_id=1, source_target_pairs={{0,16},{4,20},{1,17},{5,21},{8,24},{12,28},{9,25},{13,29},{18,2},{... | collective-permute-start | bytes 393224 | tf_op jit(solution)/shard_map/ppermute | solution.py:230
  103.7 5.5 %collective-permute-done.3 = f16[252,1024]{1,0:T(8,128)(2,1)S(1)} collective-permute-done((f16[252,1024]{1,0:T(8,128)(2,1)S(1)}, f16[252,1024]{1,0:T(8,128)(2,1)S(1)}, u32[]{:S(2)}, u32[]{:S(2)}) %collective-permute-start.3) | collective-permute-done | bytes 516128 | tf_op jit(solution)/shard_map/ppermute | solution.py:184
  112.0 26.3 %collective-permute-done.4 = f16[252,1024]{1,0:T(8,128)(2,1)S(1)} collective-permute-done((f16[252,1024]{1,0:T(8,128)(2,1)S(1)}, f16[252,1024]{1,0:T(8,128)(2,1)S(1)}, u32[]{:S(2)}, u32[]{:S(2)}) %collective-permute-start.4) | collective-permute-done | bytes 516128 | tf_op jit(solution)/shard_map/ppermute | solution.py:230
  140.5 8.1 %shard_map.92 = (f32[252,1024]{1,0:T(8,128)}, f32[8,1024]{1,0:T(8,128)}) custom-call(f32[252,1024]{1,0:T(8,128)} %maximum_add_fusion.lad_ref, f32[252,1024]{1,0:T(8,128)} %src_ref.1, f32[252,128]{1,0:T(8,128)} %broadcast_in_dim.75.occ_ref, f32[1,1024]{1,0:T(1,128)} %bitcast.164, bf16[5,252,1024]{2,1,0:T(8,128)(2,1)} %amp_ref.3, bf16[5,252,1024]{2,1,0:T(8,128)(2,1)} %err_ref.3), custom_call_target="tpu_custom_call" | custom-call | flops 5160960 | bytes 6193152 | tf_op jit(solution)/shard_map/pallas_call | solution.py:87
  149.6 10.6 %all_to_all.5.sum_ref = f32[32,8,128]{2,1,0:T(8,128)} all-to-all(f32[32,8,128]{2,1,0:T(8,128)S(1)} %broadcast_in_dim.79), channel_id=1, replica_groups=mesh['row'=8,'col'=4] {'row','col'}, dimensions={0} | all-to-all | bytes 262144 | tf_op jit(solution)/shard_map/all_to_all | solution.py:266
  160.2 4.8 %shard_map.93 = f32[252,1024]{1,0:T(8,128)} custom-call(f32[32,8,128]{2,1,0:T(8,128)} %all_to_all.5.sum_ref, f32[252,1024]{1,0:T(8,128)} %get-tuple-element.20.raw_ref, bf16[5,252,1024]{2,1,0:T(8,128)(2,1)} %amp_ref.3), custom_call_target="tpu_custom_call" | custom-call | tf_op jit(solution)/shard_map/pallas_call | solution.py:158
  (94 shorter events, 25.3 us)
Async XLA Ops:
  2.8 30.7 %collective-permute-start.23 = (bf16[2,60,2048]{2,1,0:T(8,128)(2,1)}, bf16[2,60,2048]{2,1,0:T(8,128)(2,1)}, u32[]{:S(2)}, u32[]{:S(2)}) collective-permute-start(bf16[2,60,2048]{2,1,0:T(8,128)(2,1)} %slice.175), channel_id=1, source_target_pairs={{0,2},{1,3},{2,0},{3,1},{4,6},{5,7},{6,4},{7,5},{8,10},{9,11},{10,... | collective-permute-start | bytes 1474568 | tf_op jit(solution)/shard_map/ppermute | solution.py:181
  7.0 29.8 %collective-permute-start.17 = (bf16[2,64,2048]{2,1,0:T(8,128)(2,1)}, bf16[2,64,2048]{2,1,0:T(8,128)(2,1)}, u32[]{:S(2)}, u32[]{:S(2)}) collective-permute-start(bf16[2,64,2048]{2,1,0:T(8,128)(2,1)} %get-tuple-element.41), channel_id=1, source_target_pairs={{0,2},{1,3},{2,0},{3,1},{4,6},{5,7},{6,4},{7,5},{8,10},{9,11},{10,... | collective-permute-start | bytes 1572872 | tf_op jit(solution)/shard_map/ppermute | solution.py:181
  7.0 34.2 %collective-permute-start.11 = (bf16[2,64,2048]{2,1,0:T(8,128)(2,1)}, bf16[2,64,2048]{2,1,0:T(8,128)(2,1)S(1)}, u32[]{:S(2)}, u32[]{:S(2)}) collective-permute-start(bf16[2,64,2048]{2,1,0:T(8,128)(2,1)} %get-tuple-element.42), channel_id=1, source_target_pairs={{0,2},{1,3},{2,0},{3,1},{4,6},{5,7},{6,4},{7,5},{8,10},{9,11},{10,... | collective-permute-start | bytes 1572872 | tf_op jit(solution)/shard_map/ppermute | solution.py:181
  9.0 42.6 %collective-permute-start.5 = (bf16[2,64,2048]{2,1,0:T(8,128)(2,1)}, bf16[2,64,2048]{2,1,0:T(8,128)(2,1)S(1)}, u32[]{:S(2)}, u32[]{:S(2)}) collective-permute-start(bf16[2,64,2048]{2,1,0:T(8,128)(2,1)} %get-tuple-element.40), channel_id=1, source_target_pairs={{0,2},{1,3},{2,0},{3,1},{4,6},{5,7},{6,4},{7,5},{8,10},{9,11},{10,... | collective-permute-start | bytes 1572872 | tf_op jit(solution)/shard_map/ppermute | solution.py:181
  18.6 8.1 %copy-start.2 = (s32[2,1024]{1,0:T(2,128)S(1)}, s32[2,1024]{1,0:T(2,128)}, u32[]{:S(2)}) copy-start(s32[2,1024]{1,0:T(2,128)} %param.19) | copy-start | bytes 24580
  18.6 8.1 %copy-start.3 = (f32[800]{0:T(1024)S(1)}, f32[800]{0:T(1024)}, u32[]{:S(2)}) copy-start(f32[800]{0:T(1024)} %param.17) | copy-start | bytes 9604
  21.2 70.0 %collective-permute-start = (f16[1,252,1024]{2,1,0:T(8,128)(2,1)}, f16[1,252,1024]{2,1,0:T(8,128)(2,1)}, u32[]{:S(2)}, u32[]{:S(2)}) collective-permute-start(f16[1,252,1024]{2,1,0:T(8,128)(2,1)} %fusion.48), channel_id=1, source_target_pairs={{0,4},{4,0},{8,12},{12,8},{16,20},{20,16},{24,28},{28,24},{1,5},{5... | collective-permute-start | bytes 1548296 | tf_op jit(solution)/shard_map/ppermute | solution.py:184
  33.5 46.6 %collective-permute-start.1 = (bf16[2,252,2048]{2,0,1:T(2,128)(2,1)}, bf16[2,252,2048]{2,0,1:T(2,128)(2,1)S(1)}, u32[]{:S(2)}, u32[]{:S(2)}) collective-permute-start(bf16[2,252,2048]{2,0,1:T(2,128)(2,1)} %copy.12), channel_id=1, source_target_pairs={{0,1},{1,0},{2,3},{3,2},{4,5},{5,4},{6,7},{7,6},{8,9},{9,8},{10,11... | collective-permute-start | bytes 6193160 | tf_op jit(solution)/shard_map/ppermute | solution.py:181
  36.8 24.4 %collective-permute-start.24 = (f16[1,60,1024]{2,1,0:T(8,128)(2,1)S(1)}, f16[1,60,1024]{2,1,0:T(8,128)(2,1)S(1)}, u32[]{:S(2)}, u32[]{:S(2)}) collective-permute-start(f16[1,60,1024]{2,1,0:T(8,128)(2,1)S(1)} %fusion.61), channel_id=1, source_target_pairs={{0,4},{4,0},{8,12},{12,8},{16,20},{20,16},{24,28},{28,24},{1,5},{5... | collective-permute-start | bytes 368648 | tf_op jit(solution)/shard_map/ppermute | solution.py:184
  41.2 12.9 %collective-permute-start.25 = (bf16[2,60,2048]{2,1,0:T(8,128)(2,1)}, bf16[2,60,2048]{2,1,0:T(8,128)(2,1)S(1)}, u32[]{:S(2)}, u32[]{:S(2)}) collective-permute-start(bf16[2,60,2048]{2,1,0:T(8,128)(2,1)} %collective-permute-done.23), channel_id=1, source_target_pairs={{0,1},{1,0},{2,3},{3,2},{4,5},{5,4},{6,7},{7,6},{8,9},{9,8},{10,11... | collective-permute-start | bytes 1474568 | tf_op jit(solution)/shard_map/ppermute | solution.py:181
  51.6 15.0 %collective-permute-start.18 = (f16[1,64,1024]{2,1,0:T(8,128)(2,1)S(1)}, f16[1,64,1024]{2,1,0:T(8,128)(2,1)S(1)}, u32[]{:S(2)}, u32[]{:S(2)}) collective-permute-start(f16[1,64,1024]{2,1,0:T(8,128)(2,1)S(1)} %fusion.58), channel_id=1, source_target_pairs={{0,4},{4,0},{8,12},{12,8},{16,20},{20,16},{24,28},{28,24},{1,5},{5... | collective-permute-start | bytes 393224 | tf_op jit(solution)/shard_map/ppermute | solution.py:184
  54.2 2.2 %collective-permute-start.19 = (bf16[2,64,2048]{2,1,0:T(8,128)(2,1)}, bf16[2,64,2048]{2,1,0:T(8,128)(2,1)S(1)}, u32[]{:S(2)}, u32[]{:S(2)}) collective-permute-start(bf16[2,64,2048]{2,1,0:T(8,128)(2,1)} %collective-permute-done.17), channel_id=1, source_target_pairs={{0,1},{1,0},{2,3},{3,2},{4,5},{5,4},{6,7},{7,6},{8,9},{9,8},{10,11... | collective-permute-start | bytes 1572872 | tf_op jit(solution)/shard_map/ppermute | solution.py:181
  56.4 1.9 %collective-permute-start.13 = (bf16[2,64,2048]{2,1,0:T(8,128)(2,1)S(1)}, bf16[2,64,2048]{2,1,0:T(8,128)(2,1)S(1)}, u32[]{:S(2)}, u32[]{:S(2)}) collective-permute-start(bf16[2,64,2048]{2,1,0:T(8,128)(2,1)S(1)} %collective-permute-done.11), channel_id=1, source_target_pairs={{0,1},{1,0},{2,3},{3,2},{4,5},{5,4},{6,7},{7,6},{8,9},{9,8},{10,11... | collective-permute-start | bytes 1572872 | tf_op jit(solution)/shard_map/ppermute | solution.py:181
  58.3 1.9 %collective-permute-start.7 = (bf16[2,64,2048]{2,1,0:T(8,128)(2,1)S(1)}, bf16[2,64,2048]{2,1,0:T(8,128)(2,1)S(1)}, u32[]{:S(2)}, u32[]{:S(2)}) collective-permute-start(bf16[2,64,2048]{2,1,0:T(8,128)(2,1)S(1)} %collective-permute-done.5), channel_id=1, source_target_pairs={{0,1},{1,0},{2,3},{3,2},{4,5},{5,4},{6,7},{7,6},{8,9},{9,8},{10,11... | collective-permute-start | bytes 1572872 | tf_op jit(solution)/shard_map/ppermute | solution.py:181
  60.2 6.3 %collective-permute-start.26 = (f16[1,60,1024]{2,1,0:T(8,128)(2,1)S(1)}, f16[1,60,1024]{2,1,0:T(8,128)(2,1)S(1)}, u32[]{:S(2)}, u32[]{:S(2)}) collective-permute-start(f16[1,60,1024]{2,1,0:T(8,128)(2,1)S(1)} %fusion.62), channel_id=1, source_target_pairs={{0,4},{4,0},{8,12},{12,8},{16,20},{20,16},{24,28},{28,24},{1,5},{5... | collective-permute-start | bytes 368648 | tf_op jit(solution)/shard_map/ppermute | solution.py:184
  61.3 11.8 %collective-permute-start.12 = (f16[1,64,1024]{2,1,0:T(8,128)(2,1)S(1)}, f16[1,64,1024]{2,1,0:T(8,128)(2,1)S(1)}, u32[]{:S(2)}, u32[]{:S(2)}) collective-permute-start(f16[1,64,1024]{2,1,0:T(8,128)(2,1)S(1)} %fusion.55), channel_id=1, source_target_pairs={{0,4},{4,0},{8,12},{12,8},{16,20},{20,16},{24,28},{28,24},{1,5},{5... | collective-permute-start | bytes 393224 | tf_op jit(solution)/shard_map/ppermute | solution.py:184
  66.5 6.4 %collective-permute-start.20 = (f16[1,64,1024]{2,1,0:T(8,128)(2,1)S(1)}, f16[1,64,1024]{2,1,0:T(8,128)(2,1)S(1)}, u32[]{:S(2)}, u32[]{:S(2)}) collective-permute-start(f16[1,64,1024]{2,1,0:T(8,128)(2,1)S(1)} %fusion.59), channel_id=1, source_target_pairs={{0,4},{4,0},{8,12},{12,8},{16,20},{20,16},{24,28},{28,24},{1,5},{5... | collective-permute-start | bytes 393224 | tf_op jit(solution)/shard_map/ppermute | solution.py:184
  66.7 16.9 %collective-permute-start.6 = (f16[1,64,1024]{2,1,0:T(8,128)(2,1)S(1)}, f16[1,64,1024]{2,1,0:T(8,128)(2,1)S(1)}, u32[]{:S(2)}, u32[]{:S(2)}) collective-permute-start(f16[1,64,1024]{2,1,0:T(8,128)(2,1)S(1)} %fusion.52), channel_id=1, source_target_pairs={{0,4},{4,0},{8,12},{12,8},{16,20},{20,16},{24,28},{28,24},{1,5},{5... | collective-permute-start | bytes 393224 | tf_op jit(solution)/shard_map/ppermute | solution.py:184
  73.0 5.4 %collective-permute-start.14 = (f16[1,64,1024]{2,1,0:T(8,128)(2,1)S(1)}, f16[1,64,1024]{2,1,0:T(8,128)(2,1)S(1)}, u32[]{:S(2)}, u32[]{:S(2)}) collective-permute-start(f16[1,64,1024]{2,1,0:T(8,128)(2,1)S(1)} %fusion.56), channel_id=1, source_target_pairs={{0,4},{4,0},{8,12},{12,8},{16,20},{20,16},{24,28},{28,24},{1,5},{5... | collective-permute-start | bytes 393224 | tf_op jit(solution)/shard_map/ppermute | solution.py:184
  73.1 12.2 %collective-permute-start.8 = (f16[1,64,1024]{2,1,0:T(8,128)(2,1)S(1)}, f16[1,64,1024]{2,1,0:T(8,128)(2,1)S(1)}, u32[]{:S(2)}, u32[]{:S(2)}) collective-permute-start(f16[1,64,1024]{2,1,0:T(8,128)(2,1)S(1)} %fusion.53), channel_id=1, source_target_pairs={{0,4},{4,0},{8,12},{12,8},{16,20},{20,16},{24,28},{28,24},{1,5},{5... | collective-permute-start | bytes 393224 | tf_op jit(solution)/shard_map/ppermute | solution.py:184
  78.4 7.5 %collective-permute-start.27 = (f16[60,1024]{1,0:T(8,128)(2,1)S(1)}, f16[60,1024]{1,0:T(8,128)(2,1)S(1)}, u32[]{:S(2)}, u32[]{:S(2)}) collective-permute-start(f16[60,1024]{1,0:T(8,128)(2,1)S(1)} %get-tuple-element.37), channel_id=1, source_target_pairs={{0,8},{4,12},{8,0},{12,4},{16,24},{20,28},{24,16},{28,20},{1,9},{5... | collective-permute-start | bytes 368648 | tf_op jit(solution)/shard_map/ppermute | solution.py:184
  80.1 6.6 %collective-permute-start.21 = (f16[64,1024]{1,0:T(8,128)(2,1)S(1)}, f16[64,1024]{1,0:T(8,128)(2,1)S(1)}, u32[]{:S(2)}, u32[]{:S(2)}) collective-permute-start(f16[64,1024]{1,0:T(8,128)(2,1)S(1)} %get-tuple-element.34), channel_id=1, source_target_pairs={{0,8},{4,12},{8,0},{12,4},{16,24},{20,28},{24,16},{28,20},{1,9},{5... | collective-permute-start | bytes 393224 | tf_op jit(solution)/shard_map/ppermute | solution.py:184
  83.4 12.0 %copy-start.1 = (f32[1,2,252,1024]{3,2,1,0:T(8,128)S(1)}, f32[1,2,252,1024]{3,2,1,0:T(8,128)}, u32[]{:S(2)}) copy-start(f32[1,2,252,1024]{3,2,1,0:T(8,128)} %reshape_reshape.2) | copy-start | bytes 6193156
  83.6 14.1 %collective-permute-start.15 = (f16[64,1024]{1,0:T(8,128)(2,1)S(1)}, f16[64,1024]{1,0:T(8,128)(2,1)S(1)}, u32[]{:S(2)}, u32[]{:S(2)}) collective-permute-start(f16[64,1024]{1,0:T(8,128)(2,1)S(1)} %get-tuple-element.31), channel_id=1, source_target_pairs={{0,8},{4,12},{8,0},{12,4},{16,24},{20,28},{24,16},{28,20},{1,9},{5... | collective-permute-start | bytes 393224 | tf_op jit(solution)/shard_map/ppermute | solution.py:184
  85.3 10.1 %collective-permute-start.2 = (f16[1,252,1024]{2,1,0:T(8,128)(2,1)S(1)}, f16[1,252,1024]{2,1,0:T(8,128)(2,1)S(1)}, u32[]{:S(2)}, u32[]{:S(2)}) collective-permute-start(f16[1,252,1024]{2,1,0:T(8,128)(2,1)S(1)} %fusion.49), channel_id=1, source_target_pairs={{0,4},{4,0},{8,12},{12,8},{16,20},{20,16},{24,28},{28,24},{1,5},{5... | collective-permute-start | bytes 1548296 | tf_op jit(solution)/shard_map/ppermute | solution.py:184
  85.9 16.3 %collective-permute-start.9 = (f16[64,1024]{1,0:T(8,128)(2,1)S(1)}, f16[64,1024]{1,0:T(8,128)(2,1)S(1)}, u32[]{:S(2)}, u32[]{:S(2)}) collective-permute-start(f16[64,1024]{1,0:T(8,128)(2,1)S(1)} %get-tuple-element.28), channel_id=1, source_target_pairs={{0,8},{4,12},{8,0},{12,4},{16,24},{20,28},{24,16},{28,20},{1,9},{5... | collective-permute-start | bytes 393224 | tf_op jit(solution)/shard_map/ppermute | solution.py:184
  86.7 16.9 %collective-permute-start.28 = (f16[60,1024]{1,0:T(8,128)(2,1)S(1)}, f16[60,1024]{1,0:T(8,128)(2,1)S(1)}, u32[]{:S(2)}, u32[]{:S(2)}) collective-permute-start(f16[60,1024]{1,0:T(8,128)(2,1)S(1)} %fusion.67), channel_id=1, source_target_pairs={{0,16},{4,20},{1,17},{5,21},{8,24},{12,28},{9,25},{13,29},{18,2},{... | collective-permute-start | bytes 368648 | tf_op jit(solution)/shard_map/ppermute | solution.py:230
  91.2 19.5 %collective-permute-start.22 = (f16[64,1024]{1,0:T(8,128)(2,1)S(1)}, f16[64,1024]{1,0:T(8,128)(2,1)S(1)}, u32[]{:S(2)}, u32[]{:S(2)}) collective-permute-start(f16[64,1024]{1,0:T(8,128)(2,1)S(1)} %fusion.66), channel_id=1, source_target_pairs={{0,16},{4,20},{1,17},{5,21},{8,24},{12,28},{9,25},{13,29},{18,2},{... | collective-permute-start | bytes 393224 | tf_op jit(solution)/shard_map/ppermute | solution.py:230
  97.1 12.0 %collective-permute-start.3 = (f16[252,1024]{1,0:T(8,128)(2,1)S(1)}, f16[252,1024]{1,0:T(8,128)(2,1)S(1)}, u32[]{:S(2)}, u32[]{:S(2)}) collective-permute-start(f16[252,1024]{1,0:T(8,128)(2,1)S(1)} %get-tuple-element.25), channel_id=1, source_target_pairs={{0,8},{4,12},{8,0},{12,4},{16,24},{20,28},{24,16},{28,20},{1,9},{5... | collective-permute-start | bytes 1548296 | tf_op jit(solution)/shard_map/ppermute | solution.py:184
  97.7 13.1 %collective-permute-start.16 = (f16[64,1024]{1,0:T(8,128)(2,1)S(1)}, f16[64,1024]{1,0:T(8,128)(2,1)S(1)}, u32[]{:S(2)}, u32[]{:S(2)}) collective-permute-start(f16[64,1024]{1,0:T(8,128)(2,1)S(1)} %fusion.65), channel_id=1, source_target_pairs={{0,16},{4,20},{1,17},{5,21},{8,24},{12,28},{9,25},{13,29},{18,2},{... | collective-permute-start | bytes 393224 | tf_op jit(solution)/shard_map/ppermute | solution.py:230
  102.3 9.7 %collective-permute-start.10 = (f16[64,1024]{1,0:T(8,128)(2,1)S(1)}, f16[64,1024]{1,0:T(8,128)(2,1)S(1)}, u32[]{:S(2)}, u32[]{:S(2)}) collective-permute-start(f16[64,1024]{1,0:T(8,128)(2,1)S(1)} %fusion.64), channel_id=1, source_target_pairs={{0,16},{4,20},{1,17},{5,21},{8,24},{12,28},{9,25},{13,29},{18,2},{... | collective-permute-start | bytes 393224 | tf_op jit(solution)/shard_map/ppermute | solution.py:230
  109.4 29.0 %collective-permute-start.4 = (f16[252,1024]{1,0:T(8,128)(2,1)S(1)}, f16[252,1024]{1,0:T(8,128)(2,1)S(1)}, u32[]{:S(2)}, u32[]{:S(2)}) collective-permute-start(f16[252,1024]{1,0:T(8,128)(2,1)S(1)} %fusion.51), channel_id=1, source_target_pairs={{2,18},{6,22},{3,19},{7,23},{10,26},{14,30},{11,27},{15,31},{16,0}... | collective-permute-start | bytes 1548296 | tf_op jit(solution)/shard_map/ppermute | solution.py:230
  (3 other events, 19.6 us)

commit v2 on v1

v2 whole, which is shorter than its diff:
```python
import jax
import jax.numpy as jnp
from jax import lax
from jax.experimental import pallas as pl
from jax.experimental.pallas import tpu as pltpu
from jax.sharding import PartitionSpec as P

f32 = jnp.float32
wire = jnp.float16


def pair_energy(pairs, energies):
    levels = jnp.arange(energies.shape[0], dtype=jnp.int32)
    first = jnp.sum(jnp.where(pairs[0][:, None] == levels[None, :], energies[None, :], 0.0), axis=1)
    second = jnp.sum(
        jnp.where(pairs[1][:, None] == levels[None, :], energies[None, :], 0.0), axis=1
    )
    return first + second


def row_steps(rows, step, width, count, term):
    whole = rows // step

    def body(i, acc):
        parts = term(pl.ds(pl.multiple_of(i * step, step), step))
        return tuple(a + jnp.sum(p.reshape(step // 8, 8, width), axis=0) for a, p in zip(acc, parts))

    acc = tuple(jnp.zeros((8, width), f32) for _ in range(count))
    if whole:
        acc = lax.fori_loop(0, whole, body, acc, unroll=min(whole, 5))
    sums = [jnp.sum(a, axis=0, keepdims=True) for a in acc]
    if rows % step:
        parts = term(pl.ds(whole * step, rows % step))
        sums = [s + jnp.sum(p, axis=0, keepdims=True) for s, p in zip(sums, parts)]
    return sums


def column_block(width):
    return 256 if width % 256 == 0 else width


def padded(count):
    return -(-count // 8) * 8


def stored_products(hist_err):
    count, rows, width = hist_err.shape
    block = column_block(width)
    pairs = [(k, m) for k in range(count) for m in range(k + 1)]

    def kernel(err_ref, out_ref):
        def term(at):
            e = [err_ref[k, at, :].astype(f32) for k in range(count)]
            return [e[k] * e[m] for k, m in pairs]

        out_ref[...] = jnp.zeros_like(out_ref)
        for n, s in enumerate(row_steps(rows, 16, block, len(pairs), term)):
            out_ref[n : n + 1, :] = s

    return pl.pallas_call(
        kernel,
        grid=(width // block,),
        in_specs=[pl.BlockSpec((count, rows, block), lambda i: (0, 0, i))],
        out_specs=pl.BlockSpec((padded(len(pairs)), block), lambda i: (0, i)),
        out_shape=jax.ShapeDtypeStruct((padded(len(pairs)), width), f32),
        cost_estimate=pl.CostEstimate(
            flops=2 * len(pairs) * rows * width,
            bytes_accessed=hist_err.size * 2,
            transcendentals=0,
        ),
    )(hist_err)


def new_products(ladder, source_terms, occ_energy, vir_energy, hist_amp, hist_err, stored, copies):
    count, rows, width = hist_err.shape
    block = column_block(width)
    grid = width // block
    pairs = count * (count + 1) // 2
    fresh_at = stored.shape[0]

    def kernel(
        lad_ref, src_ref, occ_ref, vir_ref, amp_ref, err_ref, sto_ref, raw_ref, out_ref, sum_ref
    ):
        step = pl.program_id(0)

        @pl.when(step == 0)
        def _():
            sum_ref[...] = jnp.zeros_like(sum_ref)

        def term(at):
            den = occ_ref[at, 0:1] - vir_ref[...]
            raw = (src_ref[at, :] + lad_ref[at, :]) / den
            raw_ref[at, :] = raw
            new = raw - amp_ref[0, at, :].astype(f32)
            return [err_ref[k, at, :].astype(f32) * new for k in range(count)] + [new * new]

        sum_ref[0:fresh_at, :] += sto_ref[...]
        for n, s in enumerate(row_steps(rows, 16, block, count + 1, term)):
            sum_ref[fresh_at + n : fresh_at + n + 1, :] += s

        @pl.when(step == grid - 1)
        def _():
            column = jnp.sum(sum_ref[...], axis=1, keepdims=True)
            shape = (sum_ref.shape[0], 128)
            lane = lax.broadcasted_iota(jnp.int32, shape, 1)
            item = lax.broadcasted_iota(jnp.int32, shape, 0)
            place = jnp.where(item < fresh_at, item, item - fresh_at + pairs)
            used = (item < pairs) | (item >= fresh_at)
            spread = jnp.where((lane == place) & used, column, 0.0)
            out_ref[...] = jnp.broadcast_to(
                jnp.sum(spread, axis=0, keepdims=True), out_ref.shape
            )

    columns = lambda i: (0, i)
    return pl.pallas_call(
        kernel,
        grid=(grid,),
        in_specs=[
            pl.BlockSpec((ladder.shape[0], block), columns),
            pl.BlockSpec((rows, block), columns),
            pl.BlockSpec((rows, 128), lambda i: (0, 0)),
            pl.BlockSpec((1, block), columns),
            pl.BlockSpec((1, rows, block), lambda i: (0, 0, i)),
            pl.BlockSpec((count, rows, block), lambda i: (0, 0, i)),
            pl.BlockSpec((fresh_at, block), columns),
        ],
        out_specs=[
            pl.BlockSpec((rows, block), columns),
            pl.BlockSpec((copies, 128), lambda i: (0, 0)),
        ],
        out_shape=[
            jax.ShapeDtypeStruct((rows, width), f32),
            jax.ShapeDtypeStruct((copies, 128), f32),
        ],
        scratch_shapes=[pltpu.VMEM((fresh_at + padded(count + 1), block), f32)],
        cost_estimate=pl.CostEstimate(
            flops=20 * rows * width,
            bytes_accessed=hist_err.size * 2 + 14 * rows * width,
            transcendentals=0,
        ),
    )(ladder, source_terms, occ_energy, vir_energy, hist_amp, hist_err, stored)


def extrapolate(gathered, raw, hist_amp):
    count, rows, width = hist_amp.shape
    order = count + 1
    block = column_block(width)

    def solve(totals):
        lane = lax.broadcasted_iota(jnp.int32, totals.shape, 1)
        corr = {}
        for k in range(order):
            for m in range(k + 1):
                hit = lane == k * (k + 1) // 2 + m
                corr[k, m] = jnp.sum(jnp.where(hit, totals, 0.0), axis=1, keepdims=True)
        factor = {}
        for m in range(order):
            diag = corr[m, m]
            for j in range(m):
                diag = diag - factor[m, j] * factor[m, j]
            factor[m, m] = jnp.sqrt(diag)
            for k in range(m + 1, order):
                value = corr[k, m]
                for j in range(m):
                    value = value - factor[k, j] * factor[m, j]
                factor[k, m] = value / factor[m, m]
        forward = []
        for k in range(order):
            running = jnp.ones((1, 1), f32)
            for m in range(k):
                running = running - factor[k, m] * forward[m]
            forward.append(running / factor[k, k])
        backward = [None] * order
        for k in reversed(range(order)):
            running = forward[k]
            for m in range(k + 1, order):
                running = running - factor[m, k] * backward[m]
            backward[k] = running / factor[k, k]
        whole = backward[0]
        for k in range(1, order):
            whole = whole + backward[k]
        return [b / whole for b in backward]

    def kernel(sum_ref, raw_ref, amp_ref, out_ref, weight_ref):
        @pl.when(pl.program_id(0) == 0)
        def _():
            weights = solve(jnp.sum(sum_ref[...], axis=0, keepdims=True))
            for k in range(order):
                weight_ref[k : k + 1, :] = jnp.broadcast_to(weights[k], (1, 128))

        updated = weight_ref[count : count + 1, 0:1] * raw_ref[...]
        for k in range(count):
            updated = updated + weight_ref[k : k + 1, 0:1] * amp_ref[k].astype(f32)
        out_ref[...] = updated

    columns = lambda i: (0, i)
    return pl.pallas_call(
        kernel,
        grid=(width // block,),
        in_specs=[
            pl.BlockSpec(gathered.shape, lambda i: (0, 0)),
            pl.BlockSpec((rows, block), columns),
            pl.BlockSpec((count, rows, block), lambda i: (0, 0, i)),
        ],
        out_specs=pl.BlockSpec((rows, block), columns),
        out_shape=jax.ShapeDtypeStruct((rows, width), f32),
        scratch_shapes=[pltpu.VMEM((padded(order), 128), f32)],
    )(gathered, raw, hist_amp)


def cuts_of(rows):
    first = max(16, rows * 3 // 8 // 16 * 16)
    return [(at, min(first, rows - at)) for at in range(0, rows, first)]


def after(x, *earlier):
    return lax.optimization_barrier((x, *earlier))[0]


def make(mesh):
    row_n, col_n = mesh.shape["row"], mesh.shape["col"]
    total = row_n * col_n

    def send_col(x, m):
        return lax.ppermute(x, "col", [(i, i ^ m) for i in range(col_n)])

    def send_row(x, m):
        return lax.ppermute(x, "row", [(i, i ^ m) for i in range(row_n)])

    def on_device(
        integrals, lambda2, source_terms, hist_amp, hist_err, eps_occ, eps_vir, occ_pair, vir_pair
    ):
        rows, width = source_terms.shape
        depth = lambda2.shape[1]
        near = lambda2.shape[0] // rows
        r, c = lax.axis_index("row"), lax.axis_index("col")
        zi = r // near
        low = lax.rem(zi, 2) == lax.rem(c, 2)

        height = -(-rows // 16) * 16

        def multiply(piece):
            out = jnp.dot(
                piece.reshape(-1, depth), integrals, preferred_element_type=f32
            )
            return out.reshape(near, -1, width)

        def near_begin(part):
            bit = 1
            while True:
                halves = part.reshape(part.shape[0] // 2, 2, *part.shape[1:])
                mine = (r // bit) % 2 == 0
                send = jnp.where(mine, halves[:, 1], halves[:, 0]).astype(wire)
                keep = jnp.where(mine, halves[:, 0], halves[:, 1])
                taken = send_row(send, bit)
                if keep.shape[0] == 1:
                    return keep[0], taken[0], send
                part = keep + taken.astype(f32)
                bit *= 2

        def near_end(keep, taken):
            return keep + taken.astype(f32)

        def pair_begin(first, second):
            send = jnp.where(low, second, first).astype(wire)
            keep = jnp.where(low, first, second)
            return keep, send_row(send, near), send

        def far_begin(part, pair):
            kept = jnp.where(zi // 2 == (c // 2) ^ pair, part, 0.0)
            data = part.astype(wire)
            taken = []
            for d in range(1, col_n // 2):
                links = []
                for z in range(col_n):
                    for y in range(col_n):
                        if (z // 2) ^ (y // 2) ^ pair == d:
                            for x in range(near):
                                source = (z * near + x) * col_n + y
                                target = ((z ^ (2 * d)) * near + x) * col_n + y
                                links.append((source, target))
                taken.append(lax.ppermute(data, ("row", "col"), links))
            return kept, taken, data

        def far_end(kept, taken):
            for one in taken:
                kept = kept + one.astype(f32)
            return kept

        own = jnp.pad(
            lambda2.reshape(near, rows, depth), ((0, 0), (0, height - rows), (0, 0))
        )
        own = lax.optimization_barrier(own)
        cuts = cuts_of(height)
        stages = [(m, at, size) for m in range(2, col_n, 2) for at, size in cuts]
        last = len(stages) - 1
        far, nears, pairs, fars = {}, {}, {}, {}

        def start(n, *earlier):
            if n <= last:
                m, at, size = stages[n]
                far[n] = send_col(after(own[:, at : at + size], *earlier), m)

        start(0)
        start(1)
        sibling = send_col(own, 1)
        one = multiply(own)
        first = near_begin(one)
        two = multiply(after(sibling, first[2]))
        second = near_begin(two)
        stored = stored_products(after(hist_err, second[2]))
        nears[-1] = (first, second)
        token = stored

        def to_pair(n, token):
            (keep1, taken1, _), (keep2, taken2, _) = nears[n]
            taken1, taken2, _ = lax.optimization_barrier((taken1, taken2, token))
            pairs[n] = pair_begin(near_end(keep1, taken1), near_end(keep2, taken2))
            return pairs[n][2]

        def to_far(n, token):
            keep, taken, _ = pairs[n]
            taken = after(taken, token)
            m = stages[n][0] if n >= 0 else 0
            fars[n] = far_begin(near_end(keep, taken), m // 2)
            return fars[n][2]

        for n in range(last + 1):
            here = after(far[n], token)
            start(n + 2, here)
            swap = send_col(here, 1)
            one = multiply(here)
            two = multiply(after(swap, one))
            first, second = near_begin(one), near_begin(two)
            nears[n] = (first, second)
            token = second[2]
            token = to_pair(n - 1, token)
            if n >= 1:
                if n == 1:
                    token = to_far(-1, token)
                token = to_far(n - 1, token)
        token = to_pair(last, token)
        if last == 0:
            token = to_far(-1, token)
        token = to_far(last, token)

        ladder = far_end(*fars[-1][:2])
        for p in range(len(cuts), last + 2, len(cuts)):
            parts = [far_end(*fars[n][:2]) for n in range(p - len(cuts), p)]
            ladder = ladder + jnp.concatenate(parts, axis=0)

        occ_energy = jnp.broadcast_to(pair_energy(occ_pair, eps_occ)[:, None], (rows, 128))
        vir_energy = pair_energy(vir_pair, eps_vir)[None, :]
        raw, shares = new_products(
            ladder, source_terms, occ_energy, vir_energy, hist_amp, hist_err, stored, total
        )
        gathered = lax.all_to_all(shares, ("row", "col"), 0, 0, tiled=True)
        return extrapolate(gathered, raw, hist_amp)

    return on_device


def solution(mesh):
    placed = (
        P("row", "col"),
        P("col", "row"),
        P("row", "col"),
        P(None, "row", "col"),
        P(None, "row", "col"),
        P(),
        P(),
        P(None, "row"),
        P(None, "col"),
    )
    return jax.shard_map(
        make(mesh), mesh=mesh, in_specs=placed, out_specs=P("row", "col"), check_vma=False
    )
```

time: 166 us -> 137 us (0.83)
  waiting for transfers between devices: 62.2 us -> 35.9 us
  blocking collectives: 10.6 us -> 15.6 us
  other arithmetic: 10.9 us -> 7.08 us
  Pallas kernels: 17.4 us -> 14.5 us
    ppermute x5 -> x4, waiting for transfers between devices: 27.4 us -> 3.11 us  [far_begin(): taken.append(lax.ppermute(data, ('row', 'col'), links))]
    ppermute x9 -> x7, waiting for transfers between devices: 15.3 us -> 0.61 us  [send_col(): return lax.ppermute(x, 'col', [(i, i ^ m) for i in range(col_n)])]
    ppermute x15 -> x12, waiting for transfers between devices: 19.5 us -> 32.2 us  [send_row(): return lax.ppermute(x, 'row', [(i, i ^ m) for i in range(row_n)])]
    all_to_all x1, blocking collectives: 10.6 us -> 15.6 us  [on_device(): gathered = lax.all_to_all(shares, ('row', 'col'), 0, 0, tiled=True)]
    another operation x1 -> x0, local copies, waits for them, and re-layouts: 3.12 us -> none  [over_near(): halves = part.reshape(part.shape[0] // 2, 2, *part.shape[1:])]
    unnamed x12 -> x16, local copies, waits for them, and re-layouts: 0.13 us -> 2.84 us
    pallas_call x1, Pallas kernels: 8.14 us -> 5.63 us  [new_products(): pl.pallas_call(kernel, grid=(grid,), in_specs=[pl.BlockSpec((ladder.shape...]
    reshape x2 -> x1, local copies, waits for them, and re-layouts: 5.4 us -> 3.32 us  [on_device(): lambda2.reshape(near, rows, depth)]
  transfers between devices with their start and end apart: 29 -> 23, of which waited for: 13 -> 12; matrix products, arithmetic and copies ran while one was open for 21% -> 19% of each run, Pallas kernels for 3% -> 3%
where the time goes in v2:
time: 137 us; the launch traced here: 136 us
  waiting for transfers between devices  35.9 us (26%)
  starting transfers between devices  33.5 us (24%)
  matrix products  18.5 us (14%)
  blocking collectives  15.6 us (11%)
  Pallas kernels  14.5 us (11%)
  local copies, waits for them, and re-layouts  10.8 us (8%)
  other arithmetic  7.08 us (5%)
    ppermute x12, waiting for transfers between devices, send_row(): return lax.ppermute(x, 'row', [(i, i ^ m) for i in range(row_n)])  32.2 us
    dot_general x8, matrix products, multiply(): jnp.dot(piece.reshape(-1, depth), integrals, preferred_element_type=f32)  18.5 us
    all_to_all x1, blocking collectives, on_device(): gathered = lax.all_to_all(shares, ('row', 'col'), 0, 0, tiled=True)  15.6 us
    ppermute x4, starting transfers between devices, far_begin(): taken.append(lax.ppermute(data, ('row', 'col'), links))  14.8 us
    ppermute x12, starting transfers between devices, send_row(): return lax.ppermute(x, 'row', [(i, i ^ m) for i in range(row_n)])  14 us
    pallas_call x1, Pallas kernels, new_products(): pl.pallas_call(kernel, grid=(grid,), in_specs=[pl.BlockSpec((ladder.shape...  5.63 us
    ppermute x7, starting transfers between devices, send_col(): return lax.ppermute(x, 'col', [(i, i ^ m) for i in range(col_n)])  4.81 us
    pallas_call x1, Pallas kernels, extrapolate(): pl.pallas_call(kernel, grid=(width // block,), in_specs=[pl.BlockSpec(gat...  4.54 us
  transfers between devices with their start and end apart: 23, of which 12 were waited for; matrix products, arithmetic and copies ran while one was open for 19% of the time, Pallas kernels for 3%

profile of v2, /device:TPU:0, one launch (start us, length us, event | category | flops | bytes accessed | tf_op | source)
XLA Modules:
  0.0 136.3 jit_solution(7781780044968289984)
XLA Ops:
  0.0 3.3 %reshape.367 = bf16[2,252,2048]{2,1,0:T(8,128)(2,1)} reshape(bf16[504,2048]{1,0:T(8,128)(2,1)} %param.10) | data formatting | bytes 4128768 | tf_op jit(solution)/shard_map/reshape | solution.py:291
  3.3 1.7 %pad.4 = bf16[2,256,2048]{2,1,0:T(8,128)(2,1)S(1)} pad(bf16[2,252,2048]{2,1,0:T(8,128)(2,1)} %reshape.367, bf16[]{:T(256)} %constant.99.clone.1), padding=0_0x0_4x0_0 | pad | bytes 4161538 | tf_op jit(solution)/shard_map/jit(_pad)/pad | solution.py:290
  6.9 2.5 %collective-permute-start.3 = (bf16[2,96,2048]{2,1,0:T(8,128)(2,1)}, bf16[2,96,2048]{2,1,0:T(8,128)(2,1)}, u32[]{:S(2)}, u32[]{:S(2)}) collective-permute-start(bf16[2,96,2048]{2,1,0:T(8,128)(2,1)} %get-tuple-element.62), channel_id=1, source_target_pairs={{0,2},{1,3},{2,0},{3,1},{4,6},{5,7},{6,4},{7,5},{8,10},{9,11},{10,... | collective-permute-start | bytes 2359304 | tf_op jit(solution)/shard_map/ppermute | solution.py:225
  9.4 4.5 %fusion.16 = f32[1,2,256,1024]{3,2,1,0:T(8,128)S(1)} fusion(bf16[2,256,2048]{2,1,0:T(8,128)(2,1)S(1)} %pad.4, bf16[2048,1024]{1,0:T(8,128)(2,1)} %param.9), kind=kOutput, calls=%fused_computation.20 | convolution fusion | flops 2147483648 | bytes 8388608 | tf_op jit(solution)/shard_map/dot_general | solution.py:243
  16.3 2.0 %collective-permute-start = (f16[1,256,1024]{2,1,0:T(8,128)(2,1)}, f16[1,256,1024]{2,1,0:T(8,128)(2,1)S(1)}, u32[]{:S(2)}, u32[]{:S(2)}) collective-permute-start(f16[1,256,1024]{2,1,0:T(8,128)(2,1)} %fusion.40), channel_id=1, source_target_pairs={{0,4},{4,0},{8,12},{12,8},{16,20},{20,16},{24,28},{28,24},{1,5},{5... | collective-permute-start | bytes 1572872 | tf_op jit(solution)/shard_map/ppermute | solution.py:228
  19.2 5.2 %fusion.19 = f32[1,2,256,1024]{3,2,1,0:T(8,128)S(1)} fusion(bf16[2,256,2048]{2,1,0:T(8,128)(2,1)} %collective-permute-done.1, bf16[2048,1024]{1,0:T(8,128)(2,1)} %param.9), kind=kOutput, calls=%fused_computation.21 | convolution fusion | flops 2147483648 | bytes 8388608 | tf_op jit(solution)/shard_map/dot_general | solution.py:243
  25.4 4.3 %shard_map.91.sto_ref = f32[16,1024]{1,0:T(8,128)} custom-call(bf16[5,252,1024]{2,1,0:T(8,128)(2,1)} %err_ref.2), custom_call_target="tpu_custom_call" | custom-call | flops 7741440 | bytes 2580480 | tf_op jit(solution)/shard_map/pallas_call | solution.py:60
  32.2 3.2 %fusion.22 = f32[1,2,96,1024]{3,2,1,0:T(8,128)S(1)} fusion(bf16[2,96,2048]{2,1,0:T(8,128)(2,1)S(1)} %collective-permute-done.4, bf16[2048,1024]{1,0:T(8,128)(2,1)} %param.9), kind=kOutput, calls=%fused_computation.22 | convolution fusion | flops 805306368 | bytes 5767168 | tf_op jit(solution)/shard_map/dot_general | solution.py:243
  35.4 10.3 %collective-permute-done.2 = f16[1,256,1024]{2,1,0:T(8,128)(2,1)S(1)} collective-permute-done((f16[1,256,1024]{2,1,0:T(8,128)(2,1)}, f16[1,256,1024]{2,1,0:T(8,128)(2,1)S(1)}, u32[]{:S(2)}, u32[]{:S(2)}) %collective-permute-start.2) | collective-permute-done | bytes 524320 | tf_op jit(solution)/shard_map/ppermute | solution.py:228
  46.5 1.5 %copy-done = bf16[2048,1024]{1,0:T(8,128)(2,1)S(1)} copy-done((bf16[2048,1024]{1,0:T(8,128)(2,1)S(1)}, bf16[2048,1024]{1,0:T(8,128)(2,1)}, u32[]{:S(2)}) %copy-start) | copy-done | bytes 4194328
  48.0 2.2 %fusion.25 = f32[1,2,96,1024]{3,2,1,0:T(8,128)S(1)} fusion(bf16[2,96,2048]{2,1,0:T(8,128)(2,1)} %collective-permute-done.3, bf16[2048,1024]{1,0:T(8,128)(2,1)S(1)} %copy-done), kind=kOutput, calls=%fused_computation.23 | convolution fusion | flops 805306368 | bytes 5767168 | tf_op jit(solution)/shard_map/dot_general | solution.py:243
  50.1 1.6 %collective-permute-start.15 = (bf16[2,64,2048]{2,1,0:T(8,128)(2,1)S(1)}, bf16[2,64,2048]{2,1,0:T(8,128)(2,1)S(1)}, u32[]{:S(2)}, u32[]{:S(2)}) collective-permute-start(bf16[2,64,2048]{2,1,0:T(8,128)(2,1)S(1)} %copy-done.3), channel_id=1, source_target_pairs={{0,2},{1,3},{2,0},{3,1},{4,6},{5,7},{6,4},{7,5},{8,10},{9,11},{10,... | collective-permute-start | bytes 1572872 | tf_op jit(solution)/shard_map/ppermute | solution.py:225
  52.4 1.5 %collective-permute-start.7 = (f16[1,96,1024]{2,1,0:T(8,128)(2,1)S(1)}, f16[1,96,1024]{2,1,0:T(8,128)(2,1)S(1)}, u32[]{:S(2)}, u32[]{:S(2)}) collective-permute-start(f16[1,96,1024]{2,1,0:T(8,128)(2,1)S(1)} %fusion.42), channel_id=1, source_target_pairs={{0,4},{4,0},{8,12},{12,8},{16,20},{20,16},{24,28},{28,24},{1,5},{5... | collective-permute-start | bytes 589832 | tf_op jit(solution)/shard_map/ppermute | solution.py:228
  53.9 1.6 %collective-permute-start.5 = (f16[256,1024]{1,0:T(8,128)(2,1)S(1)}, f16[256,1024]{1,0:T(8,128)(2,1)S(1)}, u32[]{:S(2)}, u32[]{:S(2)}) collective-permute-start(f16[256,1024]{1,0:T(8,128)(2,1)S(1)} %get-tuple-element.58), channel_id=1, source_target_pairs={{0,8},{4,12},{8,0},{12,4},{16,24},{20,28},{24,16},{28,20},{1,9},{5... | collective-permute-start | bytes 1572872 | tf_op jit(solution)/shard_map/ppermute | solution.py:228
  57.6 2.1 %collective-permute-done.6 = f16[1,96,1024]{2,1,0:T(8,128)(2,1)S(1)} collective-permute-done((f16[1,96,1024]{2,1,0:T(8,128)(2,1)S(1)}, f16[1,96,1024]{2,1,0:T(8,128)(2,1)S(1)}, u32[]{:S(2)}, u32[]{:S(2)}) %collective-permute-start.6) | collective-permute-done | bytes 196640 | tf_op jit(solution)/shard_map/ppermute | solution.py:228
  59.7 2.6 %collective-permute-done.7 = f16[1,96,1024]{2,1,0:T(8,128)(2,1)S(1)} collective-permute-done((f16[1,96,1024]{2,1,0:T(8,128)(2,1)S(1)}, f16[1,96,1024]{2,1,0:T(8,128)(2,1)S(1)}, u32[]{:S(2)}, u32[]{:S(2)}) %collective-permute-start.7) | collective-permute-done | bytes 196640 | tf_op jit(solution)/shard_map/ppermute | solution.py:228
  62.5 1.6 %collective-permute-start.11 = (f16[96,1024]{1,0:T(8,128)(2,1)S(1)}, f16[96,1024]{1,0:T(8,128)(2,1)S(1)}, u32[]{:S(2)}, u32[]{:S(2)}) collective-permute-start(f16[96,1024]{1,0:T(8,128)(2,1)S(1)} %get-tuple-element.55), channel_id=1, source_target_pairs={{0,8},{4,12},{8,0},{12,4},{16,24},{20,28},{24,16},{28,20},{1,9},{5... | collective-permute-start | bytes 589832 | tf_op jit(solution)/shard_map/ppermute | solution.py:228
  64.1 4.5 %collective-permute-done.5 = f16[256,1024]{1,0:T(8,128)(2,1)S(1)} collective-permute-done((f16[256,1024]{1,0:T(8,128)(2,1)S(1)}, f16[256,1024]{1,0:T(8,128)(2,1)S(1)}, u32[]{:S(2)}, u32[]{:S(2)}) %collective-permute-start.5) | collective-permute-done | bytes 524320 | tf_op jit(solution)/shard_map/ppermute | solution.py:228
  68.9 1.8 %collective-permute-done.11 = f16[96,1024]{1,0:T(8,128)(2,1)S(1)} collective-permute-done((f16[96,1024]{1,0:T(8,128)(2,1)S(1)}, f16[96,1024]{1,0:T(8,128)(2,1)S(1)}, u32[]{:S(2)}, u32[]{:S(2)}) %collective-permute-start.11) | collective-permute-done | bytes 196640 | tf_op jit(solution)/shard_map/ppermute | solution.py:228
  71.6 1.5 %collective-permute-start.14 = (f16[1,96,1024]{2,1,0:T(8,128)(2,1)S(1)}, f16[1,96,1024]{2,1,0:T(8,128)(2,1)S(1)}, u32[]{:S(2)}, u32[]{:S(2)}) collective-permute-start(f16[1,96,1024]{2,1,0:T(8,128)(2,1)S(1)} %fusion.44), channel_id=1, source_target_pairs={{0,4},{4,0},{8,12},{12,8},{16,20},{20,16},{24,28},{28,24},{1,5},{5... | collective-permute-start | bytes 589832 | tf_op jit(solution)/shard_map/ppermute | solution.py:228
  74.4 5.7 %collective-permute-start.12 = (f16[96,1024]{1,0:T(8,128)(2,1)S(1)}, f16[96,1024]{1,0:T(8,128)(2,1)S(1)}, u32[]{:S(2)}, u32[]{:S(2)}) collective-permute-start(f16[96,1024]{1,0:T(8,128)(2,1)S(1)} %fusion.49), channel_id=1, source_target_pairs={{0,16},{4,20},{1,17},{5,21},{8,24},{12,28},{9,25},{13,29},{18,2},{... | collective-permute-start | bytes 589832 | tf_op jit(solution)/shard_map/ppermute | solution.py:282
  82.8 1.6 %collective-permute-start.17 = (f16[96,1024]{1,0:T(8,128)(2,1)S(1)}, f16[96,1024]{1,0:T(8,128)(2,1)S(1)}, u32[]{:S(2)}, u32[]{:S(2)}) collective-permute-start(f16[96,1024]{1,0:T(8,128)(2,1)S(1)} %get-tuple-element.52), channel_id=1, source_target_pairs={{0,8},{4,12},{8,0},{12,4},{16,24},{20,28},{24,16},{28,20},{1,9},{5... | collective-permute-start | bytes 589832 | tf_op jit(solution)/shard_map/ppermute | solution.py:228
  85.0 1.5 %collective-permute-start.20 = (f16[1,64,1024]{2,1,0:T(8,128)(2,1)S(1)}, f16[1,64,1024]{2,1,0:T(8,128)(2,1)S(1)}, u32[]{:S(2)}, u32[]{:S(2)}) collective-permute-start(f16[1,64,1024]{2,1,0:T(8,128)(2,1)S(1)} %fusion.47), channel_id=1, source_target_pairs={{0,4},{4,0},{8,12},{12,8},{16,20},{20,16},{24,28},{28,24},{1,5},{5... | collective-permute-start | bytes 393224 | tf_op jit(solution)/shard_map/ppermute | solution.py:228
  86.5 2.8 %collective-permute-done.17 = f16[96,1024]{1,0:T(8,128)(2,1)S(1)} collective-permute-done((f16[96,1024]{1,0:T(8,128)(2,1)S(1)}, f16[96,1024]{1,0:T(8,128)(2,1)S(1)}, u32[]{:S(2)}, u32[]{:S(2)}) %collective-permute-start.17) | collective-permute-done | bytes 196640 | tf_op jit(solution)/shard_map/ppermute | solution.py:228
  90.7 1.4 %collective-permute-done.20 = f16[1,64,1024]{2,1,0:T(8,128)(2,1)S(1)} collective-permute-done((f16[1,64,1024]{2,1,0:T(8,128)(2,1)S(1)}, f16[1,64,1024]{2,1,0:T(8,128)(2,1)S(1)}, u32[]{:S(2)}, u32[]{:S(2)}) %collective-permute-start.20) | collective-permute-done | bytes 131104 | tf_op jit(solution)/shard_map/ppermute | solution.py:228
  92.9 6.5 %collective-permute-start.18 = (f16[96,1024]{1,0:T(8,128)(2,1)S(1)}, f16[96,1024]{1,0:T(8,128)(2,1)S(1)}, u32[]{:S(2)}, u32[]{:S(2)}) collective-permute-start(f16[96,1024]{1,0:T(8,128)(2,1)S(1)} %fusion.50), channel_id=1, source_target_pairs={{0,16},{4,20},{1,17},{5,21},{8,24},{12,28},{9,25},{13,29},{18,2},{... | collective-permute-start | bytes 589832 | tf_op jit(solution)/shard_map/ppermute | solution.py:282
  99.4 4.2 %collective-permute-done.21 = f16[64,1024]{1,0:T(8,128)(2,1)S(1)} collective-permute-done((f16[64,1024]{1,0:T(8,128)(2,1)S(1)}, f16[64,1024]{1,0:T(8,128)(2,1)S(1)}, u32[]{:S(2)}, u32[]{:S(2)}) %collective-permute-start.21) | collective-permute-done | bytes 131104 | tf_op jit(solution)/shard_map/ppermute | solution.py:228
  105.2 3.1 %collective-permute-done.22 = f16[64,1024]{1,0:T(8,128)(2,1)S(1)} collective-permute-done((f16[64,1024]{1,0:T(8,128)(2,1)S(1)}, f16[64,1024]{1,0:T(8,128)(2,1)S(1)}, u32[]{:S(2)}, u32[]{:S(2)}) %collective-permute-start.22) | collective-permute-done | bytes 131104 | tf_op jit(solution)/shard_map/ppermute | solution.py:282
  108.4 1.4 %maximum_add_fusion.lad_ref = f32[256,1024]{1,0:T(8,128)} fusion(f32[64,1024]{1,0:T(8,128)S(1)} %convert_add_fusion.5, f32[96,1024]{1,0:T(8,128)S(1)} %convert_add_fusion.1, f32[96,1024]{1,0:T(8,128)S(1)} %convert_add_fusion.3, f16[256,1024]{1,0:T(8,128)(2,1)S(1)} %collective-permute-done.10, pred[]{:T(512)S(6)} %eq.90, ...), kind=kLoop, calls=%fused_computation.28 | loop fusion | flops 2359296 | bytes 5242882 | tf_op jit(solution)/shard_map/add | solution.py:350
  110.5 5.6 %shard_map.92 = (f32[252,1024]{1,0:T(8,128)}, f32[32,128]{1,0:T(8,128)}) custom-call(f32[256,1024]{1,0:T(8,128)} %maximum_add_fusion.lad_ref, f32[252,1024]{1,0:T(8,128)} %src_ref.1, f32[252,128]{1,0:T(8,128)} %broadcast_in_dim.65.occ_ref, f32[1,1024]{1,0:T(1,128)} %bitcast.123, bf16[5,252,1024]{2,1,0:T(8,128)(2,1)} %amp_ref.3, ...), custom_call_target="tpu_custom_call" | custom-call | flops 5160960 | bytes 6193152 | tf_op jit(solution)/shard_map/pallas_call | solution.py:115
  116.1 15.6 %all_to_all.11 = f32[32,1,128]{2,1,0:T(1,128)} all-to-all(f32[32,1,128]{2,1,0:T(1,128)} %bitcast.124), channel_id=1, replica_groups=mesh['row'=8,'col'=4] {'row','col'}, dimensions={0} | all-to-all | bytes 32768 | tf_op jit(solution)/shard_map/all_to_all | solution.py:357
  131.8 4.5 %shard_map.93 = f32[252,1024]{1,0:T(8,128)} custom-call(f32[32,128]{1,0:T(8,128)} %bitcast.122, f32[252,1024]{1,0:T(8,128)} %get-tuple-element.44.raw_ref, bf16[5,252,1024]{2,1,0:T(8,128)(2,1)} %amp_ref.3), custom_call_target="tpu_custom_call" | custom-call | tf_op jit(solution)/shard_map/pallas_call | solution.py:197
  (73 shorter events, 22.3 us)
Async XLA Ops:
  5.1 14.1 %collective-permute-start.1 = (bf16[2,256,2048]{2,1,0:T(8,128)(2,1)S(1)}, bf16[2,256,2048]{2,1,0:T(8,128)(2,1)}, u32[]{:S(2)}, u32[]{:S(2)}) collective-permute-start(bf16[2,256,2048]{2,1,0:T(8,128)(2,1)S(1)} %pad.4), channel_id=1, source_target_pairs={{0,1},{1,0},{2,3},{3,2},{4,5},{5,4},{6,7},{7,6},{8,9},{9,8},{10,11... | collective-permute-start | bytes 6291464 | tf_op jit(solution)/shard_map/ppermute | solution.py:225
  6.9 22.8 %collective-permute-start.3 = (bf16[2,96,2048]{2,1,0:T(8,128)(2,1)}, bf16[2,96,2048]{2,1,0:T(8,128)(2,1)}, u32[]{:S(2)}, u32[]{:S(2)}) collective-permute-start(bf16[2,96,2048]{2,1,0:T(8,128)(2,1)} %get-tuple-element.62), channel_id=1, source_target_pairs={{0,2},{1,3},{2,0},{3,1},{4,6},{5,7},{6,4},{7,5},{8,10},{9,11},{10,... | collective-permute-start | bytes 2359304 | tf_op jit(solution)/shard_map/ppermute | solution.py:225
  9.4 37.0 %collective-permute-start.8 = (bf16[2,96,2048]{2,1,0:T(8,128)(2,1)}, bf16[2,96,2048]{2,1,0:T(8,128)(2,1)S(1)}, u32[]{:S(2)}, u32[]{:S(2)}) collective-permute-start(bf16[2,96,2048]{2,1,0:T(8,128)(2,1)} %get-tuple-element.61), channel_id=1, source_target_pairs={{0,2},{1,3},{2,0},{3,1},{4,6},{5,7},{6,4},{7,5},{8,10},{9,11},{10,... | collective-permute-start | bytes 2359304 | tf_op jit(solution)/shard_map/ppermute | solution.py:225
  14.0 1.3 copy-start.1
  16.3 19.1 %collective-permute-start = (f16[1,256,1024]{2,1,0:T(8,128)(2,1)}, f16[1,256,1024]{2,1,0:T(8,128)(2,1)S(1)}, u32[]{:S(2)}, u32[]{:S(2)}) collective-permute-start(f16[1,256,1024]{2,1,0:T(8,128)(2,1)} %fusion.40), channel_id=1, source_target_pairs={{0,4},{4,0},{8,12},{12,8},{16,20},{20,16},{24,28},{28,24},{1,5},{5... | collective-permute-start | bytes 1572872 | tf_op jit(solution)/shard_map/ppermute | solution.py:228
  24.3 5.4 %copy-start.6 = (s32[2,252]{1,0:T(2,128)S(1)}, s32[2,252]{1,0:T(2,128)}, u32[]{:S(2)}) copy-start(s32[2,252]{1,0:T(2,128)} %param.16) | copy-start | bytes 6052
  24.3 5.4 %copy-start.7 = (f32[64]{0:T(128)S(1)}, f32[64]{0:T(128)}, u32[]{:S(2)}) copy-start(f32[64]{0:T(128)} %param.14) | copy-start | bytes 772
  24.3 5.5 %copy-start.4 = (s32[2,1024]{1,0:T(2,128)S(1)}, s32[2,1024]{1,0:T(2,128)}, u32[]{:S(2)}) copy-start(s32[2,1024]{1,0:T(2,128)} %param.17) | copy-start | bytes 24580
  24.3 5.5 %copy-start.5 = (f32[800]{0:T(1024)S(1)}, f32[800]{0:T(1024)}, u32[]{:S(2)}) copy-start(f32[800]{0:T(1024)} %param.15) | copy-start | bytes 9604
  29.7 2.5 %collective-permute-start.4 = (bf16[2,96,2048]{2,1,0:T(8,128)(2,1)}, bf16[2,96,2048]{2,1,0:T(8,128)(2,1)S(1)}, u32[]{:S(2)}, u32[]{:S(2)}) collective-permute-start(bf16[2,96,2048]{2,1,0:T(8,128)(2,1)} %collective-permute-done.3), channel_id=1, source_target_pairs={{0,1},{1,0},{2,3},{3,2},{4,5},{5,4},{6,7},{7,6},{8,9},{9,8},{10,11... | collective-permute-start | bytes 2359304 | tf_op jit(solution)/shard_map/ppermute | solution.py:225
  31.2 14.5 %copy-start.2 = (f32[1,2,256,1024]{3,2,1,0:T(8,128)S(1)}, f32[1,2,256,1024]{3,2,1,0:T(8,128)}, u32[]{:S(2)}) copy-start(f32[1,2,256,1024]{3,2,1,0:T(8,128)} %copy-done.1) | copy-start | bytes 6291460
  31.2 14.5 %collective-permute-start.2 = (f16[1,256,1024]{2,1,0:T(8,128)(2,1)}, f16[1,256,1024]{2,1,0:T(8,128)(2,1)S(1)}, u32[]{:S(2)}, u32[]{:S(2)}) collective-permute-start(f16[1,256,1024]{2,1,0:T(8,128)(2,1)} %fusion.41), channel_id=1, source_target_pairs={{0,4},{4,0},{8,12},{12,8},{16,20},{20,16},{24,28},{28,24},{1,5},{5... | collective-permute-start | bytes 1572872 | tf_op jit(solution)/shard_map/ppermute | solution.py:228
  45.8 2.2 %copy-start = (bf16[2048,1024]{1,0:T(8,128)(2,1)S(1)}, bf16[2048,1024]{1,0:T(8,128)(2,1)}, u32[]{:S(2)}) copy-start(bf16[2048,1024]{1,0:T(8,128)(2,1)} %param.9) | copy-start | bytes 12582916
  46.4 3.7 %copy-start.3 = (bf16[2,64,2048]{2,1,0:T(8,128)(2,1)S(1)}, bf16[2,64,2048]{2,1,0:T(8,128)(2,1)}, u32[]{:S(2)}) copy-start(bf16[2,64,2048]{2,1,0:T(8,128)(2,1)} %slice.122) | copy-start | bytes 1572868
  46.4 10.1 %collective-permute-start.9 = (bf16[2,96,2048]{2,1,0:T(8,128)(2,1)S(1)}, bf16[2,96,2048]{2,1,0:T(8,128)(2,1)S(1)}, u32[]{:S(2)}, u32[]{:S(2)}) collective-permute-start(bf16[2,96,2048]{2,1,0:T(8,128)(2,1)S(1)} %collective-permute-done.8), channel_id=1, source_target_pairs={{0,1},{1,0},{2,3},{3,2},{4,5},{5,4},{6,7},{7,6},{8,9},{9,8},{10,11... | collective-permute-start | bytes 2359304 | tf_op jit(solution)/shard_map/ppermute | solution.py:225
  50.1 20.7 %collective-permute-start.15 = (bf16[2,64,2048]{2,1,0:T(8,128)(2,1)S(1)}, bf16[2,64,2048]{2,1,0:T(8,128)(2,1)S(1)}, u32[]{:S(2)}, u32[]{:S(2)}) collective-permute-start(bf16[2,64,2048]{2,1,0:T(8,128)(2,1)S(1)} %copy-done.3), channel_id=1, source_target_pairs={{0,2},{1,3},{2,0},{3,1},{4,6},{5,7},{6,4},{7,5},{8,10},{9,11},{10,... | collective-permute-start | bytes 1572872 | tf_op jit(solution)/shard_map/ppermute | solution.py:225
  51.8 7.9 %collective-permute-start.6 = (f16[1,96,1024]{2,1,0:T(8,128)(2,1)S(1)}, f16[1,96,1024]{2,1,0:T(8,128)(2,1)S(1)}, u32[]{:S(2)}, u32[]{:S(2)}) collective-permute-start(f16[1,96,1024]{2,1,0:T(8,128)(2,1)S(1)} %fusion.43), channel_id=1, source_target_pairs={{0,4},{4,0},{8,12},{12,8},{16,20},{20,16},{24,28},{28,24},{1,5},{5... | collective-permute-start | bytes 589832 | tf_op jit(solution)/shard_map/ppermute | solution.py:228
  52.4 9.9 %collective-permute-start.7 = (f16[1,96,1024]{2,1,0:T(8,128)(2,1)S(1)}, f16[1,96,1024]{2,1,0:T(8,128)(2,1)S(1)}, u32[]{:S(2)}, u32[]{:S(2)}) collective-permute-start(f16[1,96,1024]{2,1,0:T(8,128)(2,1)S(1)} %fusion.42), channel_id=1, source_target_pairs={{0,4},{4,0},{8,12},{12,8},{16,20},{20,16},{24,28},{28,24},{1,5},{5... | collective-permute-start | bytes 589832 | tf_op jit(solution)/shard_map/ppermute | solution.py:228
  53.9 14.8 %collective-permute-start.5 = (f16[256,1024]{1,0:T(8,128)(2,1)S(1)}, f16[256,1024]{1,0:T(8,128)(2,1)S(1)}, u32[]{:S(2)}, u32[]{:S(2)}) collective-permute-start(f16[256,1024]{1,0:T(8,128)(2,1)S(1)} %get-tuple-element.58), channel_id=1, source_target_pairs={{0,8},{4,12},{8,0},{12,4},{16,24},{20,28},{24,16},{28,20},{1,9},{5... | collective-permute-start | bytes 1572872 | tf_op jit(solution)/shard_map/ppermute | solution.py:228
  62.5 8.3 %collective-permute-start.11 = (f16[96,1024]{1,0:T(8,128)(2,1)S(1)}, f16[96,1024]{1,0:T(8,128)(2,1)S(1)}, u32[]{:S(2)}, u32[]{:S(2)}) collective-permute-start(f16[96,1024]{1,0:T(8,128)(2,1)S(1)} %get-tuple-element.55), channel_id=1, source_target_pairs={{0,8},{4,12},{8,0},{12,4},{16,24},{20,28},{24,16},{28,20},{1,9},{5... | collective-permute-start | bytes 589832 | tf_op jit(solution)/shard_map/ppermute | solution.py:228
  70.9 9.9 %collective-permute-start.16 = (bf16[2,64,2048]{2,1,0:T(8,128)(2,1)S(1)}, bf16[2,64,2048]{2,1,0:T(8,128)(2,1)S(1)}, u32[]{:S(2)}, u32[]{:S(2)}) collective-permute-start(bf16[2,64,2048]{2,1,0:T(8,128)(2,1)S(1)} %collective-permute-done.15), channel_id=1, source_target_pairs={{0,1},{1,0},{2,3},{3,2},{4,5},{5,4},{6,7},{7,6},{8,9},{9,8},{10,11... | collective-permute-start | bytes 1572872 | tf_op jit(solution)/shard_map/ppermute | solution.py:225
  71.0 10.6 %collective-permute-start.13 = (f16[1,96,1024]{2,1,0:T(8,128)(2,1)S(1)}, f16[1,96,1024]{2,1,0:T(8,128)(2,1)S(1)}, u32[]{:S(2)}, u32[]{:S(2)}) collective-permute-start(f16[1,96,1024]{2,1,0:T(8,128)(2,1)S(1)} %fusion.45), channel_id=1, source_target_pairs={{0,4},{4,0},{8,12},{12,8},{16,20},{20,16},{24,28},{28,24},{1,5},{5... | collective-permute-start | bytes 589832 | tf_op jit(solution)/shard_map/ppermute | solution.py:228
  71.6 11.0 %collective-permute-start.14 = (f16[1,96,1024]{2,1,0:T(8,128)(2,1)S(1)}, f16[1,96,1024]{2,1,0:T(8,128)(2,1)S(1)}, u32[]{:S(2)}, u32[]{:S(2)}) collective-permute-start(f16[1,96,1024]{2,1,0:T(8,128)(2,1)S(1)} %fusion.44), channel_id=1, source_target_pairs={{0,4},{4,0},{8,12},{12,8},{16,20},{20,16},{24,28},{28,24},{1,5},{5... | collective-permute-start | bytes 589832 | tf_op jit(solution)/shard_map/ppermute | solution.py:228
  73.1 35.3 %collective-permute-start.10 = (f16[256,1024]{1,0:T(8,128)(2,1)S(1)}, f16[256,1024]{1,0:T(8,128)(2,1)S(1)}, u32[]{:S(2)}, u32[]{:S(2)}) collective-permute-start(f16[256,1024]{1,0:T(8,128)(2,1)S(1)} %fusion.46), channel_id=1, source_target_pairs={{2,18},{6,22},{3,19},{7,23},{10,26},{14,30},{11,27},{15,31},{16,0}... | collective-permute-start | bytes 1572872 | tf_op jit(solution)/shard_map/ppermute | solution.py:282
  74.4 18.4 %collective-permute-start.12 = (f16[96,1024]{1,0:T(8,128)(2,1)S(1)}, f16[96,1024]{1,0:T(8,128)(2,1)S(1)}, u32[]{:S(2)}, u32[]{:S(2)}) collective-permute-start(f16[96,1024]{1,0:T(8,128)(2,1)S(1)} %fusion.49), channel_id=1, source_target_pairs={{0,16},{4,20},{1,17},{5,21},{8,24},{12,28},{9,25},{13,29},{18,2},{... | collective-permute-start | bytes 589832 | tf_op jit(solution)/shard_map/ppermute | solution.py:282
  82.8 6.6 %collective-permute-start.17 = (f16[96,1024]{1,0:T(8,128)(2,1)S(1)}, f16[96,1024]{1,0:T(8,128)(2,1)S(1)}, u32[]{:S(2)}, u32[]{:S(2)}) collective-permute-start(f16[96,1024]{1,0:T(8,128)(2,1)S(1)} %get-tuple-element.52), channel_id=1, source_target_pairs={{0,8},{4,12},{8,0},{12,4},{16,24},{20,28},{24,16},{28,20},{1,9},{5... | collective-permute-start | bytes 589832 | tf_op jit(solution)/shard_map/ppermute | solution.py:228
  84.4 6.3 %collective-permute-start.19 = (f16[1,64,1024]{2,1,0:T(8,128)(2,1)S(1)}, f16[1,64,1024]{2,1,0:T(8,128)(2,1)S(1)}, u32[]{:S(2)}, u32[]{:S(2)}) collective-permute-start(f16[1,64,1024]{2,1,0:T(8,128)(2,1)S(1)} %fusion.48), channel_id=1, source_target_pairs={{0,4},{4,0},{8,12},{12,8},{16,20},{20,16},{24,28},{28,24},{1,5},{5... | collective-permute-start | bytes 393224 | tf_op jit(solution)/shard_map/ppermute | solution.py:228
  85.0 7.1 %collective-permute-start.20 = (f16[1,64,1024]{2,1,0:T(8,128)(2,1)S(1)}, f16[1,64,1024]{2,1,0:T(8,128)(2,1)S(1)}, u32[]{:S(2)}, u32[]{:S(2)}) collective-permute-start(f16[1,64,1024]{2,1,0:T(8,128)(2,1)S(1)} %fusion.47), channel_id=1, source_target_pairs={{0,4},{4,0},{8,12},{12,8},{16,20},{20,16},{24,28},{28,24},{1,5},{5... | collective-permute-start | bytes 393224 | tf_op jit(solution)/shard_map/ppermute | solution.py:228
  92.3 11.4 %collective-permute-start.21 = (f16[64,1024]{1,0:T(8,128)(2,1)S(1)}, f16[64,1024]{1,0:T(8,128)(2,1)S(1)}, u32[]{:S(2)}, u32[]{:S(2)}) collective-permute-start(f16[64,1024]{1,0:T(8,128)(2,1)S(1)} %get-tuple-element.49), channel_id=1, source_target_pairs={{0,8},{4,12},{8,0},{12,4},{16,24},{20,28},{24,16},{28,20},{1,9},{5... | collective-permute-start | bytes 393224 | tf_op jit(solution)/shard_map/ppermute | solution.py:228
  92.9 12.1 %collective-permute-start.18 = (f16[96,1024]{1,0:T(8,128)(2,1)S(1)}, f16[96,1024]{1,0:T(8,128)(2,1)S(1)}, u32[]{:S(2)}, u32[]{:S(2)}) collective-permute-start(f16[96,1024]{1,0:T(8,128)(2,1)S(1)} %fusion.50), channel_id=1, source_target_pairs={{0,16},{4,20},{1,17},{5,21},{8,24},{12,28},{9,25},{13,29},{18,2},{... | collective-permute-start | bytes 589832 | tf_op jit(solution)/shard_map/ppermute | solution.py:282
  103.7 4.5 %collective-permute-start.22 = (f16[64,1024]{1,0:T(8,128)(2,1)S(1)}, f16[64,1024]{1,0:T(8,128)(2,1)S(1)}, u32[]{:S(2)}, u32[]{:S(2)}) collective-permute-start(f16[64,1024]{1,0:T(8,128)(2,1)S(1)} %fusion.51), channel_id=1, source_target_pairs={{0,16},{4,20},{1,17},{5,21},{8,24},{12,28},{9,25},{13,29},{18,2},{... | collective-permute-start | bytes 393224 | tf_op jit(solution)/shard_map/ppermute | solution.py:282

commit v3 on v2

--- a/solution.py
+++ b/solution.py
@@ -209,8 +209,15 @@
 
 
 def cuts_of(rows):
-    first = max(16, rows * 3 // 8 // 16 * 16)
-    return [(at, min(first, rows - at)) for at in range(0, rows, first)]
+    cuts, at = [], 0
+    for part in (rows * 7 // 16, rows * 3 // 8):
+        size = min(max(16, -(-part // 16) * 16), rows - at)
+        if size:
+            cuts.append((at, size))
+        at += size
+    if at < rows:
+        cuts.append((at, rows - at))
+    return cuts
 
 
 def after(x, *earlier):
@@ -235,50 +242,55 @@
         near = lambda2.shape[0] // rows
         r, c = lax.axis_index("row"), lax.axis_index("col")
         zi = r // near
-        low = lax.rem(zi, 2) == lax.rem(c, 2)
-
+        holder = lax.rem(zi, 2) == lax.rem(c, 2)
         height = -(-rows // 16) * 16
 
-        def multiply(piece):
+        def links_of(pair_of):
+            links = []
+            for z in range(col_n):
+                for y in range(col_n):
+                    z2 = pair_of(z, y)
+                    if z2 is not None:
+                        for x in range(near):
+                            links.append(
+                                ((z * near + x) * col_n + y, (z2 * near + x) * col_n + y)
+                            )
+            return links
+
+        def multiply(piece, right):
             out = jnp.dot(
-                piece.reshape(-1, depth), integrals, preferred_element_type=f32
+                piece.reshape(-1, depth), right, preferred_element_type=f32
             )
             return out.reshape(near, -1, width)
 
         def near_begin(part):
             bit = 1
             while True:
-                halves = part.reshape(part.shape[0] // 2, 2, *part.shape[1:])
+                count = part.shape[0]
+                halves = part.reshape(count, part.shape[1] // 2, 2, *part.shape[2:])
                 mine = (r // bit) % 2 == 0
-                send = jnp.where(mine, halves[:, 1], halves[:, 0]).astype(wire)
-                keep = jnp.where(mine, halves[:, 0], halves[:, 1])
+                send = jnp.where(mine, halves[:, :, 1], halves[:, :, 0]).astype(wire)
+                keep = jnp.where(mine, halves[:, :, 0], halves[:, :, 1])
                 taken = send_row(send, bit)
-                if keep.shape[0] == 1:
-                    return keep[0], taken[0], send
+                if keep.shape[1] == 1:
+                    return keep[:, 0], taken[:, 0], send
                 part = keep + taken.astype(f32)
                 bit *= 2
 
-        def near_end(keep, taken):
-            return keep + taken.astype(f32)
-
-        def pair_begin(first, second):
-            send = jnp.where(low, second, first).astype(wire)
-            keep = jnp.where(low, first, second)
-            return keep, send_row(send, near), send
+        even_links = links_of(lambda z, y: z ^ 1 if (z ^ y) & 1 else None)
+
+        def pair_begin(part):
+            send = part.astype(wire)
+            return part, lax.ppermute(send, ("row", "col"), even_links), send
 
         def far_begin(part, pair):
-            kept = jnp.where(zi // 2 == (c // 2) ^ pair, part, 0.0)
+            kept = jnp.where(zi == c ^ (2 * pair), part, 0.0)
             data = part.astype(wire)
             taken = []
             for d in range(1, col_n // 2):
-                links = []
-                for z in range(col_n):
-                    for y in range(col_n):
-                        if (z // 2) ^ (y // 2) ^ pair == d:
-                            for x in range(near):
-                                source = (z * near + x) * col_n + y
-                                target = ((z ^ (2 * d)) * near + x) * col_n + y
-                                links.append((source, target))
+                links = links_of(
+                    lambda z, y: z ^ (2 * d) if z ^ y ^ (2 * pair) == 2 * d else None
+                )
                 taken.append(lax.ppermute(data, ("row", "col"), links))
             return kept, taken, data
 
@@ -287,70 +299,86 @@
                 kept = kept + one.astype(f32)
             return kept
 
-        own = jnp.pad(
-            lambda2.reshape(near, rows, depth), ((0, 0), (0, height - rows), (0, 0))
-        )
-        own = lax.optimization_barrier(own)
+        def cut(at, size):
+            parts = []
+            for x in range(near):
+                part = lambda2[x * rows + at : x * rows + min(at + size, rows)]
+                parts.append(jnp.pad(part, ((0, size - part.shape[0]), (0, 0))))
+            return jnp.stack(parts)
+
         cuts = cuts_of(height)
         stages = [(m, at, size) for m in range(2, col_n, 2) for at, size in cuts]
-        last = len(stages) - 1
-        far, nears, pairs, fars = {}, {}, {}, {}
-
-        def start(n, *earlier):
-            if n <= last:
+        far = {}
+
+        def send_far(n, *earlier):
+            if n < len(stages):
                 m, at, size = stages[n]
-                far[n] = send_col(after(own[:, at : at + size], *earlier), m)
-
-        start(0)
-        start(1)
-        sibling = send_col(own, 1)
-        one = multiply(own)
-        first = near_begin(one)
-        two = multiply(after(sibling, first[2]))
-        second = near_begin(two)
-        stored = stored_products(after(hist_err, second[2]))
-        nears[-1] = (first, second)
-        token = stored
-
-        def to_pair(n, token):
-            (keep1, taken1, _), (keep2, taken2, _) = nears[n]
-            taken1, taken2, _ = lax.optimization_barrier((taken1, taken2, token))
-            pairs[n] = pair_begin(near_end(keep1, taken1), near_end(keep2, taken2))
-            return pairs[n][2]
-
-        def to_far(n, token):
-            keep, taken, _ = pairs[n]
-            taken = after(taken, token)
-            m = stages[n][0] if n >= 0 else 0
-            fars[n] = far_begin(near_end(keep, taken), m // 2)
-            return fars[n][2]
-
-        for n in range(last + 1):
-            here = after(far[n], token)
-            start(n + 2, here)
-            swap = send_col(here, 1)
-            one = multiply(here)
-            two = multiply(after(swap, one))
-            first, second = near_begin(one), near_begin(two)
-            nears[n] = (first, second)
-            token = second[2]
-            token = to_pair(n - 1, token)
-            if n >= 1:
-                if n == 1:
-                    token = to_far(-1, token)
-                token = to_far(n - 1, token)
-        token = to_pair(last, token)
-        if last == 0:
-            token = to_far(-1, token)
-        token = to_far(last, token)
-
-        ladder = far_end(*fars[-1][:2])
-        for p in range(len(cuts), last + 2, len(cuts)):
-            parts = [far_end(*fars[n][:2]) for n in range(p - len(cuts), p)]
-            ladder = ladder + jnp.concatenate(parts, axis=0)
-
+                far[n] = send_col(lax.optimization_barrier((cut(at, size), *earlier))[0], m)
+                return far[n]
+
+        piece = lax.optimization_barrier(cut(*cuts[0]))
+        far[0] = send_col(piece, stages[0][0])
+        across = send_col(after(integrals, piece), 1)
+        own = after(cut(0, height), piece)
+
+        nears, pairs, fars = {}, {}, {}
+        nears[0] = near_begin(multiply(own, integrals)[None])
+        send_far(1, nears[0][2])
+        stored = stored_products(after(hist_err, nears[0][2]))
         occ_energy = jnp.broadcast_to(pair_energy(occ_pair, eps_occ)[:, None], (rows, 128))
         vir_energy = pair_energy(vir_pair, eps_vir)[None, :]
+        stored, occ_energy, vir_energy = lax.optimization_barrier((stored, occ_energy, vir_energy))
+        across = after(across, stored)
+        nears[1] = near_begin(multiply(own, across)[None])
+        send_far(2, nears[1][2])
+        last = len(stages) + 1
+
+        def to_near(n, token):
+            here = after(far[n - 2], token)
+            send_far(n + 1, here)
+            nears[n] = near_begin(
+                jnp.stack([multiply(here, integrals), multiply(here, across)])
+            )
+            return nears[n][2]
+
+        def to_pair(n, token):
+            if 0 <= n <= last:
+                keep, taken, _ = nears[n]
+                pairs[n] = pair_begin(keep + after(taken, token).astype(f32))
+                token = pairs[n][2]
+            return token
+
+        def to_far(n, token):
+            if 0 <= n <= last:
+                keep, taken, _ = pairs[n]
+                kept = jnp.where(holder, keep, 0.0) + after(taken, token).astype(f32)
+                fars[n] = far_begin(kept, stages[n - 2][0] // 2 if n >= 2 else 0)
+                token = fars[n][2]
+            return token
+
+        token = nears[1][2]
+        for n in range(2, last + 3):
+            token = to_far(n - 3, token)
+            token = to_pair(n - 2, token)
+            if n <= last:
+                token = to_near(n, token)
+        token = to_far(last, token)
+
+        first = far_end(*fars[0][:2])[0]
+        second = far_end(*fars[1][:2])[0]
+        done = []
+        for q, (at, size) in enumerate(cuts):
+            mine, other = first[at : at + size], second[at : at + size]
+            for p in range(q + 2, last + 1, len(cuts)):
+                total_rows = far_end(*fars[p][:2])
+                mine, other = mine + total_rows[0], other + total_rows[1]
+            done.append((mine, other))
+        early = [other for _, other in done[:-1]]
+        swapped = send_col(jnp.concatenate(early, axis=0), 1) if early else None
+        swapped_last = send_col(done[-1][1], 1)
+        taken = swapped_last if swapped is None else jnp.concatenate([swapped, swapped_last])
+        ladder = jnp.concatenate([mine for mine, _ in done], axis=0) + taken
+
         raw, shares = new_products(
             ladder, source_terms, occ_energy, vir_energy, hist_amp, hist_err, stored, total
         )

time: 137 us -> 122 us (0.89)
  waiting for transfers between devices: 35.9 us -> 27.7 us
  local copies, waits for them, and re-layouts: 10.8 us -> 5.9 us
  blocking collectives: 15.6 us -> 11 us
  starting transfers between devices: 33.5 us -> 29.7 us
  other arithmetic: 7.08 us -> 10.7 us
  matrix products: 18.5 us -> 21.4 us
    ppermute x12 -> x5, waiting for transfers between devices: 32.2 us -> 0.01 us  [send_row(): return lax.ppermute(x, 'row', [(i, i ^ m) for i in range(row_n)])]
    ppermute x0 -> x5, waiting for transfers between devices: none -> 22.2 us  [pair_begin(): return (part, lax.ppermute(send, ('row', 'col'), even_links), send)]
    ppermute x12 -> x5, starting transfers between devices: 14 us -> 5.32 us  [send_row(): return lax.ppermute(x, 'row', [(i, i ^ m) for i in range(row_n)])]
    ppermute x0 -> x5, starting transfers between devices: none -> 6.9 us  [pair_begin(): return (part, lax.ppermute(send, ('row', 'col'), even_links), send)]
    all_to_all x1, blocking collectives: 15.6 us -> 11 us  [on_device(): gathered = lax.all_to_all(shares, ('row', 'col'), 0, 0, tiled=True)]
    reshape x1 -> x0, local copies, waits for them, and re-layouts: 3.32 us -> none  [on_device(): lambda2.reshape(near, rows, depth)]
    dot_general x8, matrix products: 18.5 us -> 21.4 us  [multiply(): out = jnp.dot(piece.reshape(-1, depth), right, preferred_element_type=f32)]
    ppermute x4 -> x5, starting transfers between devices: 14.8 us -> 12.3 us  [far_begin(): taken.append(lax.ppermute(data, ('row', 'col'), links))]
  transfers between devices with their start and end apart: 23 -> 21, of which waited for: 12 -> 9; matrix products, arithmetic and copies ran while one was open for 19% -> 26% of each run, Pallas kernels for 3% -> 4%
where the time goes in v3:
time: 122 us; the launch traced here: 121 us
  starting transfers between devices  29.7 us (24%)
  waiting for transfers between devices  27.7 us (23%)
  matrix products  21.4 us (18%)
  Pallas kernels  14.4 us (12%)
  blocking collectives  11 us (9%)
  other arithmetic  10.7 us (9%)
  local copies, waits for them, and re-layouts  5.9 us (5%)
    ppermute x5, waiting for transfers between devices, pair_begin(): return (part, lax.ppermute(send, ('row', 'col'), even_links), send)  22.2 us
    dot_general x8, matrix products, multiply(): out = jnp.dot(piece.reshape(-1, depth), right, preferred_element_type=f32)  21.4 us
    ppermute x5, starting transfers between devices, far_begin(): taken.append(lax.ppermute(data, ('row', 'col'), links))  12.3 us
    all_to_all x1, blocking collectives, on_device(): gathered = lax.all_to_all(shares, ('row', 'col'), 0, 0, tiled=True)  11 us
    ppermute x5, starting transfers between devices, pair_begin(): return (part, lax.ppermute(send, ('row', 'col'), even_links), send)  6.9 us
    pallas_call x1, Pallas kernels, new_products(): pl.pallas_call(kernel, grid=(grid,), in_specs=[pl.BlockSpec((ladder.shape...  5.59 us
    ppermute x5, starting transfers between devices, send_row(): return lax.ppermute(x, 'row', [(i, i ^ m) for i in range(row_n)])  5.32 us
    ppermute x6, starting transfers between devices, send_col(): return lax.ppermute(x, 'col', [(i, i ^ m) for i in range(col_n)])  5.2 us
  transfers between devices with their start and end apart: 21, of which 9 were waited for; matrix products, arithmetic and copies ran while one was open for 26% of the time, Pallas kernels for 4%

profile of v3, /device:TPU:0, one launch (start us, length us, event | category | flops | bytes accessed | tf_op | source)
XLA Modules:
  0.0 121.4 jit_solution(7652132143180452291)
XLA Ops:
  0.0 1.4 %slice_bitcast_fusion.1 = (bf16[1,112,2048]{2,1,0:T(8,128)(2,1)S(1)}, bf16[1,112,2048]{2,1,0:T(8,128)(2,1)S(1)}) fusion(bf16[504,2048]{1,0:T(8,128)(2,1)} %param.10), kind=kLoop, calls=%fused_computation.66 | loop fusion | bytes 1835008 | tf_op jit(solution)/shard_map/stack | solution.py:307
  2.4 3.0 %collective-permute-start.3 = (bf16[2,112,2048]{2,1,0:T(8,128)(2,1)}, bf16[2,112,2048]{2,1,0:T(8,128)(2,1)}, u32[]{:S(2)}, u32[]{:S(2)}) collective-permute-start(bf16[2,112,2048]{2,1,0:T(8,128)(2,1)} %pad_maximum_fusion.1), channel_id=1, source_target_pairs={{0,2},{1,3},{2,0},{3,1},{4,6},{5,7},{6,4},{7,5},{8,10},{9,11},{10,... | collective-permute-start | bytes 2752520 | tf_op jit(solution)/shard_map/ppermute | solution.py:232
  6.2 2.0 %copy-done = bf16[2048,1024]{1,0:T(8,128)(2,1)S(1)} copy-done((bf16[2048,1024]{1,0:T(8,128)(2,1)S(1)}, bf16[2048,1024]{1,0:T(8,128)(2,1)}, u32[]{:S(2)}) %copy-start) | copy-done | bytes 4194328
  8.2 2.3 %fusion.16 = f32[1,1,2,256,1024]{4,3,2,1,0:T(8,128)S(1)} fusion(bf16[2,256,2048]{2,1,0:T(8,128)(2,1)S(1)} %pad_maximum_fusion, bf16[2048,1024]{1,0:T(8,128)(2,1)S(1)} %copy-done), kind=kOutput, calls=%fused_computation.22 | convolution fusion | flops 2147483648 | bytes 8388608 | tf_op jit(solution)/shard_map/dot_general | solution.py:261
  10.6 1.3 %fusion.43 = f16[1,1,256,1024]{3,2,1,0:T(8,128)(2,1)} fusion(f32[1,1,2,256,1024]{4,3,2,1,0:T(8,128)S(1)} %fusion.16, pred[]{:T(512)S(6)} %eq.87), kind=kLoop, calls=%fused_computation.57 | loop fusion | flops 524288 | bytes 2621441 | tf_op jit(solution)/shard_map/convert_element_type | solution.py:272
  11.9 1.5 %collective-permute-start = (f16[1,1,256,1024]{3,2,1,0:T(8,128)(2,1)}, f16[1,1,256,1024]{3,2,1,0:T(8,128)(2,1)S(1)}, u32[]{:S(2)}, u32[]{:S(2)}) collective-permute-start(f16[1,1,256,1024]{3,2,1,0:T(8,128)(2,1)} %fusion.43), channel_id=1, source_target_pairs={{0,4},{4,0},{8,12},{12,8},{16,20},{20,16},{24,28},{28,24},{1,5},{5... | collective-permute-start | bytes 1572872 | tf_op jit(solution)/shard_map/ppermute | solution.py:235
  16.5 4.3 %shard_map.91.sto_ref = f32[16,1024]{1,0:T(8,128)} custom-call(bf16[5,252,1024]{2,1,0:T(8,128)(2,1)} %err_ref.2), custom_call_target="tpu_custom_call" | custom-call | flops 7741440 | bytes 2580480 | tf_op jit(solution)/shard_map/pallas_call | solution.py:60
  21.7 5.2 %fusion.19 = f32[1,1,2,256,1024]{4,3,2,1,0:T(8,128)S(1)} fusion(bf16[2,256,2048]{2,1,0:T(8,128)(2,1)} %copy-done.5, bf16[2048,1024]{1,0:T(8,128)(2,1)} %collective-permute-done.1), kind=kOutput, calls=%fused_computation.23 | convolution fusion | flops 2147483648 | bytes 8388608 | tf_op jit(solution)/shard_map/dot_general | solution.py:261
  28.8 1.6 %collective-permute-start.2 = (f16[1,256,1024]{2,1,0:T(8,128)(2,1)S(1)}, f16[1,256,1024]{2,1,0:T(8,128)(2,1)S(1)}, u32[]{:S(2)}, u32[]{:S(2)}) collective-permute-start(f16[1,256,1024]{2,1,0:T(8,128)(2,1)S(1)} %get-tuple-element.65), channel_id=1, source_target_pairs={{1,9},{5,13},{3,11},{7,15},{8,0},{12,4},{10,2},{14,6},{17,25},{21,... | collective-permute-start | bytes 1572872 | tf_op jit(solution)/shard_map/ppermute | solution.py:284
  30.4 3.6 %fusion.25 = f32[1,2,112,1024]{3,2,0,1:T(8,128)S(1)} fusion(bf16[2,112,2048]{2,1,0:T(8,128)(2,1)} %collective-permute-done.3, bf16[2048,1024]{1,0:T(8,128)(2,1)} %collective-permute-done.1), kind=kOutput, calls=%fused_computation.26 | convolution fusion | flops 939524096 | bytes 6029312 | tf_op jit(solution)/shard_map/dot_general | solution.py:261
  34.0 2.3 %fusion.22 = f32[1,2,112,1024]{3,2,0,1:T(8,128)S(1)} fusion(bf16[2,112,2048]{2,1,0:T(8,128)(2,1)} %collective-permute-done.3, bf16[2048,1024]{1,0:T(8,128)(2,1)S(1)} %copy-done.1), kind=kOutput, calls=%fused_computation.25 | convolution fusion | flops 939524096 | bytes 6029312 | tf_op jit(solution)/shard_map/dot_general | solution.py:261
  36.3 1.6 %collective-permute-start.10 = (bf16[2,48,2048]{2,1,0:T(8,128)(2,1)S(1)}, bf16[2,48,2048]{2,1,0:T(8,128)(2,1)S(1)}, u32[]{:S(2)}, u32[]{:S(2)}) collective-permute-start(bf16[2,48,2048]{2,1,0:T(8,128)(2,1)S(1)} %pad_maximum_fusion.4), channel_id=1, source_target_pairs={{0,2},{1,3},{2,0},{3,1},{4,6},{5,7},{6,4},{7,5},{8,10},{9,11},{10,... | collective-permute-start | bytes 1179656 | tf_op jit(solution)/shard_map/ppermute | solution.py:232
  40.4 1.3 %collective-permute-start.4 = (f16[1,256,1024]{2,1,0:T(8,128)(2,1)S(1)}, f16[1,256,1024]{2,1,0:T(8,128)(2,1)S(1)}, u32[]{:S(2)}, u32[]{:S(2)}) collective-permute-start(f16[1,256,1024]{2,1,0:T(8,128)(2,1)S(1)} %fusion.40), channel_id=1, source_target_pairs={{2,18},{6,22},{11,27},{15,31},{16,0},{20,4},{25,9},{29,13}} | collective-permute-start | bytes 1572872 | tf_op jit(solution)/shard_map/ppermute | solution.py:294
  42.0 1.5 %collective-permute-start.7 = (f16[1,256,1024]{2,1,0:T(8,128)(2,1)S(1)}, f16[1,256,1024]{2,1,0:T(8,128)(2,1)S(1)}, u32[]{:S(2)}, u32[]{:S(2)}) collective-permute-start(f16[1,256,1024]{2,1,0:T(8,128)(2,1)S(1)} %get-tuple-element.63), channel_id=1, source_target_pairs={{1,9},{5,13},{3,11},{7,15},{8,0},{12,4},{10,2},{14,6},{17,25},{21,... | collective-permute-start | bytes 1572872 | tf_op jit(solution)/shard_map/ppermute | solution.py:284
  43.7 3.2 %fusion.31 = f32[1,2,96,1024]{3,2,0,1:T(8,128)S(1)} fusion(bf16[2,96,2048]{2,1,0:T(8,128)(2,1)S(1)} %collective-permute-done.8, bf16[2048,1024]{1,0:T(8,128)(2,1)} %collective-permute-done.1), kind=kOutput, calls=%fused_computation.28 | convolution fusion | flops 805306368 | bytes 5767168 | tf_op jit(solution)/shard_map/dot_general | solution.py:261
  48.1 2.1 %collective-permute-start.12 = (f16[2,1,96,1024]{3,2,0,1:T(8,128)(2,1)S(1)}, f16[2,1,96,1024]{3,2,0,1:T(8,128)(2,1)S(1)}, u32[]{:S(2)}, u32[]{:S(2)}) collective-permute-start(f16[2,1,96,1024]{3,2,0,1:T(8,128)(2,1)S(1)} %fusion.49), channel_id=1, source_target_pairs={{0,4},{4,0},{8,12},{12,8},{16,20},{20,16},{24,28},{28,24},{1,5},{5... | collective-permute-start | bytes 1179656 | tf_op jit(solution)/shard_map/ppermute | solution.py:235
  50.2 8.4 %collective-permute-done.7 = f16[1,256,1024]{2,1,0:T(8,128)(2,1)S(1)} collective-permute-done((f16[1,256,1024]{2,1,0:T(8,128)(2,1)S(1)}, f16[1,256,1024]{2,1,0:T(8,128)(2,1)S(1)}, u32[]{:S(2)}, u32[]{:S(2)}) %collective-permute-start.7) | collective-permute-done | bytes 524320 | tf_op jit(solution)/shard_map/ppermute | solution.py:284
  59.1 1.3 %collective-permute-start.9 = (f16[2,112,1024]{2,1,0:T(8,128)(2,1)S(1)}, f16[2,112,1024]{2,1,0:T(8,128)(2,1)S(1)}, u32[]{:S(2)}, u32[]{:S(2)}) collective-permute-start(f16[2,112,1024]{2,1,0:T(8,128)(2,1)S(1)} %get-tuple-element.61), channel_id=1, source_target_pairs={{1,9},{5,13},{3,11},{7,15},{8,0},{12,4},{10,2},{14,6},{17,25},{21,... | collective-permute-start | bytes 1376264 | tf_op jit(solution)/shard_map/ppermute | solution.py:284
  60.4 3.0 %fusion.37 = f32[1,2,48,1024]{3,2,0,1:T(8,128)S(1)} fusion(bf16[2,48,2048]{2,1,0:T(8,128)(2,1)S(1)} %collective-permute-done.10, bf16[2048,1024]{1,0:T(8,128)(2,1)} %collective-permute-done.1), kind=kOutput, calls=%fused_computation.30 | convolution fusion | flops 402653184 | bytes 4980736 | tf_op jit(solution)/shard_map/dot_general | solution.py:261
  64.2 1.3 %collective-permute-start.18 = (f16[1,256,1024]{2,1,0:T(8,128)(2,1)S(1)}, f16[1,256,1024]{2,1,0:T(8,128)(2,1)S(1)}, u32[]{:S(2)}, u32[]{:S(2)}) collective-permute-start(f16[1,256,1024]{2,1,0:T(8,128)(2,1)S(1)} %fusion.41), channel_id=1, source_target_pairs={{2,18},{6,22},{11,27},{15,31},{16,0},{20,4},{25,9},{29,13}} | collective-permute-start | bytes 1572872 | tf_op jit(solution)/shard_map/ppermute | solution.py:294
  66.4 3.0 %collective-permute-done.9 = f16[2,112,1024]{2,1,0:T(8,128)(2,1)S(1)} collective-permute-done((f16[2,112,1024]{2,1,0:T(8,128)(2,1)S(1)}, f16[2,112,1024]{2,1,0:T(8,128)(2,1)S(1)}, u32[]{:S(2)}, u32[]{:S(2)}) %collective-permute-start.9) | collective-permute-done | bytes 458784 | tf_op jit(solution)/shard_map/ppermute | solution.py:284
  69.8 1.3 %collective-permute-start.13 = (f16[2,96,1024]{2,1,0:T(8,128)(2,1)S(1)}, f16[2,96,1024]{2,1,0:T(8,128)(2,1)S(1)}, u32[]{:S(2)}, u32[]{:S(2)}) collective-permute-start(f16[2,96,1024]{2,1,0:T(8,128)(2,1)S(1)} %get-tuple-element.59), channel_id=1, source_target_pairs={{1,9},{5,13},{3,11},{7,15},{8,0},{12,4},{10,2},{14,6},{17,25},{21,... | collective-permute-start | bytes 1179656 | tf_op jit(solution)/shard_map/ppermute | solution.py:284
  71.4 5.6 %collective-permute-start.11 = (f16[2,112,1024]{2,1,0:T(8,128)(2,1)S(1)}, f16[2,112,1024]{2,1,0:T(8,128)(2,1)S(1)}, u32[]{:S(2)}, u32[]{:S(2)}) collective-permute-start(f16[2,112,1024]{2,1,0:T(8,128)(2,1)S(1)} %fusion.42), channel_id=1, source_target_pairs={{0,16},{4,20},{9,25},{13,29},{18,2},{22,6},{27,11},{31,15}} | collective-permute-start | bytes 1376264 | tf_op jit(solution)/shard_map/ppermute | solution.py:294
  78.5 3.8 %collective-permute-done.13 = f16[2,96,1024]{2,1,0:T(8,128)(2,1)S(1)} collective-permute-done((f16[2,96,1024]{2,1,0:T(8,128)(2,1)S(1)}, f16[2,96,1024]{2,1,0:T(8,128)(2,1)S(1)}, u32[]{:S(2)}, u32[]{:S(2)}) %collective-permute-start.13) | collective-permute-done | bytes 393248 | tf_op jit(solution)/shard_map/ppermute | solution.py:284
  82.5 2.8 %collective-permute-start.14 = (f16[2,96,1024]{2,1,0:T(8,128)(2,1)S(1)}, f16[2,96,1024]{2,1,0:T(8,128)(2,1)S(1)}, u32[]{:S(2)}, u32[]{:S(2)}) collective-permute-start(f16[2,96,1024]{2,1,0:T(8,128)(2,1)S(1)} %fusion.45), channel_id=1, source_target_pairs={{0,16},{4,20},{9,25},{13,29},{18,2},{22,6},{27,11},{31,15}} | collective-permute-start | bytes 1179656 | tf_op jit(solution)/shard_map/ppermute | solution.py:294
  87.1 5.9 %collective-permute-done.16 = f16[2,48,1024]{2,1,0:T(8,128)(2,1)S(1)} collective-permute-done((f16[2,48,1024]{2,1,0:T(8,128)(2,1)S(1)}, f16[2,48,1024]{2,1,0:T(8,128)(2,1)S(1)}, u32[]{:S(2)}, u32[]{:S(2)}) %collective-permute-start.16) | collective-permute-done | bytes 196640 | tf_op jit(solution)/shard_map/ppermute | solution.py:284
  93.0 1.3 %collective-permute-start.17 = (f16[2,48,1024]{2,1,0:T(8,128)(2,1)S(1)}, f16[2,48,1024]{2,1,0:T(8,128)(2,1)S(1)}, u32[]{:S(2)}, u32[]{:S(2)}) collective-permute-start(f16[2,48,1024]{2,1,0:T(8,128)(2,1)S(1)} %fusion.52), channel_id=1, source_target_pairs={{0,16},{4,20},{9,25},{13,29},{18,2},{22,6},{27,11},{31,15}} | collective-permute-start | bytes 589832 | tf_op jit(solution)/shard_map/ppermute | solution.py:294
  94.8 2.7 %collective-permute-done.17 = f16[2,48,1024]{2,1,0:T(8,128)(2,1)S(1)} collective-permute-done((f16[2,48,1024]{2,1,0:T(8,128)(2,1)S(1)}, f16[2,48,1024]{2,1,0:T(8,128)(2,1)S(1)}, u32[]{:S(2)}, u32[]{:S(2)}) %collective-permute-start.17) | collective-permute-done | bytes 196640 | tf_op jit(solution)/shard_map/ppermute | solution.py:294
  97.7 1.4 %collective-permute-done.20 = f32[48,1024]{1,0:T(8,128)S(1)} collective-permute-done((f32[48,1024]{1,0:T(8,128)S(1)}, f32[48,1024]{1,0:T(8,128)S(1)}, u32[]{:S(2)}, u32[]{:S(2)}) %collective-permute-start.20) | collective-permute-done | bytes 196640 | tf_op jit(solution)/shard_map/ppermute | solution.py:232
  100.3 5.6 %shard_map.92 = (f32[252,1024]{1,0:T(8,128)}, f32[32,128]{1,0:T(8,128)}) custom-call(f32[256,1024]{1,0:T(8,128)} %maximum_add_fusion.lad_ref, f32[252,1024]{1,0:T(8,128)} %src_ref.1, f32[252,128]{1,0:T(8,128)} %broadcast_in_dim.71.occ_ref, f32[1,1024]{1,0:T(1,128)} %bitcast.137, bf16[5,252,1024]{2,1,0:T(8,128)(2,1)} %amp_ref.3, ...), custom_call_target="tpu_custom_call" | custom-call | flops 5160960 | bytes 6193152 | tf_op jit(solution)/shard_map/pallas_call | solution.py:115
  105.9 11.0 %all_to_all.11 = f32[32,1,128]{2,1,0:T(1,128)} all-to-all(f32[32,1,128]{2,1,0:T(1,128)} %bitcast.138), channel_id=1, replica_groups=mesh['row'=8,'col'=4] {'row','col'}, dimensions={0} | all-to-all | bytes 32768 | tf_op jit(solution)/shard_map/all_to_all | solution.py:385
  116.9 4.5 %shard_map.93 = f32[252,1024]{1,0:T(8,128)} custom-call(f32[32,128]{1,0:T(8,128)} %bitcast.136, f32[252,1024]{1,0:T(8,128)} %get-tuple-element.52.raw_ref, bf16[5,252,1024]{2,1,0:T(8,128)(2,1)} %amp_ref.3), custom_call_target="tpu_custom_call" | custom-call | tf_op jit(solution)/shard_map/pallas_call | solution.py:197
  (89 shorter events, 19.8 us)
Async XLA Ops:
  0.0 5.7 %copy-start.9 = (pred[256]{0:T(512)(128)(4,1)S(1)}, pred[256]{0:T(512)(128)(4,1)}, u32[]{:S(2)}) copy-start(pred[256]{0:T(512)(128)(4,1)} %constant.66.clone.1) | copy-start | bytes 772
  0.0 5.4 %copy-start.2 = (bf16[504,2048]{1,0:T(8,128)(2,1)S(1)}, bf16[504,2048]{1,0:T(8,128)(2,1)}, u32[]{:S(2)}) copy-start(bf16[504,2048]{1,0:T(8,128)(2,1)} %param.10) | copy-start | bytes 6193156
  2.4 28.0 %collective-permute-start.3 = (bf16[2,112,2048]{2,1,0:T(8,128)(2,1)}, bf16[2,112,2048]{2,1,0:T(8,128)(2,1)}, u32[]{:S(2)}, u32[]{:S(2)}) collective-permute-start(bf16[2,112,2048]{2,1,0:T(8,128)(2,1)} %pad_maximum_fusion.1), channel_id=1, source_target_pairs={{0,2},{1,3},{2,0},{3,1},{4,6},{5,7},{6,4},{7,5},{8,10},{9,11},{10,... | collective-permute-start | bytes 2752520 | tf_op jit(solution)/shard_map/ppermute | solution.py:232
  5.4 16.3 %collective-permute-start.1 = (bf16[2048,1024]{1,0:T(8,128)(2,1)}, bf16[2048,1024]{1,0:T(8,128)(2,1)}, u32[]{:S(2)}, u32[]{:S(2)}) collective-permute-start(bf16[2048,1024]{1,0:T(8,128)(2,1)} %param.9), channel_id=1, source_target_pairs={{0,1},{1,0},{2,3},{3,2},{4,5},{5,4},{6,7},{7,6},{8,9},{9,8},{10,11... | collective-permute-start | bytes 12582920 | tf_op jit(solution)/shard_map/ppermute | solution.py:232
  6.0 2.2 %copy-start = (bf16[2048,1024]{1,0:T(8,128)(2,1)S(1)}, bf16[2048,1024]{1,0:T(8,128)(2,1)}, u32[]{:S(2)}) copy-start(bf16[2048,1024]{1,0:T(8,128)(2,1)} %param.9) | copy-start | bytes 12582916
  8.2 2.4 %copy-start.5 = (bf16[2,256,2048]{2,1,0:T(8,128)(2,1)}, bf16[2,256,2048]{2,1,0:T(8,128)(2,1)S(1)}, u32[]{:S(2)}) copy-start(bf16[2,256,2048]{2,1,0:T(8,128)(2,1)S(1)} %pad_maximum_fusion) | copy-start | bytes 6291460
  10.6 3.9 %copy-start.3 = (f32[1,1,2,256,1024]{4,3,2,1,0:T(8,128)}, f32[1,1,2,256,1024]{4,3,2,1,0:T(8,128)S(1)}, u32[]{:S(2)}) copy-start(f32[1,1,2,256,1024]{4,3,2,1,0:T(8,128)S(1)} %fusion.16) | copy-start | bytes 6291460
  10.6 4.4 %copy-start.8 = (s32[2,252]{1,0:T(2,128)S(1)}, s32[2,252]{1,0:T(2,128)}, u32[]{:S(2)}) copy-start(s32[2,252]{1,0:T(2,128)} %param.16) | copy-start | bytes 6052
  10.6 4.4 %copy-start.10 = (f32[64]{0:T(128)S(1)}, f32[64]{0:T(128)}, u32[]{:S(2)}) copy-start(f32[64]{0:T(128)} %param.14) | copy-start | bytes 772
  10.6 4.5 %copy-start.6 = (s32[2,1024]{1,0:T(2,128)S(1)}, s32[2,1024]{1,0:T(2,128)}, u32[]{:S(2)}) copy-start(s32[2,1024]{1,0:T(2,128)} %param.17) | copy-start | bytes 24580
  10.6 4.5 %copy-start.7 = (f32[800]{0:T(1024)S(1)}, f32[800]{0:T(1024)}, u32[]{:S(2)}) copy-start(f32[800]{0:T(1024)} %param.15) | copy-start | bytes 9604
  11.9 15.3 %collective-permute-start = (f16[1,1,256,1024]{3,2,1,0:T(8,128)(2,1)}, f16[1,1,256,1024]{3,2,1,0:T(8,128)(2,1)S(1)}, u32[]{:S(2)}, u32[]{:S(2)}) collective-permute-start(f16[1,1,256,1024]{3,2,1,0:T(8,128)(2,1)} %fusion.43), channel_id=1, source_target_pairs={{0,4},{4,0},{8,12},{12,8},{16,20},{20,16},{24,28},{28,24},{1,5},{5... | collective-permute-start | bytes 1572872 | tf_op jit(solution)/shard_map/ppermute | solution.py:235
  14.5 29.2 %collective-permute-start.8 = (bf16[2,96,2048]{2,1,0:T(8,128)(2,1)}, bf16[2,96,2048]{2,1,0:T(8,128)(2,1)S(1)}, u32[]{:S(2)}, u32[]{:S(2)}) collective-permute-start(bf16[2,96,2048]{2,1,0:T(8,128)(2,1)} %pad_maximum_fusion.3), channel_id=1, source_target_pairs={{0,2},{1,3},{2,0},{3,1},{4,6},{5,7},{6,4},{7,5},{8,10},{9,11},{10,... | collective-permute-start | bytes 2359304 | tf_op jit(solution)/shard_map/ppermute | solution.py:232
  26.9 1.6 %copy-start.4 = (f32[1,1,2,256,1024]{4,3,2,1,0:T(8,128)S(1)}, f32[1,1,2,256,1024]{4,3,2,1,0:T(8,128)}, u32[]{:S(2)}) copy-start(f32[1,1,2,256,1024]{4,3,2,1,0:T(8,128)} %copy-done.3) | copy-start | bytes 6291460
  27.1 14.5 %collective-permute-start.6 = (f16[1,1,256,1024]{3,2,1,0:T(8,128)(2,1)S(1)}, f16[1,1,256,1024]{3,2,1,0:T(8,128)(2,1)S(1)}, u32[]{:S(2)}, u32[]{:S(2)}) collective-permute-start(f16[1,1,256,1024]{3,2,1,0:T(8,128)(2,1)S(1)} %fusion.44), channel_id=1, source_target_pairs={{0,4},{4,0},{8,12},{12,8},{16,20},{20,16},{24,28},{28,24},{1,5},{5... | collective-permute-start | bytes 1572872 | tf_op jit(solution)/shard_map/ppermute | solution.py:235
  28.8 5.2 %copy-start.1 = (bf16[2048,1024]{1,0:T(8,128)(2,1)S(1)}, bf16[2048,1024]{1,0:T(8,128)(2,1)}, u32[]{:S(2)}) copy-start(bf16[2048,1024]{1,0:T(8,128)(2,1)} %param.9) | copy-start | bytes 12582916
  28.8 11.3 %collective-permute-start.2 = (f16[1,256,1024]{2,1,0:T(8,128)(2,1)S(1)}, f16[1,256,1024]{2,1,0:T(8,128)(2,1)S(1)}, u32[]{:S(2)}, u32[]{:S(2)}) collective-permute-start(f16[1,256,1024]{2,1,0:T(8,128)(2,1)S(1)} %get-tuple-element.65), channel_id=1, source_target_pairs={{1,9},{5,13},{3,11},{7,15},{8,0},{12,4},{10,2},{14,6},{17,25},{21,... | collective-permute-start | bytes 1572872 | tf_op jit(solution)/shard_map/ppermute | solution.py:284
  36.3 24.0 %collective-permute-start.10 = (bf16[2,48,2048]{2,1,0:T(8,128)(2,1)S(1)}, bf16[2,48,2048]{2,1,0:T(8,128)(2,1)S(1)}, u32[]{:S(2)}, u32[]{:S(2)}) collective-permute-start(bf16[2,48,2048]{2,1,0:T(8,128)(2,1)S(1)} %pad_maximum_fusion.4), channel_id=1, source_target_pairs={{0,2},{1,3},{2,0},{3,1},{4,6},{5,7},{6,4},{7,5},{8,10},{9,11},{10,... | collective-permute-start | bytes 1179656 | tf_op jit(solution)/shard_map/ppermute | solution.py:232
  38.3 20.5 %collective-permute-start.5 = (f16[2,1,112,1024]{3,2,0,1:T(8,128)(2,1)S(1)}, f16[2,1,112,1024]{3,2,0,1:T(8,128)(2,1)S(1)}, u32[]{:S(2)}, u32[]{:S(2)}) collective-permute-start(f16[2,1,112,1024]{3,2,0,1:T(8,128)(2,1)S(1)} %fusion.46), channel_id=1, source_target_pairs={{0,4},{4,0},{8,12},{12,8},{16,20},{20,16},{24,28},{28,24},{1,5},{5... | collective-permute-start | bytes 1376264 | tf_op jit(solution)/shard_map/ppermute | solution.py:235
  40.4 30.8 %collective-permute-start.4 = (f16[1,256,1024]{2,1,0:T(8,128)(2,1)S(1)}, f16[1,256,1024]{2,1,0:T(8,128)(2,1)S(1)}, u32[]{:S(2)}, u32[]{:S(2)}) collective-permute-start(f16[1,256,1024]{2,1,0:T(8,128)(2,1)S(1)} %fusion.40), channel_id=1, source_target_pairs={{2,18},{6,22},{11,27},{15,31},{16,0},{20,4},{25,9},{29,13}} | collective-permute-start | bytes 1572872 | tf_op jit(solution)/shard_map/ppermute | solution.py:294
  42.0 16.6 %collective-permute-start.7 = (f16[1,256,1024]{2,1,0:T(8,128)(2,1)S(1)}, f16[1,256,1024]{2,1,0:T(8,128)(2,1)S(1)}, u32[]{:S(2)}, u32[]{:S(2)}) collective-permute-start(f16[1,256,1024]{2,1,0:T(8,128)(2,1)S(1)} %get-tuple-element.63), channel_id=1, source_target_pairs={{1,9},{5,13},{3,11},{7,15},{8,0},{12,4},{10,2},{14,6},{17,25},{21,... | collective-permute-start | bytes 1572872 | tf_op jit(solution)/shard_map/ppermute | solution.py:284
  48.1 21.5 %collective-permute-start.12 = (f16[2,1,96,1024]{3,2,0,1:T(8,128)(2,1)S(1)}, f16[2,1,96,1024]{3,2,0,1:T(8,128)(2,1)S(1)}, u32[]{:S(2)}, u32[]{:S(2)}) collective-permute-start(f16[2,1,96,1024]{3,2,0,1:T(8,128)(2,1)S(1)} %fusion.49), channel_id=1, source_target_pairs={{0,4},{4,0},{8,12},{12,8},{16,20},{20,16},{24,28},{28,24},{1,5},{5... | collective-permute-start | bytes 1179656 | tf_op jit(solution)/shard_map/ppermute | solution.py:235
  59.1 10.4 %collective-permute-start.9 = (f16[2,112,1024]{2,1,0:T(8,128)(2,1)S(1)}, f16[2,112,1024]{2,1,0:T(8,128)(2,1)S(1)}, u32[]{:S(2)}, u32[]{:S(2)}) collective-permute-start(f16[2,112,1024]{2,1,0:T(8,128)(2,1)S(1)} %get-tuple-element.61), channel_id=1, source_target_pairs={{1,9},{5,13},{3,11},{7,15},{8,0},{12,4},{10,2},{14,6},{17,25},{21,... | collective-permute-start | bytes 1376264 | tf_op jit(solution)/shard_map/ppermute | solution.py:284
  64.2 14.1 %collective-permute-start.18 = (f16[1,256,1024]{2,1,0:T(8,128)(2,1)S(1)}, f16[1,256,1024]{2,1,0:T(8,128)(2,1)S(1)}, u32[]{:S(2)}, u32[]{:S(2)}) collective-permute-start(f16[1,256,1024]{2,1,0:T(8,128)(2,1)S(1)} %fusion.41), channel_id=1, source_target_pairs={{2,18},{6,22},{11,27},{15,31},{16,0},{20,4},{25,9},{29,13}} | collective-permute-start | bytes 1572872 | tf_op jit(solution)/shard_map/ppermute | solution.py:294
  65.6 19.7 %collective-permute-start.15 = (f16[2,1,48,1024]{3,2,0,1:T(8,128)(2,1)S(1)}, f16[2,1,48,1024]{3,2,0,1:T(8,128)(2,1)S(1)}, u32[]{:S(2)}, u32[]{:S(2)}) collective-permute-start(f16[2,1,48,1024]{3,2,0,1:T(8,128)(2,1)S(1)} %fusion.53), channel_id=1, source_target_pairs={{0,4},{4,0},{8,12},{12,8},{16,20},{20,16},{24,28},{28,24},{1,5},{5... | collective-permute-start | bytes 589832 | tf_op jit(solution)/shard_map/ppermute | solution.py:235
  69.8 12.5 %collective-permute-start.13 = (f16[2,96,1024]{2,1,0:T(8,128)(2,1)S(1)}, f16[2,96,1024]{2,1,0:T(8,128)(2,1)S(1)}, u32[]{:S(2)}, u32[]{:S(2)}) collective-permute-start(f16[2,96,1024]{2,1,0:T(8,128)(2,1)S(1)} %get-tuple-element.59), channel_id=1, source_target_pairs={{1,9},{5,13},{3,11},{7,15},{8,0},{12,4},{10,2},{14,6},{17,25},{21,... | collective-permute-start | bytes 1179656 | tf_op jit(solution)/shard_map/ppermute | solution.py:284
  71.4 15.3 %collective-permute-start.11 = (f16[2,112,1024]{2,1,0:T(8,128)(2,1)S(1)}, f16[2,112,1024]{2,1,0:T(8,128)(2,1)S(1)}, u32[]{:S(2)}, u32[]{:S(2)}) collective-permute-start(f16[2,112,1024]{2,1,0:T(8,128)(2,1)S(1)} %fusion.42), channel_id=1, source_target_pairs={{0,16},{4,20},{9,25},{13,29},{18,2},{22,6},{27,11},{31,15}} | collective-permute-start | bytes 1376264 | tf_op jit(solution)/shard_map/ppermute | solution.py:294
  82.5 11.8 %collective-permute-start.14 = (f16[2,96,1024]{2,1,0:T(8,128)(2,1)S(1)}, f16[2,96,1024]{2,1,0:T(8,128)(2,1)S(1)}, u32[]{:S(2)}, u32[]{:S(2)}) collective-permute-start(f16[2,96,1024]{2,1,0:T(8,128)(2,1)S(1)} %fusion.45), channel_id=1, source_target_pairs={{0,16},{4,20},{9,25},{13,29},{18,2},{22,6},{27,11},{31,15}} | collective-permute-start | bytes 1179656 | tf_op jit(solution)/shard_map/ppermute | solution.py:294
  85.4 7.6 %collective-permute-start.16 = (f16[2,48,1024]{2,1,0:T(8,128)(2,1)S(1)}, f16[2,48,1024]{2,1,0:T(8,128)(2,1)S(1)}, u32[]{:S(2)}, u32[]{:S(2)}) collective-permute-start(f16[2,48,1024]{2,1,0:T(8,128)(2,1)S(1)} %get-tuple-element.57), channel_id=1, source_target_pairs={{1,9},{5,13},{3,11},{7,15},{8,0},{12,4},{10,2},{14,6},{17,25},{21,... | collective-permute-start | bytes 589832 | tf_op jit(solution)/shard_map/ppermute | solution.py:284
  93.0 4.5 %collective-permute-start.17 = (f16[2,48,1024]{2,1,0:T(8,128)(2,1)S(1)}, f16[2,48,1024]{2,1,0:T(8,128)(2,1)S(1)}, u32[]{:S(2)}, u32[]{:S(2)}) collective-permute-start(f16[2,48,1024]{2,1,0:T(8,128)(2,1)S(1)} %fusion.52), channel_id=1, source_target_pairs={{0,16},{4,20},{9,25},{13,29},{18,2},{22,6},{27,11},{31,15}} | collective-permute-start | bytes 589832 | tf_op jit(solution)/shard_map/ppermute | solution.py:294
  94.7 4.4 %collective-permute-start.19 = (f32[208,1024]{1,0:T(8,128)S(1)}, f32[208,1024]{1,0:T(8,128)S(1)}, u32[]{:S(2)}, u32[]{:S(2)}) collective-permute-start(f32[208,1024]{1,0:T(8,128)S(1)} %pad_maximum_fusion.2), channel_id=1, source_target_pairs={{0,1},{1,0},{2,3},{3,2},{4,5},{5,4},{6,7},{7,6},{8,9},{9,8},{10,11... | collective-permute-start | bytes 2555912 | tf_op jit(solution)/shard_map/ppermute | solution.py:232
  97.7 1.5 %collective-permute-start.20 = (f32[48,1024]{1,0:T(8,128)S(1)}, f32[48,1024]{1,0:T(8,128)S(1)}, u32[]{:S(2)}, u32[]{:S(2)}) collective-permute-start(f32[48,1024]{1,0:T(8,128)S(1)} %get-tuple-element.77), channel_id=1, source_target_pairs={{0,1},{1,0},{2,3},{3,2},{4,5},{5,4},{6,7},{7,6},{8,9},{9,8},{10,11... | collective-permute-start | bytes 589832 | tf_op jit(solution)/shard_map/ppermute | solution.py:232

commit v4 on v3

--- a/solution.py
+++ b/solution.py
@@ -6,6 +6,7 @@
 from jax.sharding import PartitionSpec as P
 
 f32 = jnp.float32
+small = pltpu.CompilerParams(vmem_limit_bytes=10 * 1024 * 1024)
 wire = jnp.float16
 
 
@@ -43,6 +44,40 @@
     return -(-count // 8) * 8
 
 
+def product_and_hold(left, right):
+    rows, depth = left.shape
+    width = right.shape[1]
+    block = column_block(width)
+
+    def kernel(left_ref, right_ref, out_ref, held_ref):
+        at = pl.ds(pl.multiple_of(pl.program_id(0) * block, block), block)
+        held_ref[:, at] = right_ref[...]
+        out_ref[...] = jnp.dot(left_ref[...], right_ref[...], preferred_element_type=f32)
+
+    return pl.pallas_call(
+        kernel,
+        grid=(width // block,),
+        in_specs=[
+            pl.BlockSpec((rows, depth), lambda i: (0, 0)),
+            pl.BlockSpec((depth, block), lambda i: (0, i)),
+        ],
+        out_specs=[
+            pl.BlockSpec((rows, block), lambda i: (0, i)),
+            pl.BlockSpec(memory_space=pltpu.VMEM),
+        ],
+        out_shape=[
+            jax.ShapeDtypeStruct((rows, width), f32),
+            pltpu.VMEM((depth, width), right.dtype),
+        ],
+        compiler_params=small,
+        cost_estimate=pl.CostEstimate(
+            flops=2 * rows * depth * width,
+            bytes_accessed=2 * depth * (rows + width),
+            transcendentals=0,
+        ),
+    )(left, right)
+
+
 def stored_products(hist_err):
     count, rows, width = hist_err.shape
     block = column_block(width)
@@ -59,6 +94,7 @@
 
     return pl.pallas_call(
         kernel,
+        compiler_params=small,
         grid=(width // block,),
         in_specs=[pl.BlockSpec((count, rows, block), lambda i: (0, 0, i))],
         out_specs=pl.BlockSpec((padded(len(pairs)), block), lambda i: (0, i)),
@@ -114,6 +150,7 @@
     columns = lambda i: (0, i)
     return pl.pallas_call(
         kernel,
+        compiler_params=small,
         grid=(grid,),
         in_specs=[
             pl.BlockSpec((ladder.shape[0], block), columns),
@@ -196,6 +233,7 @@
     columns = lambda i: (0, i)
     return pl.pallas_call(
         kernel,
+        compiler_params=small,
         grid=(width // block,),
         in_specs=[
             pl.BlockSpec(gathered.shape, lambda i: (0, 0)),
@@ -210,7 +248,7 @@
 
 def cuts_of(rows):
     cuts, at = [], 0
-    for part in (rows * 7 // 16, rows * 3 // 8):
+    for part in (rows * 3 // 8, rows * 5 // 16):
         size = min(max(16, -(-part // 16) * 16), rows - at)
         if size:
             cuts.append((at, size))
@@ -218,6 +256,22 @@
     if at < rows:
         cuts.append((at, rows - at))
     return cuts
+
+
+def order_of(last):
+    steps = ["p0", "n2", "p1", "f0"]
+    for n in range(3, last + 1):
+        if n > 3:
+            steps.append(f"p{n - 1}")
+        steps.append(f"n{n}")
+        if n == 3:
+            steps += ["p2", "s0"]
+        else:
+            steps.append(f"f{n - 2}")
+    if last < 3:
+        steps.append("s0")
+    steps += [f"p{last}", "f1"]
+    return steps + [f"f{n}" for n in range(max(2, last - 1), last + 1)]
 
 
 def after(x, *earlier):
@@ -324,12 +378,9 @@
         nears, pairs, fars = {}, {}, {}
         nears[0] = near_begin(multiply(own, integrals)[None])
         send_far(1, nears[0][2])
-        stored = stored_products(after(hist_err, nears[0][2]))
-        occ_energy = jnp.broadcast_to(pair_energy(occ_pair, eps_occ)[:, None], (rows, 128))
-        vir_energy = pair_energy(vir_pair, eps_vir)[None, :]
-        stored, occ_energy, vir_energy = lax.optimization_barrier((stored, occ_energy, vir_energy))
-        across = after(across, stored)
-        nears[1] = near_begin(multiply(own, across)[None])
+        across = after(across, nears[0][2])
+        beside, across = product_and_hold(own.reshape(-1, depth), across)
+        nears[1] = near_begin(beside.reshape(1, near, -1, width))
         send_far(2, nears[1][2])
         last = len(stages) + 1
 
@@ -342,27 +393,30 @@
             return nears[n][2]
 
         def to_pair(n, token):
-            if 0 <= n <= last:
-                keep, taken, _ = nears[n]
-                pairs[n] = pair_begin(keep + after(taken, token).astype(f32))
-                token = pairs[n][2]
-            return token
+            keep, taken, _ = nears[n]
+            pairs[n] = pair_begin(keep + after(taken, token).astype(f32))
+            return pairs[n][2]
 
         def to_far(n, token):
-            if 0 <= n <= last:
-                keep, taken, _ = pairs[n]
-                kept = jnp.where(holder, keep, 0.0) + after(taken, token).astype(f32)
-                fars[n] = far_begin(kept, stages[n - 2][0] // 2 if n >= 2 else 0)
-                token = fars[n][2]
-            return token
+            keep, taken, _ = pairs[n]
+            kept = jnp.where(holder, keep, 0.0) + after(taken, token).astype(f32)
+            fars[n] = far_begin(kept, stages[n - 2][0] // 2 if n >= 2 else 0)
+            return fars[n][2]
+
+        def reduce_stored(token):
+            out = stored_products(after(hist_err, token))
+            occ = jnp.broadcast_to(pair_energy(occ_pair, eps_occ)[:, None], (rows, 128))
+            vir = pair_energy(vir_pair, eps_vir)[None, :]
+            return lax.optimization_barrier((out, occ, vir))
 
         token = nears[1][2]
-        for n in range(2, last + 3):
-            token = to_far(n - 3, token)
-            token = to_pair(n - 2, token)
-            if n <= last:
-                token = to_near(n, token)
-        token = to_far(last, token)
+        for step in order_of(last):
+            kind, n = step[0], int(step[1:])
+            if kind == "s":
+                stored, occ_energy, vir_energy = reduce_stored(token)
+                token = stored
+            else:
+                token = {"n": to_near, "p": to_pair, "f": to_far}[kind](n, token)
 
         first = far_end(*fars[0][:2])[0]
         second = far_end(*fars[1][:2])[0]

time: 122 us -> 113 us (0.926)
  matrix products: 21.4 us -> 10.2 us
  waiting for transfers between devices: 27.7 us -> 20.5 us
  other arithmetic: 10.7 us -> 15.6 us
  starting transfers between devices: 29.7 us -> 32.1 us
  local copies, waits for them, and re-layouts: 5.9 us -> 8.22 us
  Pallas kernels: 14.4 us -> 13 us
    ppermute x5, waiting for transfers between devices: 22.2 us -> 10.7 us  [pair_begin(): return (part, lax.ppermute(send, ('row', 'col'), even_links), send)]
    dot_general x8 -> x7, matrix products: 21.4 us -> 10.2 us  [multiply(): out = jnp.dot(piece.reshape(-1, depth), right, preferred_element_type=f32)]
    convert_element_type x5, other arithmetic: 1.23 us -> 4.82 us  [pair_begin(): send = part.astype(wire)]
    ppermute x5, waiting for transfers between devices: 0.01 us -> 3.59 us  [send_row(): return lax.ppermute(x, 'row', [(i, i ^ m) for i in range(row_n)])]
    unnamed x22 -> x50, local copies, waits for them, and re-layouts: 3.27 us -> 6.26 us
    ppermute x5, starting transfers between devices: 5.32 us -> 7.49 us  [send_row(): return lax.ppermute(x, 'row', [(i, i ^ m) for i in range(row_n)])]
    pallas_call x3 -> x4, Pallas kernels: 14.4 us -> 13 us  [the longest x1 5.18 us: product_and_hold(): pl.pallas_call(kernel, grid=(width // block,), in_specs=[pl.BlockSpec((ro...]
  transfers between devices with their start and end apart: 21 -> 21, of which waited for: 9 -> 6; matrix products, arithmetic and copies ran while one was open for 26% -> 22% of each run, Pallas kernels for 4% -> 7%
where the time goes in v4:
time: 113 us; the launch traced here: 112 us
  starting transfers between devices  32.1 us (28%)
  waiting for transfers between devices  20.5 us (18%)
  other arithmetic  15.6 us (14%)
  Pallas kernels  13 us (12%)
  blocking collectives  11.9 us (11%)
  matrix products  10.2 us (9%)
  local copies, waits for them, and re-layouts  8.22 us (7%)
    ppermute x5, starting transfers between devices, far_begin(): taken.append(lax.ppermute(data, ('row', 'col'), links))  13.3 us
    all_to_all x1, blocking collectives, on_device(): gathered = lax.all_to_all(shares, ('row', 'col'), 0, 0, tiled=True)  11.9 us
    ppermute x5, waiting for transfers between devices, pair_begin(): return (part, lax.ppermute(send, ('row', 'col'), even_links), send)  10.7 us
    dot_general x7, matrix products, multiply(): out = jnp.dot(piece.reshape(-1, depth), right, preferred_element_type=f32)  10.2 us
    ppermute x5, starting transfers between devices, send_row(): return lax.ppermute(x, 'row', [(i, i ^ m) for i in range(row_n)])  7.49 us
    ppermute x5, starting transfers between devices, pair_begin(): return (part, lax.ppermute(send, ('row', 'col'), even_links), send)  7.3 us
    unnamed x50, local copies, waits for them, and re-layouts  6.26 us
    pallas_call x1, Pallas kernels, product_and_hold(): pl.pallas_call(kernel, grid=(width // block,), in_specs=[pl.BlockSpec((ro...  5.18 us
  transfers between devices with their start and end apart: 21, of which 6 were waited for; matrix products, arithmetic and copies ran while one was open for 22% of the time, Pallas kernels for 7%

profile of v4, /device:TPU:0, one launch (start us, length us, event | category | flops | bytes accessed | tf_op | source)
XLA Modules:
  0.0 112.4 jit_solution(1909458764753441226)
XLA Ops:
  0.0 1.4 %slice_bitcast_fusion.1 = (bf16[1,96,2048]{2,1,0:T(8,128)(2,1)S(1)}, bf16[1,96,2048]{2,1,0:T(8,128)(2,1)S(1)}) fusion(bf16[504,2048]{1,0:T(8,128)(2,1)} %param.10), kind=kLoop, calls=%fused_computation.69 | loop fusion | bytes 1572864 | tf_op jit(solution)/shard_map/stack | solution.py:361
  2.8 2.5 %collective-permute-start.4 = (bf16[2,96,2048]{2,1,0:T(8,128)(2,1)}, bf16[2,96,2048]{2,1,0:T(8,128)(2,1)}, u32[]{:S(2)}, u32[]{:S(2)}) collective-permute-start(bf16[2,96,2048]{2,1,0:T(8,128)(2,1)} %pad_maximum_fusion.1), channel_id=1, source_target_pairs={{0,2},{1,3},{2,0},{3,1},{4,6},{5,7},{6,4},{7,5},{8,10},{9,11},{10,... | collective-permute-start | bytes 2359304 | tf_op jit(solution)/shard_map/ppermute | solution.py:286
  6.1 2.0 %copy-done.5 = bf16[2048,1024]{1,0:T(8,128)(2,1)S(1)} copy-done((bf16[2048,1024]{1,0:T(8,128)(2,1)S(1)}, bf16[2048,1024]{1,0:T(8,128)(2,1)}, u32[]{:S(2)}) %copy-start.5) | copy-done | bytes 4194328
  8.1 2.4 %fusion.14 = f32[1,1,2,256,1024]{4,3,2,1,0:T(8,128)S(1)} fusion(bf16[2,256,2048]{2,1,0:T(8,128)(2,1)S(1)} %pad_maximum_fusion, bf16[2048,1024]{1,0:T(8,128)(2,1)S(1)} %copy-done.5), kind=kOutput, calls=%fused_computation.19 | convolution fusion | flops 2147483648 | bytes 8388608 | tf_op jit(solution)/shard_map/dot_general | solution.py:315
  11.5 1.5 %collective-permute-start = (f16[1,1,256,1024]{3,2,1,0:T(8,128)(2,1)}, f16[1,1,256,1024]{3,2,1,0:T(8,128)(2,1)S(1)}, u32[]{:S(2)}, u32[]{:S(2)}) collective-permute-start(f16[1,1,256,1024]{3,2,1,0:T(8,128)(2,1)} %fusion.37), channel_id=1, source_target_pairs={{0,4},{4,0},{8,12},{12,8},{16,20},{20,16},{24,28},{28,24},{1,5},{5... | collective-permute-start | bytes 1572872 | tf_op jit(solution)/shard_map/ppermute | solution.py:289
  16.5 5.2 %shard_map.91 = (f32[512,1024]{1,0:T(8,128)S(1)}, bf16[2048,1024]{1,0:T(8,128)(2,1)S(1)}) custom-call(bf16[512,2048]{1,0:T(8,128)(2,1)S(1)} %bitcast.128, bf16[2048,1024]{1,0:T(8,128)(2,1)} %collective-permute-done.1.right_ref), custom_call_target="tpu_custom_call" | custom-call | flops 2147483648 | bytes 6291456 | tf_op jit(solution)/shard_map/pallas_call | solution.py:57
  21.9 1.5 %collective-permute-start.3 = (f16[1,1,256,1024]{3,2,1,0:T(8,128)(2,1)S(1)}, f16[1,1,256,1024]{3,2,1,0:T(8,128)(2,1)S(1)}, u32[]{:S(2)}, u32[]{:S(2)}) collective-permute-start(f16[1,1,256,1024]{3,2,1,0:T(8,128)(2,1)S(1)} %fusion.38), channel_id=1, source_target_pairs={{0,4},{4,0},{8,12},{12,8},{16,20},{20,16},{24,28},{28,24},{1,5},{5... | collective-permute-start | bytes 1572872 | tf_op jit(solution)/shard_map/ppermute | solution.py:289
  23.5 3.0 %collective-permute-done = f16[1,1,256,1024]{3,2,1,0:T(8,128)(2,1)S(1)} collective-permute-done((f16[1,1,256,1024]{3,2,1,0:T(8,128)(2,1)}, f16[1,1,256,1024]{3,2,1,0:T(8,128)(2,1)S(1)}, u32[]{:S(2)}, u32[]{:S(2)}) %collective-permute-start) | collective-permute-done | bytes 524320 | tf_op jit(solution)/shard_map/ppermute | solution.py:289
  26.8 1.6 %collective-permute-start.2 = (f16[1,256,1024]{2,1,0:T(8,128)(2,1)S(1)}, f16[1,256,1024]{2,1,0:T(8,128)(2,1)S(1)}, u32[]{:S(2)}, u32[]{:S(2)}) collective-permute-start(f16[1,256,1024]{2,1,0:T(8,128)(2,1)S(1)} %get-tuple-element.69), channel_id=1, source_target_pairs={{1,9},{5,13},{3,11},{7,15},{8,0},{12,4},{10,2},{14,6},{17,25},{21,... | collective-permute-start | bytes 1572872 | tf_op jit(solution)/shard_map/ppermute | solution.py:338
  29.1 2.2 %fusion.17 = f32[1,2,96,1024]{3,2,0,1:T(8,128)S(1)} fusion(bf16[2,96,2048]{2,1,0:T(8,128)(2,1)} %collective-permute-done.4, bf16[2048,1024]{1,0:T(8,128)(2,1)S(1)} %copy-done.6), kind=kOutput, calls=%fused_computation.23 | convolution fusion | flops 805306368 | bytes 5767168 | tf_op jit(solution)/shard_map/dot_general | solution.py:315
  31.2 2.2 %fusion.20 = f32[1,2,96,1024]{3,2,0,1:T(8,128)S(1)} fusion(bf16[2,96,2048]{2,1,0:T(8,128)(2,1)} %collective-permute-done.4, bf16[2048,1024]{1,0:T(8,128)(2,1)S(1)} %get-tuple-element.37), kind=kOutput, calls=%fused_computation.24 | convolution fusion | flops 805306368 | bytes 5767168 | tf_op jit(solution)/shard_map/dot_general | solution.py:315
  35.6 1.5 %collective-permute-start.6 = (f16[2,1,96,1024]{3,2,0,1:T(8,128)(2,1)}, f16[2,1,96,1024]{3,2,0,1:T(8,128)(2,1)}, u32[]{:S(2)}, u32[]{:S(2)}) collective-permute-start(f16[2,1,96,1024]{3,2,0,1:T(8,128)(2,1)} %fusion.42), channel_id=1, source_target_pairs={{0,4},{4,0},{8,12},{12,8},{16,20},{20,16},{24,28},{28,24},{1,5},{5... | collective-permute-start | bytes 1179656 | tf_op jit(solution)/shard_map/ppermute | solution.py:289
  37.1 1.5 %fusion.54 = (f16[1,256,1024]{2,1,0:T(8,128)(2,1)}, f32[1,256,1024]{2,1,0:T(8,128)}) fusion(f16[1,256,1024]{2,1,0:T(8,128)(2,1)S(1)} %bitcast.133, f32[1,1,2,256,1024]{4,3,2,1,0:T(8,128)S(1)} %bitcast.127, pred[]{:T(512)S(6)} %eq.87), kind=kLoop, calls=%fused_computation.91 | loop fusion | flops 1048576 | bytes 4194305 | tf_op jit(solution)/shard_map/convert_element_type | solution.py:337
  43.4 1.4 %collective-permute-start.10 = (f16[2,1,80,1024]{3,2,0,1:T(8,128)(2,1)}, f16[2,1,80,1024]{3,2,0,1:T(8,128)(2,1)}, u32[]{:S(2)}, u32[]{:S(2)}) collective-permute-start(f16[2,1,80,1024]{3,2,0,1:T(8,128)(2,1)} %fusion.45), channel_id=1, source_target_pairs={{0,4},{4,0},{8,12},{12,8},{16,20},{20,16},{24,28},{28,24},{1,5},{5... | collective-permute-start | bytes 983048 | tf_op jit(solution)/shard_map/ppermute | solution.py:289
  45.0 1.3 %collective-permute-start.13 = (f16[1,256,1024]{2,1,0:T(8,128)(2,1)}, f16[1,256,1024]{2,1,0:T(8,128)(2,1)S(1)}, u32[]{:S(2)}, u32[]{:S(2)}) collective-permute-start(f16[1,256,1024]{2,1,0:T(8,128)(2,1)} %get-tuple-element.67), channel_id=1, source_target_pairs={{1,9},{5,13},{3,11},{7,15},{8,0},{12,4},{10,2},{14,6},{17,25},{21,... | collective-permute-start | bytes 1572872 | tf_op jit(solution)/shard_map/ppermute | solution.py:338
  46.3 1.3 %collective-permute-start.5 = (f16[1,256,1024]{2,1,0:T(8,128)(2,1)}, f16[1,256,1024]{2,1,0:T(8,128)(2,1)S(1)}, u32[]{:S(2)}, u32[]{:S(2)}) collective-permute-start(f16[1,256,1024]{2,1,0:T(8,128)(2,1)} %fusion.35), channel_id=1, source_target_pairs={{2,18},{6,22},{11,27},{15,31},{16,0},{20,4},{25,9},{29,13}} | collective-permute-start | bytes 1572872 | tf_op jit(solution)/shard_map/ppermute | solution.py:348
  47.6 1.8 %fusion.53 = (f16[2,96,1024]{2,1,0:T(8,128)(2,1)S(1)}, f32[2,96,1024]{2,1,0:T(8,128)S(1)}) fusion(f16[2,96,1024]{2,1,0:T(8,128)(2,1)} %bitcast.20, f32[2,1,2,96,1024]{4,3,0,2,1:T(8,128)} %copy-done.8, pred[]{:T(512)S(6)} %eq.87), kind=kLoop, calls=%fused_computation.90 | loop fusion | flops 786432 | bytes 3145729 | tf_op jit(solution)/shard_map/convert_element_type | solution.py:337
  49.4 1.7 %collective-permute-start.8 = (f16[2,96,1024]{2,1,0:T(8,128)(2,1)S(1)}, f16[2,96,1024]{2,1,0:T(8,128)(2,1)S(1)}, u32[]{:S(2)}, u32[]{:S(2)}) collective-permute-start(f16[2,96,1024]{2,1,0:T(8,128)(2,1)S(1)} %get-tuple-element.65), channel_id=1, source_target_pairs={{1,9},{5,13},{3,11},{7,15},{8,0},{12,4},{10,2},{14,6},{17,25},{21,... | collective-permute-start | bytes 1179656 | tf_op jit(solution)/shard_map/ppermute | solution.py:338
  51.1 2.2 %shard_map.92.sto_ref = f32[16,1024]{1,0:T(8,128)S(1)} custom-call(bf16[5,252,1024]{2,1,0:T(8,128)(2,1)S(1)} %copy-done.2), custom_call_target="tpu_custom_call" | custom-call | flops 7741440 | bytes 2580480 | tf_op jit(solution)/shard_map/pallas_call | solution.py:95
  58.2 1.3 %collective-permute-start.12 = (f16[2,80,1024]{2,1,0:T(8,128)(2,1)S(1)}, f16[2,80,1024]{2,1,0:T(8,128)(2,1)S(1)}, u32[]{:S(2)}, u32[]{:S(2)}) collective-permute-start(f16[2,80,1024]{2,1,0:T(8,128)(2,1)S(1)} %get-tuple-element.63), channel_id=1, source_target_pairs={{1,9},{5,13},{3,11},{7,15},{8,0},{12,4},{10,2},{14,6},{17,25},{21,... | collective-permute-start | bytes 983048 | tf_op jit(solution)/shard_map/ppermute | solution.py:338
  59.8 1.6 %collective-permute-start.14 = (f16[2,1,80,1024]{3,2,0,1:T(8,128)(2,1)S(1)}, f16[2,1,80,1024]{3,2,0,1:T(8,128)(2,1)S(1)}, u32[]{:S(2)}, u32[]{:S(2)}) collective-permute-start(f16[2,1,80,1024]{3,2,0,1:T(8,128)(2,1)S(1)} %fusion.46), channel_id=1, source_target_pairs={{0,4},{4,0},{8,12},{12,8},{16,20},{20,16},{24,28},{28,24},{1,5},{5... | collective-permute-start | bytes 983048 | tf_op jit(solution)/shard_map/ppermute | solution.py:289
  61.3 4.8 %collective-permute-done.8 = f16[2,96,1024]{2,1,0:T(8,128)(2,1)S(1)} collective-permute-done((f16[2,96,1024]{2,1,0:T(8,128)(2,1)S(1)}, f16[2,96,1024]{2,1,0:T(8,128)(2,1)S(1)}, u32[]{:S(2)}, u32[]{:S(2)}) %collective-permute-start.8) | collective-permute-done | bytes 393248 | tf_op jit(solution)/shard_map/ppermute | solution.py:338
  66.2 3.9 %collective-permute-start.11 = (f16[2,96,1024]{2,1,0:T(8,128)(2,1)S(1)}, f16[2,96,1024]{2,1,0:T(8,128)(2,1)S(1)}, u32[]{:S(2)}, u32[]{:S(2)}) collective-permute-start(f16[2,96,1024]{2,1,0:T(8,128)(2,1)S(1)} %fusion.39), channel_id=1, source_target_pairs={{0,16},{4,20},{9,25},{13,29},{18,2},{22,6},{27,11},{31,15}} | collective-permute-start | bytes 1179656 | tf_op jit(solution)/shard_map/ppermute | solution.py:348
  70.6 1.4 %collective-permute-start.16 = (f16[2,80,1024]{2,1,0:T(8,128)(2,1)S(1)}, f16[2,80,1024]{2,1,0:T(8,128)(2,1)S(1)}, u32[]{:S(2)}, u32[]{:S(2)}) collective-permute-start(f16[2,80,1024]{2,1,0:T(8,128)(2,1)S(1)} %get-tuple-element.61), channel_id=1, source_target_pairs={{1,9},{5,13},{3,11},{7,15},{8,0},{12,4},{10,2},{14,6},{17,25},{21,... | collective-permute-start | bytes 983048 | tf_op jit(solution)/shard_map/ppermute | solution.py:338
  73.7 5.5 %collective-permute-start.15 = (f16[2,80,1024]{2,1,0:T(8,128)(2,1)S(1)}, f16[2,80,1024]{2,1,0:T(8,128)(2,1)S(1)}, u32[]{:S(2)}, u32[]{:S(2)}) collective-permute-start(f16[2,80,1024]{2,1,0:T(8,128)(2,1)S(1)} %fusion.40), channel_id=1, source_target_pairs={{0,16},{4,20},{9,25},{13,29},{18,2},{22,6},{27,11},{31,15}} | collective-permute-start | bytes 983048 | tf_op jit(solution)/shard_map/ppermute | solution.py:348
  79.4 5.9 %collective-permute-done.16 = f16[2,80,1024]{2,1,0:T(8,128)(2,1)S(1)} collective-permute-done((f16[2,80,1024]{2,1,0:T(8,128)(2,1)S(1)}, f16[2,80,1024]{2,1,0:T(8,128)(2,1)S(1)}, u32[]{:S(2)}, u32[]{:S(2)}) %collective-permute-start.16) | collective-permute-done | bytes 327712 | tf_op jit(solution)/shard_map/ppermute | solution.py:338
  85.4 1.3 %collective-permute-start.17 = (f16[2,80,1024]{2,1,0:T(8,128)(2,1)S(1)}, f16[2,80,1024]{2,1,0:T(8,128)(2,1)S(1)}, u32[]{:S(2)}, u32[]{:S(2)}) collective-permute-start(f16[2,80,1024]{2,1,0:T(8,128)(2,1)S(1)} %fusion.41), channel_id=1, source_target_pairs={{0,16},{4,20},{9,25},{13,29},{18,2},{22,6},{27,11},{31,15}} | collective-permute-start | bytes 983048 | tf_op jit(solution)/shard_map/ppermute | solution.py:348
  87.3 4.0 %collective-permute-done.17 = f16[2,80,1024]{2,1,0:T(8,128)(2,1)S(1)} collective-permute-done((f16[2,80,1024]{2,1,0:T(8,128)(2,1)S(1)}, f16[2,80,1024]{2,1,0:T(8,128)(2,1)S(1)}, u32[]{:S(2)}, u32[]{:S(2)}) %collective-permute-start.17) | collective-permute-done | bytes 327712 | tf_op jit(solution)/shard_map/ppermute | solution.py:348
  92.4 2.1 %collective-permute-done.20 = f32[80,1024]{1,0:T(8,128)S(1)} collective-permute-done((f32[80,1024]{1,0:T(8,128)S(1)}, f32[80,1024]{1,0:T(8,128)S(1)}, u32[]{:S(2)}, u32[]{:S(2)}) %collective-permute-start.20) | collective-permute-done | bytes 327712 | tf_op jit(solution)/shard_map/ppermute | solution.py:286
  94.8 3.0 %shard_map.93 = (f32[252,1024]{1,0:T(8,128)S(1)}, f32[32,128]{1,0:T(8,128)S(1)}) custom-call(f32[256,1024]{1,0:T(8,128)S(1)} %maximum_add_fusion.lad_ref, f32[252,1024]{1,0:T(8,128)S(1)} %copy-done.4, f32[252,128]{1,0:T(8,128)S(1)} %broadcast_in_dim.70.occ_ref, f32[1,1024]{1,0:T(1,128)S(1)} %bitcast.130, bf16[5,252,1024]{2,1,0:T(8,128)(2,1)S(1)} %copy-done.3, ...), custom_call_target="tpu_custom_call" | custom-call | flops 5160960 | bytes 6193152 | tf_op jit(solution)/shard_map/pallas_call | solution.py:151
  97.8 11.9 %all_to_all.11 = f32[32,1,128]{2,1,0:T(1,128)S(1)} all-to-all(f32[32,1,128]{2,1,0:T(1,128)S(1)} %bitcast.131), channel_id=1, replica_groups=mesh['row'=8,'col'=4] {'row','col'}, dimensions={0} | all-to-all | bytes 32768 | tf_op jit(solution)/shard_map/all_to_all | solution.py:439
  109.6 2.7 %shard_map.94 = f32[252,1024]{1,0:T(8,128)} custom-call(f32[32,128]{1,0:T(8,128)S(1)} %bitcast.129, f32[252,1024]{1,0:T(8,128)S(1)} %get-tuple-element.56.raw_ref, bf16[5,252,1024]{2,1,0:T(8,128)(2,1)S(1)} %copy-done.3), custom_call_target="tpu_custom_call" | custom-call | tf_op jit(solution)/shard_map/pallas_call | solution.py:234
  (116 shorter events, 24.2 us)
Async XLA Ops:
  0.0 5.3 %copy-start.14 = (bf16[504,2048]{1,0:T(8,128)(2,1)S(1)}, bf16[504,2048]{1,0:T(8,128)(2,1)}, u32[]{:S(2)}) copy-start(bf16[504,2048]{1,0:T(8,128)(2,1)} %param.10) | copy-start | bytes 6193156
  1.4 4.2 %copy-start.23 = (pred[256]{0:T(512)(128)(4,1)S(1)}, pred[256]{0:T(512)(128)(4,1)}, u32[]{:S(2)}) copy-start(pred[256]{0:T(512)(128)(4,1)} %constant.66.clone.1) | copy-start | bytes 772
  2.3 14.1 %collective-permute-start.1 = (bf16[2048,1024]{1,0:T(8,128)(2,1)}, bf16[2048,1024]{1,0:T(8,128)(2,1)}, u32[]{:S(2)}, u32[]{:S(2)}) collective-permute-start(bf16[2048,1024]{1,0:T(8,128)(2,1)} %param.9), channel_id=1, source_target_pairs={{0,1},{1,0},{2,3},{3,2},{4,5},{5,4},{6,7},{7,6},{8,9},{9,8},{10,11... | collective-permute-start | bytes 12582920 | tf_op jit(solution)/shard_map/ppermute | solution.py:286
  2.8 25.6 %collective-permute-start.4 = (bf16[2,96,2048]{2,1,0:T(8,128)(2,1)}, bf16[2,96,2048]{2,1,0:T(8,128)(2,1)}, u32[]{:S(2)}, u32[]{:S(2)}) collective-permute-start(bf16[2,96,2048]{2,1,0:T(8,128)(2,1)} %pad_maximum_fusion.1), channel_id=1, source_target_pairs={{0,2},{1,3},{2,0},{3,1},{4,6},{5,7},{6,4},{7,5},{8,10},{9,11},{10,... | collective-permute-start | bytes 2359304 | tf_op jit(solution)/shard_map/ppermute | solution.py:286
  10.5 4.0 %copy-start.20 = (s32[2,1024]{1,0:T(2,128)S(1)}, s32[2,1024]{1,0:T(2,128)}, u32[]{:S(2)}) copy-start(s32[2,1024]{1,0:T(2,128)} %param.17) | copy-start | bytes 24580
  11.5 15.0 %collective-permute-start = (f16[1,1,256,1024]{3,2,1,0:T(8,128)(2,1)}, f16[1,1,256,1024]{3,2,1,0:T(8,128)(2,1)S(1)}, u32[]{:S(2)}, u32[]{:S(2)}) collective-permute-start(f16[1,1,256,1024]{3,2,1,0:T(8,128)(2,1)} %fusion.37), channel_id=1, source_target_pairs={{0,4},{4,0},{8,12},{12,8},{16,20},{20,16},{24,28},{28,24},{1,5},{5... | collective-permute-start | bytes 1572872 | tf_op jit(solution)/shard_map/ppermute | solution.py:289
  14.0 25.5 %collective-permute-start.7 = (bf16[2,80,2048]{2,1,0:T(8,128)(2,1)}, bf16[2,80,2048]{2,1,0:T(8,128)(2,1)S(1)}, u32[]{:S(2)}, u32[]{:S(2)}) collective-permute-start(bf16[2,80,2048]{2,1,0:T(8,128)(2,1)} %pad_maximum_fusion.3), channel_id=1, source_target_pairs={{0,2},{1,3},{2,0},{3,1},{4,6},{5,7},{6,4},{7,5},{8,10},{9,11},{10,... | collective-permute-start | bytes 1966088 | tf_op jit(solution)/shard_map/ppermute | solution.py:286
  21.7 18.8 %copy-start = (bf16[2048,1024]{1,0:T(8,128)(2,1)}, bf16[2048,1024]{1,0:T(8,128)(2,1)S(1)}, u32[]{:S(2)}) copy-start(bf16[2048,1024]{1,0:T(8,128)(2,1)S(1)} %get-tuple-element.37) | copy-start | bytes 12582916
  21.7 4.8 %copy-start.17 = (f32[1,1,2,256,1024]{4,3,2,1,0:T(8,128)S(1)}, f32[1,1,2,256,1024]{4,3,2,1,0:T(8,128)}, u32[]{:S(2)}) copy-start(f32[1,1,2,256,1024]{4,3,2,1,0:T(8,128)} %copy-done.16) | copy-start | bytes 6291460
  21.9 15.2 %collective-permute-start.3 = (f16[1,1,256,1024]{3,2,1,0:T(8,128)(2,1)S(1)}, f16[1,1,256,1024]{3,2,1,0:T(8,128)(2,1)S(1)}, u32[]{:S(2)}, u32[]{:S(2)}) collective-permute-start(f16[1,1,256,1024]{3,2,1,0:T(8,128)(2,1)S(1)} %fusion.38), channel_id=1, source_target_pairs={{0,4},{4,0},{8,12},{12,8},{16,20},{20,16},{24,28},{28,24},{1,5},{5... | collective-permute-start | bytes 1572872 | tf_op jit(solution)/shard_map/ppermute | solution.py:289
  26.8 11.8 %copy-start.12 = (f32[1,256,1024]{2,1,0:T(8,128)}, f32[1,256,1024]{2,1,0:T(8,128)S(1)}, u32[]{:S(2)}) copy-start(f32[1,256,1024]{2,1,0:T(8,128)S(1)} %get-tuple-element.70) | copy-start | bytes 3145732
  26.8 11.7 %collective-permute-start.2 = (f16[1,256,1024]{2,1,0:T(8,128)(2,1)S(1)}, f16[1,256,1024]{2,1,0:T(8,128)(2,1)S(1)}, u32[]{:S(2)}, u32[]{:S(2)}) collective-permute-start(f16[1,256,1024]{2,1,0:T(8,128)(2,1)S(1)} %get-tuple-element.69), channel_id=1, source_target_pairs={{1,9},{5,13},{3,11},{7,15},{8,0},{12,4},{10,2},{14,6},{17,25},{21,... | collective-permute-start | bytes 1572872 | tf_op jit(solution)/shard_map/ppermute | solution.py:338
  35.6 12.0 %collective-permute-start.6 = (f16[2,1,96,1024]{3,2,0,1:T(8,128)(2,1)}, f16[2,1,96,1024]{3,2,0,1:T(8,128)(2,1)}, u32[]{:S(2)}, u32[]{:S(2)}) collective-permute-start(f16[2,1,96,1024]{3,2,0,1:T(8,128)(2,1)} %fusion.42), channel_id=1, source_target_pairs={{0,4},{4,0},{8,12},{12,8},{16,20},{20,16},{24,28},{28,24},{1,5},{5... | collective-permute-start | bytes 1179656 | tf_op jit(solution)/shard_map/ppermute | solution.py:289
  37.1 18.0 %collective-permute-start.9 = (bf16[2,80,2048]{2,1,0:T(8,128)(2,1)}, bf16[2,80,2048]{2,1,0:T(8,128)(2,1)S(1)}, u32[]{:S(2)}, u32[]{:S(2)}) collective-permute-start(bf16[2,80,2048]{2,1,0:T(8,128)(2,1)} %pad_maximum_fusion.4), channel_id=1, source_target_pairs={{0,2},{1,3},{2,0},{3,1},{4,6},{5,7},{6,4},{7,5},{8,10},{9,11},{10,... | collective-permute-start | bytes 1966088 | tf_op jit(solution)/shard_map/ppermute | solution.py:286
  42.6 8.5 %copy-start.2 = (bf16[5,252,1024]{2,1,0:T(8,128)(2,1)S(1)}, bf16[5,252,1024]{2,1,0:T(8,128)(2,1)}, u32[]{:S(2)}) copy-start(bf16[5,252,1024]{2,1,0:T(8,128)(2,1)} %err_ref.2) | copy-start | bytes 7741444
  43.4 10.5 %collective-permute-start.10 = (f16[2,1,80,1024]{3,2,0,1:T(8,128)(2,1)}, f16[2,1,80,1024]{3,2,0,1:T(8,128)(2,1)}, u32[]{:S(2)}, u32[]{:S(2)}) collective-permute-start(f16[2,1,80,1024]{3,2,0,1:T(8,128)(2,1)} %fusion.45), channel_id=1, source_target_pairs={{0,4},{4,0},{8,12},{12,8},{16,20},{20,16},{24,28},{28,24},{1,5},{5... | collective-permute-start | bytes 983048 | tf_op jit(solution)/shard_map/ppermute | solution.py:289
  45.0 27.0 %collective-permute-start.13 = (f16[1,256,1024]{2,1,0:T(8,128)(2,1)}, f16[1,256,1024]{2,1,0:T(8,128)(2,1)S(1)}, u32[]{:S(2)}, u32[]{:S(2)}) collective-permute-start(f16[1,256,1024]{2,1,0:T(8,128)(2,1)} %get-tuple-element.67), channel_id=1, source_target_pairs={{1,9},{5,13},{3,11},{7,15},{8,0},{12,4},{10,2},{14,6},{17,25},{21,... | collective-permute-start | bytes 1572872 | tf_op jit(solution)/shard_map/ppermute | solution.py:338
  46.3 23.8 %collective-permute-start.5 = (f16[1,256,1024]{2,1,0:T(8,128)(2,1)}, f16[1,256,1024]{2,1,0:T(8,128)(2,1)S(1)}, u32[]{:S(2)}, u32[]{:S(2)}) collective-permute-start(f16[1,256,1024]{2,1,0:T(8,128)(2,1)} %fusion.35), channel_id=1, source_target_pairs={{2,18},{6,22},{11,27},{15,31},{16,0},{20,4},{25,9},{29,13}} | collective-permute-start | bytes 1572872 | tf_op jit(solution)/shard_map/ppermute | solution.py:348
  47.6 6.4 %copy-start.10 = (f32[2,1,2,80,1024]{4,3,0,2,1:T(8,128)S(1)}, f32[2,1,2,80,1024]{4,3,0,2,1:T(8,128)}, u32[]{:S(2)}) copy-start(f32[2,1,2,80,1024]{4,3,0,2,1:T(8,128)} %copy-done.9) | copy-start | bytes 3932164
  49.4 5.7 %copy-start.7 = (bf16[2048,1024]{1,0:T(8,128)(2,1)S(1)}, bf16[2048,1024]{1,0:T(8,128)(2,1)}, u32[]{:S(2)}) copy-start(bf16[2048,1024]{1,0:T(8,128)(2,1)} %param.9) | copy-start | bytes 12582916
  49.4 16.7 %collective-permute-start.8 = (f16[2,96,1024]{2,1,0:T(8,128)(2,1)S(1)}, f16[2,96,1024]{2,1,0:T(8,128)(2,1)S(1)}, u32[]{:S(2)}, u32[]{:S(2)}) collective-permute-start(f16[2,96,1024]{2,1,0:T(8,128)(2,1)S(1)} %get-tuple-element.65), channel_id=1, source_target_pairs={{1,9},{5,13},{3,11},{7,15},{8,0},{12,4},{10,2},{14,6},{17,25},{21,... | collective-permute-start | bytes 1179656 | tf_op jit(solution)/shard_map/ppermute | solution.py:338
  58.2 15.3 %collective-permute-start.12 = (f16[2,80,1024]{2,1,0:T(8,128)(2,1)S(1)}, f16[2,80,1024]{2,1,0:T(8,128)(2,1)S(1)}, u32[]{:S(2)}, u32[]{:S(2)}) collective-permute-start(f16[2,80,1024]{2,1,0:T(8,128)(2,1)S(1)} %get-tuple-element.63), channel_id=1, source_target_pairs={{1,9},{5,13},{3,11},{7,15},{8,0},{12,4},{10,2},{14,6},{17,25},{21,... | collective-permute-start | bytes 983048 | tf_op jit(solution)/shard_map/ppermute | solution.py:338
  59.6 10.5 %copy-start.13 = (f32[1,256,1024]{2,1,0:T(8,128)S(1)}, f32[1,256,1024]{2,1,0:T(8,128)}, u32[]{:S(2)}) copy-start(f32[1,256,1024]{2,1,0:T(8,128)} %copy-done.12) | copy-start | bytes 3145732
  59.6 10.5 %copy-start.19 = (f16[1,256,1024]{2,1,0:T(8,128)(2,1)S(1)}, f16[1,256,1024]{2,1,0:T(8,128)(2,1)}, u32[]{:S(2)}) copy-start(f16[1,256,1024]{2,1,0:T(8,128)(2,1)} %copy-done.18) | copy-start | bytes 1572868
  59.8 10.7 %collective-permute-start.14 = (f16[2,1,80,1024]{3,2,0,1:T(8,128)(2,1)S(1)}, f16[2,1,80,1024]{3,2,0,1:T(8,128)(2,1)S(1)}, u32[]{:S(2)}, u32[]{:S(2)}) collective-permute-start(f16[2,1,80,1024]{3,2,0,1:T(8,128)(2,1)S(1)} %fusion.46), channel_id=1, source_target_pairs={{0,4},{4,0},{8,12},{12,8},{16,20},{20,16},{24,28},{28,24},{1,5},{5... | collective-permute-start | bytes 983048 | tf_op jit(solution)/shard_map/ppermute | solution.py:289
  66.2 12.9 %collective-permute-start.11 = (f16[2,96,1024]{2,1,0:T(8,128)(2,1)S(1)}, f16[2,96,1024]{2,1,0:T(8,128)(2,1)S(1)}, u32[]{:S(2)}, u32[]{:S(2)}) collective-permute-start(f16[2,96,1024]{2,1,0:T(8,128)(2,1)S(1)} %fusion.39), channel_id=1, source_target_pairs={{0,16},{4,20},{9,25},{13,29},{18,2},{22,6},{27,11},{31,15}} | collective-permute-start | bytes 1179656 | tf_op jit(solution)/shard_map/ppermute | solution.py:348
  70.6 14.7 %collective-permute-start.16 = (f16[2,80,1024]{2,1,0:T(8,128)(2,1)S(1)}, f16[2,80,1024]{2,1,0:T(8,128)(2,1)S(1)}, u32[]{:S(2)}, u32[]{:S(2)}) collective-permute-start(f16[2,80,1024]{2,1,0:T(8,128)(2,1)S(1)} %get-tuple-element.61), channel_id=1, source_target_pairs={{1,9},{5,13},{3,11},{7,15},{8,0},{12,4},{10,2},{14,6},{17,25},{21,... | collective-permute-start | bytes 983048 | tf_op jit(solution)/shard_map/ppermute | solution.py:338
  72.2 14.7 %collective-permute-start.18 = (f16[1,256,1024]{2,1,0:T(8,128)(2,1)S(1)}, f16[1,256,1024]{2,1,0:T(8,128)(2,1)S(1)}, u32[]{:S(2)}, u32[]{:S(2)}) collective-permute-start(f16[1,256,1024]{2,1,0:T(8,128)(2,1)S(1)} %fusion.36), channel_id=1, source_target_pairs={{2,18},{6,22},{11,27},{15,31},{16,0},{20,4},{25,9},{29,13}} | collective-permute-start | bytes 1572872 | tf_op jit(solution)/shard_map/ppermute | solution.py:348
  73.7 13.1 %collective-permute-start.15 = (f16[2,80,1024]{2,1,0:T(8,128)(2,1)S(1)}, f16[2,80,1024]{2,1,0:T(8,128)(2,1)S(1)}, u32[]{:S(2)}, u32[]{:S(2)}) collective-permute-start(f16[2,80,1024]{2,1,0:T(8,128)(2,1)S(1)} %fusion.40), channel_id=1, source_target_pairs={{0,16},{4,20},{9,25},{13,29},{18,2},{22,6},{27,11},{31,15}} | collective-permute-start | bytes 983048 | tf_op jit(solution)/shard_map/ppermute | solution.py:348
  85.4 5.9 %collective-permute-start.17 = (f16[2,80,1024]{2,1,0:T(8,128)(2,1)S(1)}, f16[2,80,1024]{2,1,0:T(8,128)(2,1)S(1)}, u32[]{:S(2)}, u32[]{:S(2)}) collective-permute-start(f16[2,80,1024]{2,1,0:T(8,128)(2,1)S(1)} %fusion.41), channel_id=1, source_target_pairs={{0,16},{4,20},{9,25},{13,29},{18,2},{22,6},{27,11},{31,15}} | collective-permute-start | bytes 983048 | tf_op jit(solution)/shard_map/ppermute | solution.py:348
  91.9 2.7 %collective-permute-start.19 = (f32[176,1024]{1,0:T(8,128)S(1)}, f32[176,1024]{1,0:T(8,128)S(1)}, u32[]{:S(2)}, u32[]{:S(2)}) collective-permute-start(f32[176,1024]{1,0:T(8,128)S(1)} %pad_maximum_fusion.2), channel_id=1, source_target_pairs={{0,1},{1,0},{2,3},{3,2},{4,5},{5,4},{6,7},{7,6},{8,9},{9,8},{10,11... | collective-permute-start | bytes 2162696 | tf_op jit(solution)/shard_map/ppermute | solution.py:286
  91.9 2.6 %collective-permute-start.20 = (f32[80,1024]{1,0:T(8,128)S(1)}, f32[80,1024]{1,0:T(8,128)S(1)}, u32[]{:S(2)}, u32[]{:S(2)}) collective-permute-start(f32[80,1024]{1,0:T(8,128)S(1)} %get-tuple-element.81), channel_id=1, source_target_pairs={{0,1},{1,0},{2,3},{3,2},{4,5},{5,4},{6,7},{7,6},{8,9},{9,8},{10,11... | collective-permute-start | bytes 983048 | tf_op jit(solution)/shard_map/ppermute | solution.py:286
  (14 other events, 32.3 us)

commit v5 on v4

--- a/solution.py
+++ b/solution.py
@@ -261,13 +261,8 @@
 def order_of(last):
     steps = ["p0", "n2", "p1", "f0"]
     for n in range(3, last + 1):
-        if n > 3:
-            steps.append(f"p{n - 1}")
-        steps.append(f"n{n}")
-        if n == 3:
-            steps += ["p2", "s0"]
-        else:
-            steps.append(f"f{n - 2}")
+        steps += [f"n{n}", f"p{n - 1}"]
+        steps.append("s0" if n == 3 else f"f{n - 2}")
     if last < 3:
         steps.append("s0")
     steps += [f"p{last}", "f1"]

time: 113 us -> 109 us (0.965)
  waiting for transfers between devices: 20.5 us -> 26.9 us
  other arithmetic: 15.6 us -> 10.1 us
  local copies, waits for them, and re-layouts: 8.22 us -> 4 us
  starting transfers between devices: 32.1 us -> 30.5 us
    unnamed x50 -> x28, local copies, waits for them, and re-layouts: 6.26 us -> 2.05 us
    ppermute x6, waiting for transfers between devices: 2.16 us -> 5.6 us  [send_col(): return lax.ppermute(x, 'col', [(i, i ^ m) for i in range(col_n)])]
    convert_element_type x5, other arithmetic: 4.82 us -> 2.39 us  [pair_begin(): send = part.astype(wire)]
    ppermute x5, waiting for transfers between devices: 3.59 us -> 5.38 us  [send_row(): return lax.ppermute(x, 'row', [(i, i ^ m) for i in range(row_n)])]
    ppermute x5, waiting for transfers between devices: 10.7 us -> 12.2 us  [pair_begin(): return (part, lax.ppermute(send, ('row', 'col'), even_links), send)]
    convert_element_type x5, other arithmetic: 3.06 us -> 1.63 us  [near_begin(): send = jnp.where(mine, halves[:, :, 1], halves[:, :, 0]).astype(wire)]
  transfers between devices with their start and end apart: 21 -> 21, of which waited for: 6 -> 9; matrix products, arithmetic and copies ran while one was open for 22% -> 18% of each run, Pallas kernels for 7% -> 7%
where the time goes in v5:
time: 109 us; the launch traced here: 108 us
  starting transfers between devices  30.5 us (28%)
  waiting for transfers between devices  26.9 us (25%)
  Pallas kernels  13 us (12%)
  blocking collectives  12.6 us (12%)
  other arithmetic  10.1 us (9%)
  matrix products  10.1 us (9%)
  local copies, waits for them, and re-layouts  4 us (4%)
    all_to_all x1, blocking collectives, on_device(): gathered = lax.all_to_all(shares, ('row', 'col'), 0, 0, tiled=True)  12.6 us
    ppermute x5, starting transfers between devices, far_begin(): taken.append(lax.ppermute(data, ('row', 'col'), links))  12.6 us
    ppermute x5, waiting for transfers between devices, pair_begin(): return (part, lax.ppermute(send, ('row', 'col'), even_links), send)  12.2 us
    dot_general x7, matrix products, multiply(): out = jnp.dot(piece.reshape(-1, depth), right, preferred_element_type=f32)  10.1 us
    ppermute x5, starting transfers between devices, send_row(): return lax.ppermute(x, 'row', [(i, i ^ m) for i in range(row_n)])  6.68 us
    ppermute x5, starting transfers between devices, pair_begin(): return (part, lax.ppermute(send, ('row', 'col'), even_links), send)  6.64 us
    ppermute x6, waiting for transfers between devices, send_col(): return lax.ppermute(x, 'col', [(i, i ^ m) for i in range(col_n)])  5.6 us
    ppermute x5, waiting for transfers between devices, send_row(): return lax.ppermute(x, 'row', [(i, i ^ m) for i in range(row_n)])  5.38 us
  transfers between devices with their start and end apart: 21, of which 9 were waited for; matrix products, arithmetic and copies ran while one was open for 18% of the time, Pallas kernels for 7%

profile of v5, /device:TPU:0, one launch (start us, length us, event | category | flops | bytes accessed | tf_op | source)
XLA Modules:
  0.0 108.0 jit_solution(2205017371090580327)
XLA Ops:
  0.0 1.4 %slice_bitcast_fusion.1 = (bf16[1,96,2048]{2,1,0:T(8,128)(2,1)S(1)}, bf16[1,96,2048]{2,1,0:T(8,128)(2,1)S(1)}) fusion(bf16[504,2048]{1,0:T(8,128)(2,1)} %param.10), kind=kLoop, calls=%fused_computation.69 | loop fusion | bytes 1572864 | tf_op jit(solution)/shard_map/stack | solution.py:356
  2.4 3.0 %collective-permute-start.4 = (bf16[2,96,2048]{2,1,0:T(8,128)(2,1)}, bf16[2,96,2048]{2,1,0:T(8,128)(2,1)}, u32[]{:S(2)}, u32[]{:S(2)}) collective-permute-start(bf16[2,96,2048]{2,1,0:T(8,128)(2,1)} %pad_maximum_fusion.1), channel_id=1, source_target_pairs={{0,2},{1,3},{2,0},{3,1},{4,6},{5,7},{6,4},{7,5},{8,10},{9,11},{10,... | collective-permute-start | bytes 2359304 | tf_op jit(solution)/shard_map/ppermute | solution.py:281
  6.1 2.0 %copy-done.3 = bf16[2048,1024]{1,0:T(8,128)(2,1)S(1)} copy-done((bf16[2048,1024]{1,0:T(8,128)(2,1)S(1)}, bf16[2048,1024]{1,0:T(8,128)(2,1)}, u32[]{:S(2)}) %copy-start.3) | copy-done | bytes 4194328
  8.1 2.4 %fusion.14 = f32[1,1,2,256,1024]{4,3,2,1,0:T(8,128)S(1)} fusion(bf16[2,256,2048]{2,1,0:T(8,128)(2,1)S(1)} %pad_maximum_fusion, bf16[2048,1024]{1,0:T(8,128)(2,1)S(1)} %copy-done.3), kind=kOutput, calls=%fused_computation.19 | convolution fusion | flops 2147483648 | bytes 8388608 | tf_op jit(solution)/shard_map/dot_general | solution.py:310
  11.6 1.5 %collective-permute-start = (f16[1,1,256,1024]{3,2,1,0:T(8,128)(2,1)}, f16[1,1,256,1024]{3,2,1,0:T(8,128)(2,1)}, u32[]{:S(2)}, u32[]{:S(2)}) collective-permute-start(f16[1,1,256,1024]{3,2,1,0:T(8,128)(2,1)} %fusion.37), channel_id=1, source_target_pairs={{0,4},{4,0},{8,12},{12,8},{16,20},{20,16},{24,28},{28,24},{1,5},{5... | collective-permute-start | bytes 1572872 | tf_op jit(solution)/shard_map/ppermute | solution.py:284
  15.8 5.2 %shard_map.91 = (f32[512,1024]{1,0:T(8,128)S(1)}, bf16[2048,1024]{1,0:T(8,128)(2,1)S(1)}) custom-call(bf16[512,2048]{1,0:T(8,128)(2,1)S(1)} %bitcast.128, bf16[2048,1024]{1,0:T(8,128)(2,1)} %collective-permute-done.1.right_ref), custom_call_target="tpu_custom_call" | custom-call | flops 2147483648 | bytes 6291456 | tf_op jit(solution)/shard_map/pallas_call | solution.py:57
  21.3 1.5 %collective-permute-start.3 = (f16[1,1,256,1024]{3,2,1,0:T(8,128)(2,1)S(1)}, f16[1,1,256,1024]{3,2,1,0:T(8,128)(2,1)S(1)}, u32[]{:S(2)}, u32[]{:S(2)}) collective-permute-start(f16[1,1,256,1024]{3,2,1,0:T(8,128)(2,1)S(1)} %fusion.38), channel_id=1, source_target_pairs={{0,4},{4,0},{8,12},{12,8},{16,20},{20,16},{24,28},{28,24},{1,5},{5... | collective-permute-start | bytes 1572872 | tf_op jit(solution)/shard_map/ppermute | solution.py:284
  22.7 3.9 %collective-permute-done = f16[1,1,256,1024]{3,2,1,0:T(8,128)(2,1)} collective-permute-done((f16[1,1,256,1024]{3,2,1,0:T(8,128)(2,1)}, f16[1,1,256,1024]{3,2,1,0:T(8,128)(2,1)}, u32[]{:S(2)}, u32[]{:S(2)}) %collective-permute-start) | collective-permute-done | bytes 524320 | tf_op jit(solution)/shard_map/ppermute | solution.py:284
  26.6 1.5 %fusion.55 = (f16[1,256,1024]{2,1,0:T(8,128)(2,1)S(1)}, f32[1,256,1024]{2,1,0:T(8,128)S(1)}) fusion(f16[1,256,1024]{2,1,0:T(8,128)(2,1)} %bitcast.8, f32[1,1,2,256,1024]{4,3,2,1,0:T(8,128)S(1)} %copy-done.8, pred[]{:T(512)S(6)} %eq.87), kind=kLoop, calls=%fused_computation.92 | loop fusion | flops 1048576 | bytes 4194305 | tf_op jit(solution)/shard_map/convert_element_type | solution.py:332
  28.2 1.3 %collective-permute-start.2 = (f16[1,256,1024]{2,1,0:T(8,128)(2,1)S(1)}, f16[1,256,1024]{2,1,0:T(8,128)(2,1)S(1)}, u32[]{:S(2)}, u32[]{:S(2)}) collective-permute-start(f16[1,256,1024]{2,1,0:T(8,128)(2,1)S(1)} %get-tuple-element.69), channel_id=1, source_target_pairs={{1,9},{5,13},{3,11},{7,15},{8,0},{12,4},{10,2},{14,6},{17,25},{21,... | collective-permute-start | bytes 1572872 | tf_op jit(solution)/shard_map/ppermute | solution.py:333
  29.5 2.1 %fusion.17 = f32[1,2,96,1024]{3,2,0,1:T(8,128)S(1)} fusion(bf16[2,96,2048]{2,1,0:T(8,128)(2,1)} %collective-permute-done.4, bf16[2048,1024]{1,0:T(8,128)(2,1)S(1)} %copy-done.4), kind=kOutput, calls=%fused_computation.23 | convolution fusion | flops 805306368 | bytes 5767168 | tf_op jit(solution)/shard_map/dot_general | solution.py:310
  31.6 2.1 %fusion.20 = f32[1,2,96,1024]{3,2,0,1:T(8,128)S(1)} fusion(bf16[2,96,2048]{2,1,0:T(8,128)(2,1)} %collective-permute-done.4, bf16[2048,1024]{1,0:T(8,128)(2,1)S(1)} %get-tuple-element.37), kind=kOutput, calls=%fused_computation.24 | convolution fusion | flops 805306368 | bytes 5767168 | tf_op jit(solution)/shard_map/dot_general | solution.py:310
  34.0 1.6 %collective-permute-start.6 = (f16[2,1,96,1024]{3,2,0,1:T(8,128)(2,1)S(1)}, f16[2,1,96,1024]{3,2,0,1:T(8,128)(2,1)S(1)}, u32[]{:S(2)}, u32[]{:S(2)}) collective-permute-start(f16[2,1,96,1024]{3,2,0,1:T(8,128)(2,1)S(1)} %fusion.42), channel_id=1, source_target_pairs={{0,4},{4,0},{8,12},{12,8},{16,20},{20,16},{24,28},{28,24},{1,5},{5... | collective-permute-start | bytes 1179656 | tf_op jit(solution)/shard_map/ppermute | solution.py:284
  37.7 1.5 %collective-permute-done.2 = f16[1,256,1024]{2,1,0:T(8,128)(2,1)S(1)} collective-permute-done((f16[1,256,1024]{2,1,0:T(8,128)(2,1)S(1)}, f16[1,256,1024]{2,1,0:T(8,128)(2,1)S(1)}, u32[]{:S(2)}, u32[]{:S(2)}) %collective-permute-start.2) | collective-permute-done | bytes 524320 | tf_op jit(solution)/shard_map/ppermute | solution.py:333
  41.2 1.3 %collective-permute-start.13 = (f16[1,256,1024]{2,1,0:T(8,128)(2,1)S(1)}, f16[1,256,1024]{2,1,0:T(8,128)(2,1)S(1)}, u32[]{:S(2)}, u32[]{:S(2)}) collective-permute-start(f16[1,256,1024]{2,1,0:T(8,128)(2,1)S(1)} %get-tuple-element.67), channel_id=1, source_target_pairs={{1,9},{5,13},{3,11},{7,15},{8,0},{12,4},{10,2},{14,6},{17,25},{21,... | collective-permute-start | bytes 1572872 | tf_op jit(solution)/shard_map/ppermute | solution.py:333
  42.5 1.3 %collective-permute-start.5 = (f16[1,256,1024]{2,1,0:T(8,128)(2,1)S(1)}, f16[1,256,1024]{2,1,0:T(8,128)(2,1)S(1)}, u32[]{:S(2)}, u32[]{:S(2)}) collective-permute-start(f16[1,256,1024]{2,1,0:T(8,128)(2,1)S(1)} %fusion.35), channel_id=1, source_target_pairs={{2,18},{6,22},{11,27},{15,31},{16,0},{20,4},{25,9},{29,13}} | collective-permute-start | bytes 1572872 | tf_op jit(solution)/shard_map/ppermute | solution.py:343
  44.0 1.6 %collective-permute-start.9 = (f16[2,1,80,1024]{3,2,0,1:T(8,128)(2,1)S(1)}, f16[2,1,80,1024]{3,2,0,1:T(8,128)(2,1)S(1)}, u32[]{:S(2)}, u32[]{:S(2)}) collective-permute-start(f16[2,1,80,1024]{3,2,0,1:T(8,128)(2,1)S(1)} %fusion.45), channel_id=1, source_target_pairs={{0,4},{4,0},{8,12},{12,8},{16,20},{20,16},{24,28},{28,24},{1,5},{5... | collective-permute-start | bytes 983048 | tf_op jit(solution)/shard_map/ppermute | solution.py:284
  46.0 1.5 %collective-permute-start.8 = (f16[2,96,1024]{2,1,0:T(8,128)(2,1)S(1)}, f16[2,96,1024]{2,1,0:T(8,128)(2,1)S(1)}, u32[]{:S(2)}, u32[]{:S(2)}) collective-permute-start(f16[2,96,1024]{2,1,0:T(8,128)(2,1)S(1)} %get-tuple-element.65), channel_id=1, source_target_pairs={{1,9},{5,13},{3,11},{7,15},{8,0},{12,4},{10,2},{14,6},{17,25},{21,... | collective-permute-start | bytes 1179656 | tf_op jit(solution)/shard_map/ppermute | solution.py:333
  47.5 2.2 %shard_map.92.sto_ref = f32[16,1024]{1,0:T(8,128)S(1)} custom-call(bf16[5,252,1024]{2,1,0:T(8,128)(2,1)S(1)} %copy-done), custom_call_target="tpu_custom_call" | custom-call | flops 7741440 | bytes 2580480 | tf_op jit(solution)/shard_map/pallas_call | solution.py:95
  49.7 3.4 %collective-permute-done.10 = bf16[2,80,2048]{2,1,0:T(8,128)(2,1)S(1)} collective-permute-done((bf16[2,80,2048]{2,1,0:T(8,128)(2,1)S(1)}, bf16[2,80,2048]{2,1,0:T(8,128)(2,1)S(1)}, u32[]{:S(2)}, u32[]{:S(2)}) %collective-permute-start.10) | collective-permute-done | bytes 655392 | tf_op jit(solution)/shard_map/ppermute | solution.py:281
  55.9 1.3 %collective-permute-start.12 = (f16[2,80,1024]{2,1,0:T(8,128)(2,1)S(1)}, f16[2,80,1024]{2,1,0:T(8,128)(2,1)S(1)}, u32[]{:S(2)}, u32[]{:S(2)}) collective-permute-start(f16[2,80,1024]{2,1,0:T(8,128)(2,1)S(1)} %get-tuple-element.63), channel_id=1, source_target_pairs={{1,9},{5,13},{3,11},{7,15},{8,0},{12,4},{10,2},{14,6},{17,25},{21,... | collective-permute-start | bytes 983048 | tf_op jit(solution)/shard_map/ppermute | solution.py:333
  57.2 4.8 %collective-permute-done.8 = f16[2,96,1024]{2,1,0:T(8,128)(2,1)S(1)} collective-permute-done((f16[2,96,1024]{2,1,0:T(8,128)(2,1)S(1)}, f16[2,96,1024]{2,1,0:T(8,128)(2,1)S(1)}, u32[]{:S(2)}, u32[]{:S(2)}) %collective-permute-start.8) | collective-permute-done | bytes 393248 | tf_op jit(solution)/shard_map/ppermute | solution.py:333
  62.2 3.2 %collective-permute-start.11 = (f16[2,96,1024]{2,1,0:T(8,128)(2,1)S(1)}, f16[2,96,1024]{2,1,0:T(8,128)(2,1)S(1)}, u32[]{:S(2)}, u32[]{:S(2)}) collective-permute-start(f16[2,96,1024]{2,1,0:T(8,128)(2,1)S(1)} %fusion.39), channel_id=1, source_target_pairs={{0,16},{4,20},{9,25},{13,29},{18,2},{22,6},{27,11},{31,15}} | collective-permute-start | bytes 1179656 | tf_op jit(solution)/shard_map/ppermute | solution.py:343
  65.6 1.3 %collective-permute-start.16 = (f16[2,80,1024]{2,1,0:T(8,128)(2,1)S(1)}, f16[2,80,1024]{2,1,0:T(8,128)(2,1)S(1)}, u32[]{:S(2)}, u32[]{:S(2)}) collective-permute-start(f16[2,80,1024]{2,1,0:T(8,128)(2,1)S(1)} %get-tuple-element.61), channel_id=1, source_target_pairs={{1,9},{5,13},{3,11},{7,15},{8,0},{12,4},{10,2},{14,6},{17,25},{21,... | collective-permute-start | bytes 983048 | tf_op jit(solution)/shard_map/ppermute | solution.py:333
  68.9 5.5 %collective-permute-start.15 = (f16[2,80,1024]{2,1,0:T(8,128)(2,1)S(1)}, f16[2,80,1024]{2,1,0:T(8,128)(2,1)S(1)}, u32[]{:S(2)}, u32[]{:S(2)}) collective-permute-start(f16[2,80,1024]{2,1,0:T(8,128)(2,1)S(1)} %fusion.40), channel_id=1, source_target_pairs={{0,16},{4,20},{9,25},{13,29},{18,2},{22,6},{27,11},{31,15}} | collective-permute-start | bytes 983048 | tf_op jit(solution)/shard_map/ppermute | solution.py:343
  74.4 5.8 %collective-permute-done.16 = f16[2,80,1024]{2,1,0:T(8,128)(2,1)S(1)} collective-permute-done((f16[2,80,1024]{2,1,0:T(8,128)(2,1)S(1)}, f16[2,80,1024]{2,1,0:T(8,128)(2,1)S(1)}, u32[]{:S(2)}, u32[]{:S(2)}) %collective-permute-start.16) | collective-permute-done | bytes 327712 | tf_op jit(solution)/shard_map/ppermute | solution.py:333
  80.3 1.3 %collective-permute-start.17 = (f16[2,80,1024]{2,1,0:T(8,128)(2,1)S(1)}, f16[2,80,1024]{2,1,0:T(8,128)(2,1)S(1)}, u32[]{:S(2)}, u32[]{:S(2)}) collective-permute-start(f16[2,80,1024]{2,1,0:T(8,128)(2,1)S(1)} %fusion.41), channel_id=1, source_target_pairs={{0,16},{4,20},{9,25},{13,29},{18,2},{22,6},{27,11},{31,15}} | collective-permute-start | bytes 983048 | tf_op jit(solution)/shard_map/ppermute | solution.py:343
  82.5 3.8 %collective-permute-done.17 = f16[2,80,1024]{2,1,0:T(8,128)(2,1)S(1)} collective-permute-done((f16[2,80,1024]{2,1,0:T(8,128)(2,1)S(1)}, f16[2,80,1024]{2,1,0:T(8,128)(2,1)S(1)}, u32[]{:S(2)}, u32[]{:S(2)}) %collective-permute-start.17) | collective-permute-done | bytes 327712 | tf_op jit(solution)/shard_map/ppermute | solution.py:343
  87.3 2.1 %collective-permute-done.20 = f32[80,1024]{1,0:T(8,128)S(1)} collective-permute-done((f32[80,1024]{1,0:T(8,128)S(1)}, f32[80,1024]{1,0:T(8,128)S(1)}, u32[]{:S(2)}, u32[]{:S(2)}) %collective-permute-start.20) | collective-permute-done | bytes 327712 | tf_op jit(solution)/shard_map/ppermute | solution.py:281
  89.6 3.0 %shard_map.93 = (f32[252,1024]{1,0:T(8,128)S(1)}, f32[32,128]{1,0:T(8,128)S(1)}) custom-call(f32[256,1024]{1,0:T(8,128)S(1)} %maximum_add_fusion.lad_ref, f32[252,1024]{1,0:T(8,128)S(1)} %copy-done.2, f32[252,128]{1,0:T(8,128)S(1)} %broadcast_in_dim.70.occ_ref, f32[1,1024]{1,0:T(1,128)S(1)} %bitcast.130, bf16[5,252,1024]{2,1,0:T(8,128)(2,1)S(1)} %copy-done.1, ...), custom_call_target="tpu_custom_call" | custom-call | flops 5160960 | bytes 6193152 | tf_op jit(solution)/shard_map/pallas_call | solution.py:151
  92.6 12.6 %all_to_all.11 = f32[32,1,128]{2,1,0:T(1,128)S(1)} all-to-all(f32[32,1,128]{2,1,0:T(1,128)S(1)} %bitcast.131), channel_id=1, replica_groups=mesh['row'=8,'col'=4] {'row','col'}, dimensions={0} | all-to-all | bytes 32768 | tf_op jit(solution)/shard_map/all_to_all | solution.py:434
  105.2 2.7 %shard_map.94 = f32[252,1024]{1,0:T(8,128)} custom-call(f32[32,128]{1,0:T(8,128)S(1)} %bitcast.129, f32[252,1024]{1,0:T(8,128)S(1)} %get-tuple-element.56.raw_ref, bf16[5,252,1024]{2,1,0:T(8,128)(2,1)S(1)} %copy-done.1), custom_call_target="tpu_custom_call" | custom-call | tf_op jit(solution)/shard_map/pallas_call | solution.py:234
  (94 shorter events, 17.7 us)
Async XLA Ops:
  0.0 5.3 %copy-start.5 = (bf16[504,2048]{1,0:T(8,128)(2,1)S(1)}, bf16[504,2048]{1,0:T(8,128)(2,1)}, u32[]{:S(2)}) copy-start(bf16[504,2048]{1,0:T(8,128)(2,1)} %param.10) | copy-start | bytes 6193156
  1.4 4.2 %copy-start.12 = (pred[256]{0:T(512)(128)(4,1)S(1)}, pred[256]{0:T(512)(128)(4,1)}, u32[]{:S(2)}) copy-start(pred[256]{0:T(512)(128)(4,1)} %constant.66.clone.1) | copy-start | bytes 772
  2.4 27.1 %collective-permute-start.4 = (bf16[2,96,2048]{2,1,0:T(8,128)(2,1)}, bf16[2,96,2048]{2,1,0:T(8,128)(2,1)}, u32[]{:S(2)}, u32[]{:S(2)}) collective-permute-start(bf16[2,96,2048]{2,1,0:T(8,128)(2,1)} %pad_maximum_fusion.1), channel_id=1, source_target_pairs={{0,2},{1,3},{2,0},{3,1},{4,6},{5,7},{6,4},{7,5},{8,10},{9,11},{10,... | collective-permute-start | bytes 2359304 | tf_op jit(solution)/shard_map/ppermute | solution.py:281
  5.3 10.5 %collective-permute-start.1 = (bf16[2048,1024]{1,0:T(8,128)(2,1)}, bf16[2048,1024]{1,0:T(8,128)(2,1)}, u32[]{:S(2)}, u32[]{:S(2)}) collective-permute-start(bf16[2048,1024]{1,0:T(8,128)(2,1)} %param.9), channel_id=1, source_target_pairs={{0,1},{1,0},{2,3},{3,2},{4,5},{5,4},{6,7},{7,6},{8,9},{9,8},{10,11... | collective-permute-start | bytes 12582920 | tf_op jit(solution)/shard_map/ppermute | solution.py:281
  10.5 3.6 %copy-start.7 = (f32[1,1,2,256,1024]{4,3,2,1,0:T(8,128)}, f32[1,1,2,256,1024]{4,3,2,1,0:T(8,128)S(1)}, u32[]{:S(2)}) copy-start(f32[1,1,2,256,1024]{4,3,2,1,0:T(8,128)S(1)} %fusion.14) | copy-start | bytes 6291460
  10.5 2.6 %copy-start.6 = (bf16[504,2048]{1,0:T(8,128)(2,1)S(1)}, bf16[504,2048]{1,0:T(8,128)(2,1)}, u32[]{:S(2)}) copy-start(bf16[504,2048]{1,0:T(8,128)(2,1)} %param.10) | copy-start | bytes 6193156
  10.5 4.1 %copy-start.11 = (s32[2,252]{1,0:T(2,128)S(1)}, s32[2,252]{1,0:T(2,128)}, u32[]{:S(2)}) copy-start(s32[2,252]{1,0:T(2,128)} %param.16) | copy-start | bytes 6052
  10.5 4.1 %copy-start.9 = (s32[2,1024]{1,0:T(2,128)S(1)}, s32[2,1024]{1,0:T(2,128)}, u32[]{:S(2)}) copy-start(s32[2,1024]{1,0:T(2,128)} %param.17) | copy-start | bytes 24580
  11.6 15.0 %collective-permute-start = (f16[1,1,256,1024]{3,2,1,0:T(8,128)(2,1)}, f16[1,1,256,1024]{3,2,1,0:T(8,128)(2,1)}, u32[]{:S(2)}, u32[]{:S(2)}) collective-permute-start(f16[1,1,256,1024]{3,2,1,0:T(8,128)(2,1)} %fusion.37), channel_id=1, source_target_pairs={{0,4},{4,0},{8,12},{12,8},{16,20},{20,16},{24,28},{28,24},{1,5},{5... | collective-permute-start | bytes 1572872 | tf_op jit(solution)/shard_map/ppermute | solution.py:284
  14.1 25.3 %collective-permute-start.7 = (bf16[2,80,2048]{2,1,0:T(8,128)(2,1)}, bf16[2,80,2048]{2,1,0:T(8,128)(2,1)S(1)}, u32[]{:S(2)}, u32[]{:S(2)}) collective-permute-start(bf16[2,80,2048]{2,1,0:T(8,128)(2,1)} %pad_maximum_fusion.3), channel_id=1, source_target_pairs={{0,2},{1,3},{2,0},{3,1},{4,6},{5,7},{6,4},{7,5},{8,10},{9,11},{10,... | collective-permute-start | bytes 1966088 | tf_op jit(solution)/shard_map/ppermute | solution.py:281
  21.0 5.6 %copy-start.8 = (f32[1,1,2,256,1024]{4,3,2,1,0:T(8,128)S(1)}, f32[1,1,2,256,1024]{4,3,2,1,0:T(8,128)}, u32[]{:S(2)}) copy-start(f32[1,1,2,256,1024]{4,3,2,1,0:T(8,128)} %copy-done.7) | copy-start | bytes 6291460
  21.3 16.1 %collective-permute-start.3 = (f16[1,1,256,1024]{3,2,1,0:T(8,128)(2,1)S(1)}, f16[1,1,256,1024]{3,2,1,0:T(8,128)(2,1)S(1)}, u32[]{:S(2)}, u32[]{:S(2)}) collective-permute-start(f16[1,1,256,1024]{3,2,1,0:T(8,128)(2,1)S(1)} %fusion.38), channel_id=1, source_target_pairs={{0,4},{4,0},{8,12},{12,8},{16,20},{20,16},{24,28},{28,24},{1,5},{5... | collective-permute-start | bytes 1572872 | tf_op jit(solution)/shard_map/ppermute | solution.py:284
  26.6 2.8 %copy-start.4 = (bf16[2048,1024]{1,0:T(8,128)(2,1)S(1)}, bf16[2048,1024]{1,0:T(8,128)(2,1)}, u32[]{:S(2)}) copy-start(bf16[2048,1024]{1,0:T(8,128)(2,1)} %param.9) | copy-start | bytes 12582916
  28.2 11.1 %collective-permute-start.2 = (f16[1,256,1024]{2,1,0:T(8,128)(2,1)S(1)}, f16[1,256,1024]{2,1,0:T(8,128)(2,1)S(1)}, u32[]{:S(2)}, u32[]{:S(2)}) collective-permute-start(f16[1,256,1024]{2,1,0:T(8,128)(2,1)S(1)} %get-tuple-element.69), channel_id=1, source_target_pairs={{1,9},{5,13},{3,11},{7,15},{8,0},{12,4},{10,2},{14,6},{17,25},{21,... | collective-permute-start | bytes 1572872 | tf_op jit(solution)/shard_map/ppermute | solution.py:333
  34.0 11.7 %collective-permute-start.6 = (f16[2,1,96,1024]{3,2,0,1:T(8,128)(2,1)S(1)}, f16[2,1,96,1024]{3,2,0,1:T(8,128)(2,1)S(1)}, u32[]{:S(2)}, u32[]{:S(2)}) collective-permute-start(f16[2,1,96,1024]{3,2,0,1:T(8,128)(2,1)S(1)} %fusion.42), channel_id=1, source_target_pairs={{0,4},{4,0},{8,12},{12,8},{16,20},{20,16},{24,28},{28,24},{1,5},{5... | collective-permute-start | bytes 1179656 | tf_op jit(solution)/shard_map/ppermute | solution.py:284
  35.6 17.6 %collective-permute-start.10 = (bf16[2,80,2048]{2,1,0:T(8,128)(2,1)S(1)}, bf16[2,80,2048]{2,1,0:T(8,128)(2,1)S(1)}, u32[]{:S(2)}, u32[]{:S(2)}) collective-permute-start(bf16[2,80,2048]{2,1,0:T(8,128)(2,1)S(1)} %pad_maximum_fusion.4), channel_id=1, source_target_pairs={{0,2},{1,3},{2,0},{3,1},{4,6},{5,7},{6,4},{7,5},{8,10},{9,11},{10,... | collective-permute-start | bytes 1966088 | tf_op jit(solution)/shard_map/ppermute | solution.py:281
  41.2 25.7 %collective-permute-start.13 = (f16[1,256,1024]{2,1,0:T(8,128)(2,1)S(1)}, f16[1,256,1024]{2,1,0:T(8,128)(2,1)S(1)}, u32[]{:S(2)}, u32[]{:S(2)}) collective-permute-start(f16[1,256,1024]{2,1,0:T(8,128)(2,1)S(1)} %get-tuple-element.67), channel_id=1, source_target_pairs={{1,9},{5,13},{3,11},{7,15},{8,0},{12,4},{10,2},{14,6},{17,25},{21,... | collective-permute-start | bytes 1572872 | tf_op jit(solution)/shard_map/ppermute | solution.py:333
  42.5 26.0 %collective-permute-start.5 = (f16[1,256,1024]{2,1,0:T(8,128)(2,1)S(1)}, f16[1,256,1024]{2,1,0:T(8,128)(2,1)S(1)}, u32[]{:S(2)}, u32[]{:S(2)}) collective-permute-start(f16[1,256,1024]{2,1,0:T(8,128)(2,1)S(1)} %fusion.35), channel_id=1, source_target_pairs={{2,18},{6,22},{11,27},{15,31},{16,0},{20,4},{25,9},{29,13}} | collective-permute-start | bytes 1572872 | tf_op jit(solution)/shard_map/ppermute | solution.py:343
  43.9 3.6 %copy-start = (bf16[5,252,1024]{2,1,0:T(8,128)(2,1)S(1)}, bf16[5,252,1024]{2,1,0:T(8,128)(2,1)}, u32[]{:S(2)}) copy-start(bf16[5,252,1024]{2,1,0:T(8,128)(2,1)} %err_ref.2) | copy-start | bytes 7741444
  44.0 11.8 %collective-permute-start.9 = (f16[2,1,80,1024]{3,2,0,1:T(8,128)(2,1)S(1)}, f16[2,1,80,1024]{3,2,0,1:T(8,128)(2,1)S(1)}, u32[]{:S(2)}, u32[]{:S(2)}) collective-permute-start(f16[2,1,80,1024]{3,2,0,1:T(8,128)(2,1)S(1)} %fusion.45), channel_id=1, source_target_pairs={{0,4},{4,0},{8,12},{12,8},{16,20},{20,16},{24,28},{28,24},{1,5},{5... | collective-permute-start | bytes 983048 | tf_op jit(solution)/shard_map/ppermute | solution.py:284
  46.0 16.1 %collective-permute-start.8 = (f16[2,96,1024]{2,1,0:T(8,128)(2,1)S(1)}, f16[2,96,1024]{2,1,0:T(8,128)(2,1)S(1)}, u32[]{:S(2)}, u32[]{:S(2)}) collective-permute-start(f16[2,96,1024]{2,1,0:T(8,128)(2,1)S(1)} %get-tuple-element.65), channel_id=1, source_target_pairs={{1,9},{5,13},{3,11},{7,15},{8,0},{12,4},{10,2},{14,6},{17,25},{21,... | collective-permute-start | bytes 1179656 | tf_op jit(solution)/shard_map/ppermute | solution.py:333
  55.2 10.3 %collective-permute-start.14 = (f16[2,1,80,1024]{3,2,0,1:T(8,128)(2,1)S(1)}, f16[2,1,80,1024]{3,2,0,1:T(8,128)(2,1)S(1)}, u32[]{:S(2)}, u32[]{:S(2)}) collective-permute-start(f16[2,1,80,1024]{3,2,0,1:T(8,128)(2,1)S(1)} %fusion.46), channel_id=1, source_target_pairs={{0,4},{4,0},{8,12},{12,8},{16,20},{20,16},{24,28},{28,24},{1,5},{5... | collective-permute-start | bytes 983048 | tf_op jit(solution)/shard_map/ppermute | solution.py:284
  55.9 12.8 %collective-permute-start.12 = (f16[2,80,1024]{2,1,0:T(8,128)(2,1)S(1)}, f16[2,80,1024]{2,1,0:T(8,128)(2,1)S(1)}, u32[]{:S(2)}, u32[]{:S(2)}) collective-permute-start(f16[2,80,1024]{2,1,0:T(8,128)(2,1)S(1)} %get-tuple-element.63), channel_id=1, source_target_pairs={{1,9},{5,13},{3,11},{7,15},{8,0},{12,4},{10,2},{14,6},{17,25},{21,... | collective-permute-start | bytes 983048 | tf_op jit(solution)/shard_map/ppermute | solution.py:333
  62.2 19.4 %collective-permute-start.11 = (f16[2,96,1024]{2,1,0:T(8,128)(2,1)S(1)}, f16[2,96,1024]{2,1,0:T(8,128)(2,1)S(1)}, u32[]{:S(2)}, u32[]{:S(2)}) collective-permute-start(f16[2,96,1024]{2,1,0:T(8,128)(2,1)S(1)} %fusion.39), channel_id=1, source_target_pairs={{0,16},{4,20},{9,25},{13,29},{18,2},{22,6},{27,11},{31,15}} | collective-permute-start | bytes 1179656 | tf_op jit(solution)/shard_map/ppermute | solution.py:343
  65.6 14.6 %collective-permute-start.16 = (f16[2,80,1024]{2,1,0:T(8,128)(2,1)S(1)}, f16[2,80,1024]{2,1,0:T(8,128)(2,1)S(1)}, u32[]{:S(2)}, u32[]{:S(2)}) collective-permute-start(f16[2,80,1024]{2,1,0:T(8,128)(2,1)S(1)} %get-tuple-element.61), channel_id=1, source_target_pairs={{1,9},{5,13},{3,11},{7,15},{8,0},{12,4},{10,2},{14,6},{17,25},{21,... | collective-permute-start | bytes 983048 | tf_op jit(solution)/shard_map/ppermute | solution.py:333
  67.1 14.9 %collective-permute-start.18 = (f16[1,256,1024]{2,1,0:T(8,128)(2,1)S(1)}, f16[1,256,1024]{2,1,0:T(8,128)(2,1)S(1)}, u32[]{:S(2)}, u32[]{:S(2)}) collective-permute-start(f16[1,256,1024]{2,1,0:T(8,128)(2,1)S(1)} %fusion.36), channel_id=1, source_target_pairs={{2,18},{6,22},{11,27},{15,31},{16,0},{20,4},{25,9},{29,13}} | collective-permute-start | bytes 1572872 | tf_op jit(solution)/shard_map/ppermute | solution.py:343
  68.9 13.0 %collective-permute-start.15 = (f16[2,80,1024]{2,1,0:T(8,128)(2,1)S(1)}, f16[2,80,1024]{2,1,0:T(8,128)(2,1)S(1)}, u32[]{:S(2)}, u32[]{:S(2)}) collective-permute-start(f16[2,80,1024]{2,1,0:T(8,128)(2,1)S(1)} %fusion.40), channel_id=1, source_target_pairs={{0,16},{4,20},{9,25},{13,29},{18,2},{22,6},{27,11},{31,15}} | collective-permute-start | bytes 983048 | tf_op jit(solution)/shard_map/ppermute | solution.py:343
  80.3 5.9 %collective-permute-start.17 = (f16[2,80,1024]{2,1,0:T(8,128)(2,1)S(1)}, f16[2,80,1024]{2,1,0:T(8,128)(2,1)S(1)}, u32[]{:S(2)}, u32[]{:S(2)}) collective-permute-start(f16[2,80,1024]{2,1,0:T(8,128)(2,1)S(1)} %fusion.41), channel_id=1, source_target_pairs={{0,16},{4,20},{9,25},{13,29},{18,2},{22,6},{27,11},{31,15}} | collective-permute-start | bytes 983048 | tf_op jit(solution)/shard_map/ppermute | solution.py:343
  86.6 3.0 %copy-start.1 = (bf16[5,252,1024]{2,1,0:T(8,128)(2,1)S(1)}, bf16[5,252,1024]{2,1,0:T(8,128)(2,1)}, u32[]{:S(2)}) copy-start(bf16[5,252,1024]{2,1,0:T(8,128)(2,1)} %amp_ref.3) | copy-start | bytes 7741444
  86.6 3.0 %copy-start.2 = (f32[252,1024]{1,0:T(8,128)S(1)}, f32[252,1024]{1,0:T(8,128)}, u32[]{:S(2)}) copy-start(f32[252,1024]{1,0:T(8,128)} %src_ref.1) | copy-start | bytes 3096580
  86.7 2.7 %collective-permute-start.19 = (f32[176,1024]{1,0:T(8,128)S(1)}, f32[176,1024]{1,0:T(8,128)S(1)}, u32[]{:S(2)}, u32[]{:S(2)}) collective-permute-start(f32[176,1024]{1,0:T(8,128)S(1)} %pad_maximum_fusion.2), channel_id=1, source_target_pairs={{0,1},{1,0},{2,3},{3,2},{4,5},{5,4},{6,7},{7,6},{8,9},{9,8},{10,11... | collective-permute-start | bytes 2162696 | tf_op jit(solution)/shard_map/ppermute | solution.py:281
  86.8 2.6 %collective-permute-start.20 = (f32[80,1024]{1,0:T(8,128)S(1)}, f32[80,1024]{1,0:T(8,128)S(1)}, u32[]{:S(2)}, u32[]{:S(2)}) collective-permute-start(f32[80,1024]{1,0:T(8,128)S(1)} %get-tuple-element.81), channel_id=1, source_target_pairs={{0,1},{1,0},{2,3},{3,2},{4,5},{5,4},{6,7},{7,6},{8,9},{9,8},{10,11... | collective-permute-start | bytes 983048 | tf_op jit(solution)/shard_map/ppermute | solution.py:281
  (3 other events, 4.5 us)

commit v6 on v5

--- a/solution.py
+++ b/solution.py
@@ -422,11 +422,9 @@
                 total_rows = far_end(*fars[p][:2])
                 mine, other = mine + total_rows[0], other + total_rows[1]
             done.append((mine, other))
-        early = [other for _, other in done[:-1]]
-        swapped = send_col(jnp.concatenate(early, axis=0), 1) if early else None
-        swapped_last = send_col(done[-1][1], 1)
-        taken = swapped_last if swapped is None else jnp.concatenate([swapped, swapped_last])
-        ladder = jnp.concatenate([mine for mine, _ in done], axis=0) + taken
+        ladder = jnp.concatenate(
+            [mine + send_col(other, 1) for mine, other in done], axis=0
+        )
 
         raw, shares = new_products(
             ladder, source_terms, occ_energy, vir_energy, hist_amp, hist_err, stored, total

time: 109 us -> 108 us (level)
    ppermute x6 -> x7, waiting for transfers between devices: 5.6 us -> 4.59 us  [send_col(): return lax.ppermute(x, 'col', [(i, i ^ m) for i in range(col_n)])]
    ppermute x6 -> x7, starting transfers between devices: 4.55 us -> 4.62 us  [send_col(): return lax.ppermute(x, 'col', [(i, i ^ m) for i in range(col_n)])]
  transfers between devices with their start and end apart: 21 -> 22, of which waited for: 9 -> 10; matrix products, arithmetic and copies ran while one was open for 18% -> 18% of each run, Pallas kernels for 7% -> 7%
where the time goes in v6:
time: 108 us
  starting transfers between devices  30.5 us (28%)
  waiting for transfers between devices  26.3 us (24%)
  Pallas kernels  13 us (12%)
  blocking collectives  12.6 us (12%)
  matrix products  10.1 us (9%)
  other arithmetic  9.9 us (9%)
  local copies, waits for them, and re-layouts  4.56 us (4%)
    all_to_all x1, blocking collectives, on_device(): gathered = lax.all_to_all(shares, ('row', 'col'), 0, 0, tiled=True)  12.6 us
    ppermute x5, starting transfers between devices, far_begin(): taken.append(lax.ppermute(data, ('row', 'col'), links))  12.6 us
    ppermute x5, waiting for transfers between devices, pair_begin(): return (part, lax.ppermute(send, ('row', 'col'), even_links), send)  12.5 us
    dot_general x7, matrix products, multiply(): out = jnp.dot(piece.reshape(-1, depth), right, preferred_element_type=f32)  10.1 us
    ppermute x5, starting transfers between devices, send_row(): return lax.ppermute(x, 'row', [(i, i ^ m) for i in range(row_n)])  6.68 us
    ppermute x5, starting transfers between devices, pair_begin(): return (part, lax.ppermute(send, ('row', 'col'), even_links), send)  6.64 us
    ppermute x5, waiting for transfers between devices, send_row(): return lax.ppermute(x, 'row', [(i, i ^ m) for i in range(row_n)])  5.41 us
    pallas_call x1, Pallas kernels, product_and_hold(): pl.pallas_call(kernel, grid=(width // block,), in_specs=[pl.BlockSpec((ro...  5.17 us
  transfers between devices with their start and end apart: 22, of which 10 were waited for; matrix products, arithmetic and copies ran while one was open for 18% of the time, Pallas kernels for 7%

profile of v6, /device:TPU:0, one launch (start us, length us, event | category | flops | bytes accessed | tf_op | source)
XLA Modules:
  0.0 107.8 jit_solution(14143358450868966483)
XLA Ops:
  0.0 1.4 %slice_bitcast_fusion.1 = (bf16[1,96,2048]{2,1,0:T(8,128)(2,1)S(1)}, bf16[1,96,2048]{2,1,0:T(8,128)(2,1)S(1)}) fusion(bf16[504,2048]{1,0:T(8,128)(2,1)} %param.10), kind=kLoop, calls=%fused_computation.69 | loop fusion | bytes 1572864 | tf_op jit(solution)/shard_map/stack | solution.py:356
  2.4 3.0 %collective-permute-start.4 = (bf16[2,96,2048]{2,1,0:T(8,128)(2,1)}, bf16[2,96,2048]{2,1,0:T(8,128)(2,1)}, u32[]{:S(2)}, u32[]{:S(2)}) collective-permute-start(bf16[2,96,2048]{2,1,0:T(8,128)(2,1)} %pad_maximum_fusion.2), channel_id=1, source_target_pairs={{0,2},{1,3},{2,0},{3,1},{4,6},{5,7},{6,4},{7,5},{8,10},{9,11},{10,... | collective-permute-start | bytes 2359304 | tf_op jit(solution)/shard_map/ppermute | solution.py:281
  6.1 2.0 %copy-done.3 = bf16[2048,1024]{1,0:T(8,128)(2,1)S(1)} copy-done((bf16[2048,1024]{1,0:T(8,128)(2,1)S(1)}, bf16[2048,1024]{1,0:T(8,128)(2,1)}, u32[]{:S(2)}) %copy-start.3) | copy-done | bytes 4194328
  8.1 2.4 %fusion.14 = f32[1,1,2,256,1024]{4,3,2,1,0:T(8,128)S(1)} fusion(bf16[2,256,2048]{2,1,0:T(8,128)(2,1)S(1)} %pad_maximum_fusion, bf16[2048,1024]{1,0:T(8,128)(2,1)S(1)} %copy-done.3), kind=kOutput, calls=%fused_computation.19 | convolution fusion | flops 2147483648 | bytes 8388608 | tf_op jit(solution)/shard_map/dot_general | solution.py:310
  11.6 1.5 %collective-permute-start = (f16[1,1,256,1024]{3,2,1,0:T(8,128)(2,1)}, f16[1,1,256,1024]{3,2,1,0:T(8,128)(2,1)}, u32[]{:S(2)}, u32[]{:S(2)}) collective-permute-start(f16[1,1,256,1024]{3,2,1,0:T(8,128)(2,1)} %fusion.37), channel_id=1, source_target_pairs={{0,4},{4,0},{8,12},{12,8},{16,20},{20,16},{24,28},{28,24},{1,5},{5... | collective-permute-start | bytes 1572872 | tf_op jit(solution)/shard_map/ppermute | solution.py:284
  15.9 5.2 %shard_map.91 = (f32[512,1024]{1,0:T(8,128)S(1)}, bf16[2048,1024]{1,0:T(8,128)(2,1)S(1)}) custom-call(bf16[512,2048]{1,0:T(8,128)(2,1)S(1)} %bitcast.134, bf16[2048,1024]{1,0:T(8,128)(2,1)} %collective-permute-done.1.right_ref), custom_call_target="tpu_custom_call" | custom-call | flops 2147483648 | bytes 6291456 | tf_op jit(solution)/shard_map/pallas_call | solution.py:57
  21.3 1.5 %collective-permute-start.3 = (f16[1,1,256,1024]{3,2,1,0:T(8,128)(2,1)S(1)}, f16[1,1,256,1024]{3,2,1,0:T(8,128)(2,1)S(1)}, u32[]{:S(2)}, u32[]{:S(2)}) collective-permute-start(f16[1,1,256,1024]{3,2,1,0:T(8,128)(2,1)S(1)} %fusion.38), channel_id=1, source_target_pairs={{0,4},{4,0},{8,12},{12,8},{16,20},{20,16},{24,28},{28,24},{1,5},{5... | collective-permute-start | bytes 1572872 | tf_op jit(solution)/shard_map/ppermute | solution.py:284
  22.8 3.9 %collective-permute-done = f16[1,1,256,1024]{3,2,1,0:T(8,128)(2,1)} collective-permute-done((f16[1,1,256,1024]{3,2,1,0:T(8,128)(2,1)}, f16[1,1,256,1024]{3,2,1,0:T(8,128)(2,1)}, u32[]{:S(2)}, u32[]{:S(2)}) %collective-permute-start) | collective-permute-done | bytes 524320 | tf_op jit(solution)/shard_map/ppermute | solution.py:284
  26.6 1.5 %fusion.58 = (f16[1,256,1024]{2,1,0:T(8,128)(2,1)S(1)}, f32[1,256,1024]{2,1,0:T(8,128)S(1)}) fusion(f16[1,256,1024]{2,1,0:T(8,128)(2,1)} %bitcast.8, f32[1,1,2,256,1024]{4,3,2,1,0:T(8,128)S(1)} %copy-done.8, pred[]{:T(512)S(6)} %eq.87), kind=kLoop, calls=%fused_computation.94 | loop fusion | flops 1048576 | bytes 4194305 | tf_op jit(solution)/shard_map/convert_element_type | solution.py:332
  28.1 1.3 %collective-permute-start.2 = (f16[1,256,1024]{2,1,0:T(8,128)(2,1)S(1)}, f16[1,256,1024]{2,1,0:T(8,128)(2,1)S(1)}, u32[]{:S(2)}, u32[]{:S(2)}) collective-permute-start(f16[1,256,1024]{2,1,0:T(8,128)(2,1)S(1)} %get-tuple-element.69), channel_id=1, source_target_pairs={{1,9},{5,13},{3,11},{7,15},{8,0},{12,4},{10,2},{14,6},{17,25},{21,... | collective-permute-start | bytes 1572872 | tf_op jit(solution)/shard_map/ppermute | solution.py:333
  29.4 2.1 %fusion.17 = f32[1,2,96,1024]{3,2,0,1:T(8,128)S(1)} fusion(bf16[2,96,2048]{2,1,0:T(8,128)(2,1)} %collective-permute-done.4, bf16[2048,1024]{1,0:T(8,128)(2,1)S(1)} %copy-done.4), kind=kOutput, calls=%fused_computation.23 | convolution fusion | flops 805306368 | bytes 5767168 | tf_op jit(solution)/shard_map/dot_general | solution.py:310
  31.6 2.2 %fusion.20 = f32[1,2,96,1024]{3,2,0,1:T(8,128)S(1)} fusion(bf16[2,96,2048]{2,1,0:T(8,128)(2,1)} %collective-permute-done.4, bf16[2048,1024]{1,0:T(8,128)(2,1)S(1)} %get-tuple-element.37), kind=kOutput, calls=%fused_computation.24 | convolution fusion | flops 805306368 | bytes 5767168 | tf_op jit(solution)/shard_map/dot_general | solution.py:310
  34.0 1.6 %collective-permute-start.6 = (f16[2,1,96,1024]{3,2,0,1:T(8,128)(2,1)S(1)}, f16[2,1,96,1024]{3,2,0,1:T(8,128)(2,1)S(1)}, u32[]{:S(2)}, u32[]{:S(2)}) collective-permute-start(f16[2,1,96,1024]{3,2,0,1:T(8,128)(2,1)S(1)} %fusion.42), channel_id=1, source_target_pairs={{0,4},{4,0},{8,12},{12,8},{16,20},{20,16},{24,28},{28,24},{1,5},{5... | collective-permute-start | bytes 1179656 | tf_op jit(solution)/shard_map/ppermute | solution.py:284
  36.0 1.3 %collective-permute-done.3 = f16[1,1,256,1024]{3,2,1,0:T(8,128)(2,1)S(1)} collective-permute-done((f16[1,1,256,1024]{3,2,1,0:T(8,128)(2,1)S(1)}, f16[1,1,256,1024]{3,2,1,0:T(8,128)(2,1)S(1)}, u32[]{:S(2)}, u32[]{:S(2)}) %collective-permute-start.3) | collective-permute-done | bytes 524320 | tf_op jit(solution)/shard_map/ppermute | solution.py:284
  37.7 1.5 %collective-permute-done.2 = f16[1,256,1024]{2,1,0:T(8,128)(2,1)S(1)} collective-permute-done((f16[1,256,1024]{2,1,0:T(8,128)(2,1)S(1)}, f16[1,256,1024]{2,1,0:T(8,128)(2,1)S(1)}, u32[]{:S(2)}, u32[]{:S(2)}) %collective-permute-start.2) | collective-permute-done | bytes 524320 | tf_op jit(solution)/shard_map/ppermute | solution.py:333
  41.2 1.3 %collective-permute-start.12 = (f16[1,256,1024]{2,1,0:T(8,128)(2,1)S(1)}, f16[1,256,1024]{2,1,0:T(8,128)(2,1)S(1)}, u32[]{:S(2)}, u32[]{:S(2)}) collective-permute-start(f16[1,256,1024]{2,1,0:T(8,128)(2,1)S(1)} %get-tuple-element.67), channel_id=1, source_target_pairs={{1,9},{5,13},{3,11},{7,15},{8,0},{12,4},{10,2},{14,6},{17,25},{21,... | collective-permute-start | bytes 1572872 | tf_op jit(solution)/shard_map/ppermute | solution.py:333
  42.5 1.3 %collective-permute-start.5 = (f16[1,256,1024]{2,1,0:T(8,128)(2,1)S(1)}, f16[1,256,1024]{2,1,0:T(8,128)(2,1)S(1)}, u32[]{:S(2)}, u32[]{:S(2)}) collective-permute-start(f16[1,256,1024]{2,1,0:T(8,128)(2,1)S(1)} %fusion.35), channel_id=1, source_target_pairs={{2,18},{6,22},{11,27},{15,31},{16,0},{20,4},{25,9},{29,13}} | collective-permute-start | bytes 1572872 | tf_op jit(solution)/shard_map/ppermute | solution.py:343
  44.0 1.6 %collective-permute-start.9 = (f16[2,1,80,1024]{3,2,0,1:T(8,128)(2,1)S(1)}, f16[2,1,80,1024]{3,2,0,1:T(8,128)(2,1)S(1)}, u32[]{:S(2)}, u32[]{:S(2)}) collective-permute-start(f16[2,1,80,1024]{3,2,0,1:T(8,128)(2,1)S(1)} %fusion.46), channel_id=1, source_target_pairs={{0,4},{4,0},{8,12},{12,8},{16,20},{20,16},{24,28},{28,24},{1,5},{5... | collective-permute-start | bytes 983048 | tf_op jit(solution)/shard_map/ppermute | solution.py:284
  45.9 1.5 %collective-permute-start.8 = (f16[2,96,1024]{2,1,0:T(8,128)(2,1)S(1)}, f16[2,96,1024]{2,1,0:T(8,128)(2,1)S(1)}, u32[]{:S(2)}, u32[]{:S(2)}) collective-permute-start(f16[2,96,1024]{2,1,0:T(8,128)(2,1)S(1)} %get-tuple-element.65), channel_id=1, source_target_pairs={{1,9},{5,13},{3,11},{7,15},{8,0},{12,4},{10,2},{14,6},{17,25},{21,... | collective-permute-start | bytes 1179656 | tf_op jit(solution)/shard_map/ppermute | solution.py:333
  47.4 2.2 %shard_map.92.sto_ref = f32[16,1024]{1,0:T(8,128)S(1)} custom-call(bf16[5,252,1024]{2,1,0:T(8,128)(2,1)S(1)} %copy-done), custom_call_target="tpu_custom_call" | custom-call | flops 7741440 | bytes 2580480 | tf_op jit(solution)/shard_map/pallas_call | solution.py:95
  49.7 3.4 %collective-permute-done.10 = bf16[2,80,2048]{2,1,0:T(8,128)(2,1)S(1)} collective-permute-done((bf16[2,80,2048]{2,1,0:T(8,128)(2,1)S(1)}, bf16[2,80,2048]{2,1,0:T(8,128)(2,1)S(1)}, u32[]{:S(2)}, u32[]{:S(2)}) %collective-permute-start.10) | collective-permute-done | bytes 655392 | tf_op jit(solution)/shard_map/ppermute | solution.py:281
  55.9 1.3 %collective-permute-start.16 = (f16[2,80,1024]{2,1,0:T(8,128)(2,1)S(1)}, f16[2,80,1024]{2,1,0:T(8,128)(2,1)S(1)}, u32[]{:S(2)}, u32[]{:S(2)}) collective-permute-start(f16[2,80,1024]{2,1,0:T(8,128)(2,1)S(1)} %get-tuple-element.63), channel_id=1, source_target_pairs={{1,9},{5,13},{3,11},{7,15},{8,0},{12,4},{10,2},{14,6},{17,25},{21,... | collective-permute-start | bytes 983048 | tf_op jit(solution)/shard_map/ppermute | solution.py:333
  57.2 4.9 %collective-permute-done.8 = f16[2,96,1024]{2,1,0:T(8,128)(2,1)S(1)} collective-permute-done((f16[2,96,1024]{2,1,0:T(8,128)(2,1)S(1)}, f16[2,96,1024]{2,1,0:T(8,128)(2,1)S(1)}, u32[]{:S(2)}, u32[]{:S(2)}) %collective-permute-start.8) | collective-permute-done | bytes 393248 | tf_op jit(solution)/shard_map/ppermute | solution.py:333
  62.2 3.2 %collective-permute-start.11 = (f16[2,96,1024]{2,1,0:T(8,128)(2,1)S(1)}, f16[2,96,1024]{2,1,0:T(8,128)(2,1)S(1)}, u32[]{:S(2)}, u32[]{:S(2)}) collective-permute-start(f16[2,96,1024]{2,1,0:T(8,128)(2,1)S(1)} %fusion.39), channel_id=1, source_target_pairs={{0,16},{4,20},{9,25},{13,29},{18,2},{22,6},{27,11},{31,15}} | collective-permute-start | bytes 1179656 | tf_op jit(solution)/shard_map/ppermute | solution.py:343
  65.6 1.3 %collective-permute-start.19 = (f16[2,80,1024]{2,1,0:T(8,128)(2,1)S(1)}, f16[2,80,1024]{2,1,0:T(8,128)(2,1)S(1)}, u32[]{:S(2)}, u32[]{:S(2)}) collective-permute-start(f16[2,80,1024]{2,1,0:T(8,128)(2,1)S(1)} %get-tuple-element.61), channel_id=1, source_target_pairs={{1,9},{5,13},{3,11},{7,15},{8,0},{12,4},{10,2},{14,6},{17,25},{21,... | collective-permute-start | bytes 983048 | tf_op jit(solution)/shard_map/ppermute | solution.py:333
  68.5 5.5 %collective-permute-start.17 = (f16[2,80,1024]{2,1,0:T(8,128)(2,1)S(1)}, f16[2,80,1024]{2,1,0:T(8,128)(2,1)S(1)}, u32[]{:S(2)}, u32[]{:S(2)}) collective-permute-start(f16[2,80,1024]{2,1,0:T(8,128)(2,1)S(1)} %fusion.40), channel_id=1, source_target_pairs={{0,16},{4,20},{9,25},{13,29},{18,2},{22,6},{27,11},{31,15}} | collective-permute-start | bytes 983048 | tf_op jit(solution)/shard_map/ppermute | solution.py:343
  74.0 6.2 %collective-permute-done.19 = f16[2,80,1024]{2,1,0:T(8,128)(2,1)S(1)} collective-permute-done((f16[2,80,1024]{2,1,0:T(8,128)(2,1)S(1)}, f16[2,80,1024]{2,1,0:T(8,128)(2,1)S(1)}, u32[]{:S(2)}, u32[]{:S(2)}) %collective-permute-start.19) | collective-permute-done | bytes 327712 | tf_op jit(solution)/shard_map/ppermute | solution.py:333
  80.3 1.3 %collective-permute-start.20 = (f16[2,80,1024]{2,1,0:T(8,128)(2,1)S(1)}, f16[2,80,1024]{2,1,0:T(8,128)(2,1)S(1)}, u32[]{:S(2)}, u32[]{:S(2)}) collective-permute-start(f16[2,80,1024]{2,1,0:T(8,128)(2,1)S(1)} %fusion.41), channel_id=1, source_target_pairs={{0,16},{4,20},{9,25},{13,29},{18,2},{22,6},{27,11},{31,15}} | collective-permute-start | bytes 983048 | tf_op jit(solution)/shard_map/ppermute | solution.py:343
  82.4 3.8 %collective-permute-done.20 = f16[2,80,1024]{2,1,0:T(8,128)(2,1)S(1)} collective-permute-done((f16[2,80,1024]{2,1,0:T(8,128)(2,1)S(1)}, f16[2,80,1024]{2,1,0:T(8,128)(2,1)S(1)}, u32[]{:S(2)}, u32[]{:S(2)}) %collective-permute-start.20) | collective-permute-done | bytes 327712 | tf_op jit(solution)/shard_map/ppermute | solution.py:343
  89.5 3.0 %shard_map.93 = (f32[252,1024]{1,0:T(8,128)S(1)}, f32[32,128]{1,0:T(8,128)S(1)}) custom-call(f32[256,1024]{1,0:T(8,128)S(1)} %pad_maximum_fusion.1.lad_ref, f32[252,1024]{1,0:T(8,128)S(1)} %copy-done.2, f32[252,128]{1,0:T(8,128)S(1)} %broadcast_in_dim.70.occ_ref, f32[1,1024]{1,0:T(1,128)S(1)} %bitcast.136, bf16[5,252,1024]{2,1,0:T(8,128)(2,1)S(1)} %copy-done.1, ...), custom_call_target="tpu_custom_call" | custom-call | flops 5160960 | bytes 6193152 | tf_op jit(solution)/shard_map/pallas_call | solution.py:151
  92.4 12.6 %all_to_all.11 = f32[32,1,128]{2,1,0:T(1,128)S(1)} all-to-all(f32[32,1,128]{2,1,0:T(1,128)S(1)} %bitcast.137), channel_id=1, replica_groups=mesh['row'=8,'col'=4] {'row','col'}, dimensions={0} | all-to-all | bytes 32768 | tf_op jit(solution)/shard_map/all_to_all | solution.py:432
  105.1 2.7 %shard_map.94 = f32[252,1024]{1,0:T(8,128)} custom-call(f32[32,128]{1,0:T(8,128)S(1)} %bitcast.135, f32[252,1024]{1,0:T(8,128)S(1)} %get-tuple-element.56.raw_ref, bf16[5,252,1024]{2,1,0:T(8,128)(2,1)S(1)} %copy-done.1), custom_call_target="tpu_custom_call" | custom-call | tf_op jit(solution)/shard_map/pallas_call | solution.py:234
  (97 shorter events, 18.0 us)
Async XLA Ops:
  0.0 5.3 %copy-start.5 = (bf16[504,2048]{1,0:T(8,128)(2,1)S(1)}, bf16[504,2048]{1,0:T(8,128)(2,1)}, u32[]{:S(2)}) copy-start(bf16[504,2048]{1,0:T(8,128)(2,1)} %param.10) | copy-start | bytes 6193156
  1.4 4.2 %copy-start.12 = (pred[256]{0:T(512)(128)(4,1)S(1)}, pred[256]{0:T(512)(128)(4,1)}, u32[]{:S(2)}) copy-start(pred[256]{0:T(512)(128)(4,1)} %constant.66.clone.1) | copy-start | bytes 772
  2.4 27.1 %collective-permute-start.4 = (bf16[2,96,2048]{2,1,0:T(8,128)(2,1)}, bf16[2,96,2048]{2,1,0:T(8,128)(2,1)}, u32[]{:S(2)}, u32[]{:S(2)}) collective-permute-start(bf16[2,96,2048]{2,1,0:T(8,128)(2,1)} %pad_maximum_fusion.2), channel_id=1, source_target_pairs={{0,2},{1,3},{2,0},{3,1},{4,6},{5,7},{6,4},{7,5},{8,10},{9,11},{10,... | collective-permute-start | bytes 2359304 | tf_op jit(solution)/shard_map/ppermute | solution.py:281
  5.3 10.5 %collective-permute-start.1 = (bf16[2048,1024]{1,0:T(8,128)(2,1)}, bf16[2048,1024]{1,0:T(8,128)(2,1)}, u32[]{:S(2)}, u32[]{:S(2)}) collective-permute-start(bf16[2048,1024]{1,0:T(8,128)(2,1)} %param.9), channel_id=1, source_target_pairs={{0,1},{1,0},{2,3},{3,2},{4,5},{5,4},{6,7},{7,6},{8,9},{9,8},{10,11... | collective-permute-start | bytes 12582920 | tf_op jit(solution)/shard_map/ppermute | solution.py:281
  5.9 2.2 %copy-start.3 = (bf16[2048,1024]{1,0:T(8,128)(2,1)S(1)}, bf16[2048,1024]{1,0:T(8,128)(2,1)}, u32[]{:S(2)}) copy-start(bf16[2048,1024]{1,0:T(8,128)(2,1)} %param.9) | copy-start | bytes 12582916
  10.5 3.6 %copy-start.7 = (f32[1,1,2,256,1024]{4,3,2,1,0:T(8,128)}, f32[1,1,2,256,1024]{4,3,2,1,0:T(8,128)S(1)}, u32[]{:S(2)}) copy-start(f32[1,1,2,256,1024]{4,3,2,1,0:T(8,128)S(1)} %fusion.14) | copy-start | bytes 6291460
  10.5 2.6 %copy-start.6 = (bf16[504,2048]{1,0:T(8,128)(2,1)S(1)}, bf16[504,2048]{1,0:T(8,128)(2,1)}, u32[]{:S(2)}) copy-start(bf16[504,2048]{1,0:T(8,128)(2,1)} %param.10) | copy-start | bytes 6193156
  10.5 4.1 %copy-start.11 = (s32[2,252]{1,0:T(2,128)S(1)}, s32[2,252]{1,0:T(2,128)}, u32[]{:S(2)}) copy-start(s32[2,252]{1,0:T(2,128)} %param.16) | copy-start | bytes 6052
  10.5 4.1 %copy-start.9 = (s32[2,1024]{1,0:T(2,128)S(1)}, s32[2,1024]{1,0:T(2,128)}, u32[]{:S(2)}) copy-start(s32[2,1024]{1,0:T(2,128)} %param.17) | copy-start | bytes 24580
  11.6 15.0 %collective-permute-start = (f16[1,1,256,1024]{3,2,1,0:T(8,128)(2,1)}, f16[1,1,256,1024]{3,2,1,0:T(8,128)(2,1)}, u32[]{:S(2)}, u32[]{:S(2)}) collective-permute-start(f16[1,1,256,1024]{3,2,1,0:T(8,128)(2,1)} %fusion.37), channel_id=1, source_target_pairs={{0,4},{4,0},{8,12},{12,8},{16,20},{20,16},{24,28},{28,24},{1,5},{5... | collective-permute-start | bytes 1572872 | tf_op jit(solution)/shard_map/ppermute | solution.py:284
  14.1 25.3 %collective-permute-start.7 = (bf16[2,80,2048]{2,1,0:T(8,128)(2,1)}, bf16[2,80,2048]{2,1,0:T(8,128)(2,1)S(1)}, u32[]{:S(2)}, u32[]{:S(2)}) collective-permute-start(bf16[2,80,2048]{2,1,0:T(8,128)(2,1)} %pad_maximum_fusion.3), channel_id=1, source_target_pairs={{0,2},{1,3},{2,0},{3,1},{4,6},{5,7},{6,4},{7,5},{8,10},{9,11},{10,... | collective-permute-start | bytes 1966088 | tf_op jit(solution)/shard_map/ppermute | solution.py:281
  21.0 5.6 %copy-start.8 = (f32[1,1,2,256,1024]{4,3,2,1,0:T(8,128)S(1)}, f32[1,1,2,256,1024]{4,3,2,1,0:T(8,128)}, u32[]{:S(2)}) copy-start(f32[1,1,2,256,1024]{4,3,2,1,0:T(8,128)} %copy-done.7) | copy-start | bytes 6291460
  21.3 16.1 %collective-permute-start.3 = (f16[1,1,256,1024]{3,2,1,0:T(8,128)(2,1)S(1)}, f16[1,1,256,1024]{3,2,1,0:T(8,128)(2,1)S(1)}, u32[]{:S(2)}, u32[]{:S(2)}) collective-permute-start(f16[1,1,256,1024]{3,2,1,0:T(8,128)(2,1)S(1)} %fusion.38), channel_id=1, source_target_pairs={{0,4},{4,0},{8,12},{12,8},{16,20},{20,16},{24,28},{28,24},{1,5},{5... | collective-permute-start | bytes 1572872 | tf_op jit(solution)/shard_map/ppermute | solution.py:284
  26.6 2.8 %copy-start.4 = (bf16[2048,1024]{1,0:T(8,128)(2,1)S(1)}, bf16[2048,1024]{1,0:T(8,128)(2,1)}, u32[]{:S(2)}) copy-start(bf16[2048,1024]{1,0:T(8,128)(2,1)} %param.9) | copy-start | bytes 12582916
  28.1 11.1 %collective-permute-start.2 = (f16[1,256,1024]{2,1,0:T(8,128)(2,1)S(1)}, f16[1,256,1024]{2,1,0:T(8,128)(2,1)S(1)}, u32[]{:S(2)}, u32[]{:S(2)}) collective-permute-start(f16[1,256,1024]{2,1,0:T(8,128)(2,1)S(1)} %get-tuple-element.69), channel_id=1, source_target_pairs={{1,9},{5,13},{3,11},{7,15},{8,0},{12,4},{10,2},{14,6},{17,25},{21,... | collective-permute-start | bytes 1572872 | tf_op jit(solution)/shard_map/ppermute | solution.py:333
  34.0 11.7 %collective-permute-start.6 = (f16[2,1,96,1024]{3,2,0,1:T(8,128)(2,1)S(1)}, f16[2,1,96,1024]{3,2,0,1:T(8,128)(2,1)S(1)}, u32[]{:S(2)}, u32[]{:S(2)}) collective-permute-start(f16[2,1,96,1024]{3,2,0,1:T(8,128)(2,1)S(1)} %fusion.42), channel_id=1, source_target_pairs={{0,4},{4,0},{8,12},{12,8},{16,20},{20,16},{24,28},{28,24},{1,5},{5... | collective-permute-start | bytes 1179656 | tf_op jit(solution)/shard_map/ppermute | solution.py:284
  35.5 17.6 %collective-permute-start.10 = (bf16[2,80,2048]{2,1,0:T(8,128)(2,1)S(1)}, bf16[2,80,2048]{2,1,0:T(8,128)(2,1)S(1)}, u32[]{:S(2)}, u32[]{:S(2)}) collective-permute-start(bf16[2,80,2048]{2,1,0:T(8,128)(2,1)S(1)} %pad_maximum_fusion.4), channel_id=1, source_target_pairs={{0,2},{1,3},{2,0},{3,1},{4,6},{5,7},{6,4},{7,5},{8,10},{9,11},{10,... | collective-permute-start | bytes 1966088 | tf_op jit(solution)/shard_map/ppermute | solution.py:281
  41.2 25.7 %collective-permute-start.12 = (f16[1,256,1024]{2,1,0:T(8,128)(2,1)S(1)}, f16[1,256,1024]{2,1,0:T(8,128)(2,1)S(1)}, u32[]{:S(2)}, u32[]{:S(2)}) collective-permute-start(f16[1,256,1024]{2,1,0:T(8,128)(2,1)S(1)} %get-tuple-element.67), channel_id=1, source_target_pairs={{1,9},{5,13},{3,11},{7,15},{8,0},{12,4},{10,2},{14,6},{17,25},{21,... | collective-permute-start | bytes 1572872 | tf_op jit(solution)/shard_map/ppermute | solution.py:333
  42.5 44.6 %collective-permute-start.5 = (f16[1,256,1024]{2,1,0:T(8,128)(2,1)S(1)}, f16[1,256,1024]{2,1,0:T(8,128)(2,1)S(1)}, u32[]{:S(2)}, u32[]{:S(2)}) collective-permute-start(f16[1,256,1024]{2,1,0:T(8,128)(2,1)S(1)} %fusion.35), channel_id=1, source_target_pairs={{2,18},{6,22},{11,27},{15,31},{16,0},{20,4},{25,9},{29,13}} | collective-permute-start | bytes 1572872 | tf_op jit(solution)/shard_map/ppermute | solution.py:343
  43.9 3.6 %copy-start = (bf16[5,252,1024]{2,1,0:T(8,128)(2,1)S(1)}, bf16[5,252,1024]{2,1,0:T(8,128)(2,1)}, u32[]{:S(2)}) copy-start(bf16[5,252,1024]{2,1,0:T(8,128)(2,1)} %err_ref.2) | copy-start | bytes 7741444
  44.0 11.7 %collective-permute-start.9 = (f16[2,1,80,1024]{3,2,0,1:T(8,128)(2,1)S(1)}, f16[2,1,80,1024]{3,2,0,1:T(8,128)(2,1)S(1)}, u32[]{:S(2)}, u32[]{:S(2)}) collective-permute-start(f16[2,1,80,1024]{3,2,0,1:T(8,128)(2,1)S(1)} %fusion.46), channel_id=1, source_target_pairs={{0,4},{4,0},{8,12},{12,8},{16,20},{20,16},{24,28},{28,24},{1,5},{5... | collective-permute-start | bytes 983048 | tf_op jit(solution)/shard_map/ppermute | solution.py:284
  45.9 16.1 %collective-permute-start.8 = (f16[2,96,1024]{2,1,0:T(8,128)(2,1)S(1)}, f16[2,96,1024]{2,1,0:T(8,128)(2,1)S(1)}, u32[]{:S(2)}, u32[]{:S(2)}) collective-permute-start(f16[2,96,1024]{2,1,0:T(8,128)(2,1)S(1)} %get-tuple-element.65), channel_id=1, source_target_pairs={{1,9},{5,13},{3,11},{7,15},{8,0},{12,4},{10,2},{14,6},{17,25},{21,... | collective-permute-start | bytes 1179656 | tf_op jit(solution)/shard_map/ppermute | solution.py:333
  55.1 10.3 %collective-permute-start.13 = (f16[2,1,80,1024]{3,2,0,1:T(8,128)(2,1)S(1)}, f16[2,1,80,1024]{3,2,0,1:T(8,128)(2,1)S(1)}, u32[]{:S(2)}, u32[]{:S(2)}) collective-permute-start(f16[2,1,80,1024]{3,2,0,1:T(8,128)(2,1)S(1)} %fusion.47), channel_id=1, source_target_pairs={{0,4},{4,0},{8,12},{12,8},{16,20},{20,16},{24,28},{28,24},{1,5},{5... | collective-permute-start | bytes 983048 | tf_op jit(solution)/shard_map/ppermute | solution.py:284
  55.9 12.5 %collective-permute-start.16 = (f16[2,80,1024]{2,1,0:T(8,128)(2,1)S(1)}, f16[2,80,1024]{2,1,0:T(8,128)(2,1)S(1)}, u32[]{:S(2)}, u32[]{:S(2)}) collective-permute-start(f16[2,80,1024]{2,1,0:T(8,128)(2,1)S(1)} %get-tuple-element.63), channel_id=1, source_target_pairs={{1,9},{5,13},{3,11},{7,15},{8,0},{12,4},{10,2},{14,6},{17,25},{21,... | collective-permute-start | bytes 983048 | tf_op jit(solution)/shard_map/ppermute | solution.py:333
  62.2 19.4 %collective-permute-start.11 = (f16[2,96,1024]{2,1,0:T(8,128)(2,1)S(1)}, f16[2,96,1024]{2,1,0:T(8,128)(2,1)S(1)}, u32[]{:S(2)}, u32[]{:S(2)}) collective-permute-start(f16[2,96,1024]{2,1,0:T(8,128)(2,1)S(1)} %fusion.39), channel_id=1, source_target_pairs={{0,16},{4,20},{9,25},{13,29},{18,2},{22,6},{27,11},{31,15}} | collective-permute-start | bytes 1179656 | tf_op jit(solution)/shard_map/ppermute | solution.py:343
  65.6 14.6 %collective-permute-start.19 = (f16[2,80,1024]{2,1,0:T(8,128)(2,1)S(1)}, f16[2,80,1024]{2,1,0:T(8,128)(2,1)S(1)}, u32[]{:S(2)}, u32[]{:S(2)}) collective-permute-start(f16[2,80,1024]{2,1,0:T(8,128)(2,1)S(1)} %get-tuple-element.61), channel_id=1, source_target_pairs={{1,9},{5,13},{3,11},{7,15},{8,0},{12,4},{10,2},{14,6},{17,25},{21,... | collective-permute-start | bytes 983048 | tf_op jit(solution)/shard_map/ppermute | solution.py:333
  67.1 14.9 %collective-permute-start.14 = (f16[1,256,1024]{2,1,0:T(8,128)(2,1)S(1)}, f16[1,256,1024]{2,1,0:T(8,128)(2,1)S(1)}, u32[]{:S(2)}, u32[]{:S(2)}) collective-permute-start(f16[1,256,1024]{2,1,0:T(8,128)(2,1)S(1)} %fusion.36), channel_id=1, source_target_pairs={{2,18},{6,22},{11,27},{15,31},{16,0},{20,4},{25,9},{29,13}} | collective-permute-start | bytes 1572872 | tf_op jit(solution)/shard_map/ppermute | solution.py:343
  68.5 13.3 %collective-permute-start.17 = (f16[2,80,1024]{2,1,0:T(8,128)(2,1)S(1)}, f16[2,80,1024]{2,1,0:T(8,128)(2,1)S(1)}, u32[]{:S(2)}, u32[]{:S(2)}) collective-permute-start(f16[2,80,1024]{2,1,0:T(8,128)(2,1)S(1)} %fusion.40), channel_id=1, source_target_pairs={{0,16},{4,20},{9,25},{13,29},{18,2},{22,6},{27,11},{31,15}} | collective-permute-start | bytes 983048 | tf_op jit(solution)/shard_map/ppermute | solution.py:343
  80.3 5.9 %collective-permute-start.20 = (f16[2,80,1024]{2,1,0:T(8,128)(2,1)S(1)}, f16[2,80,1024]{2,1,0:T(8,128)(2,1)S(1)}, u32[]{:S(2)}, u32[]{:S(2)}) collective-permute-start(f16[2,80,1024]{2,1,0:T(8,128)(2,1)S(1)} %fusion.41), channel_id=1, source_target_pairs={{0,16},{4,20},{9,25},{13,29},{18,2},{22,6},{27,11},{31,15}} | collective-permute-start | bytes 983048 | tf_op jit(solution)/shard_map/ppermute | solution.py:343
  82.3 5.0 %collective-permute-start.15 = (f32[96,1024]{1,0:T(8,128)S(1)}, f32[96,1024]{1,0:T(8,128)S(1)}, u32[]{:S(2)}, u32[]{:S(2)}) collective-permute-start(f32[96,1024]{1,0:T(8,128)S(1)} %fusion.43), channel_id=1, source_target_pairs={{0,1},{1,0},{2,3},{3,2},{4,5},{5,4},{6,7},{7,6},{8,9},{9,8},{10,11... | collective-permute-start | bytes 1179656 | tf_op jit(solution)/shard_map/ppermute | solution.py:281
  86.5 1.7 %collective-permute-start.18 = (f32[80,1024]{1,0:T(8,128)S(1)}, f32[80,1024]{1,0:T(8,128)S(1)}, u32[]{:S(2)}, u32[]{:S(2)}) collective-permute-start(f32[80,1024]{1,0:T(8,128)S(1)} %get-tuple-element.79), channel_id=1, source_target_pairs={{0,1},{1,0},{2,3},{3,2},{4,5},{5,4},{6,7},{7,6},{8,9},{9,8},{10,11... | collective-permute-start | bytes 983048 | tf_op jit(solution)/shard_map/ppermute | solution.py:281
  86.6 2.1 %collective-permute-start.21 = (f32[80,1024]{1,0:T(8,128)S(1)}, f32[80,1024]{1,0:T(8,128)S(1)}, u32[]{:S(2)}, u32[]{:S(2)}) collective-permute-start(f32[80,1024]{1,0:T(8,128)S(1)} %get-tuple-element.80), channel_id=1, source_target_pairs={{0,1},{1,0},{2,3},{3,2},{4,5},{5,4},{6,7},{7,6},{8,9},{9,8},{10,11... | collective-permute-start | bytes 983048 | tf_op jit(solution)/shard_map/ppermute | solution.py:281
  (4 other events, 6.1 us)
